TPU v7x, 32 devices: a whole 2x2x4 slice. The times are simulated.
32 devices in a mesh: parts: 2 (over y), coef: 4 (over z), poly: 2 (over x), limb: 2 (over core).
Axes of the slice: x: 2, y: 2, z: 4, core: 2. Of those that a mesh axis runs over, the one named last changes fastest.
Arguments:
- coefficients: float32 [96, 128, 4096], P(('parts', 'poly', 'limb'), None, 'coef'), parts along dimension 0, may hold values from -6 to 6
- batch_weights: float32 [32, 48], P('parts', ('poly', 'limb')), parts along dimension 0, may hold values from -0.875 to 0.875
- claimed: float32 [2, 32, 48], P(None, 'parts', ('poly', 'limb')), parts along dimension 1, may hold values from -6 to 6
- point_index: int32 [32], P(('parts', 'poly', 'limb')), parts along dimension 0, may hold values from 0 to 524287
- point_cycle: int32 [32], P(('parts', 'poly', 'limb')), parts along dimension 0, may hold values from 0 to 3
Outputs:
- evaluations: float32 [2, 128, 96, 32, 128], P(None, 'coef', ('parts', 'poly', 'limb')), parts along dimension 2
- quotient: float32 [2, 32, 128, 4096], P(None, ('parts', 'poly', 'limb'), None, 'coef'), parts along dimension 1
There are 2 independent parts, one for each index of `parts`. A program takes and returns all parts, laid end to end along the dimension named above; each array names one. Nothing has to cross between parts.
All inputs are finite; a program needn't handle non-finite values.
Results may differ from a plain program's by a relative error of at most 0.0003.
Values sent between devices are 32-bit elements; how exact they have to be, the bound alone decides.
No kernel may reach another device: no remote copies, remote signals or barrier semaphores. Data moves between devices by JAX's collectives and lax.ppermute only.
A program may use at most 128 MiB of HBM per device.

v0:
```python
import math

import jax
import jax.numpy as jnp
from jax import lax
from jax.sharding import PartitionSpec as P

LEN_COLS = 128
SPLIT_HI = 32
SPLIT_LO = 128
LEN_ROWS = 4096
LENGTH = 524288


precise = lax.Precision.HIGHEST


def phase_table(row_index, col_index, length):
    product = row_index[:, None] * col_index[None, :] % length
    angles = product.astype(jnp.float32) * (2.0 * math.pi / length)
    return (jnp.cos(angles), jnp.sin(angles))


def dft_table(length):
    indices = jnp.arange(length, dtype=jnp.int32)
    cos_table, sin_table = phase_table(indices, indices, length)
    factor = 1.0 / math.sqrt(length)
    return (cos_table * factor, sin_table * factor)


def row_turns():
    return phase_table(
        jnp.arange(SPLIT_HI, dtype=jnp.int32), jnp.arange(SPLIT_LO, dtype=jnp.int32), LEN_ROWS
    )


def contract(pattern, tables, pieces, inverse):
    cos_table, sin_table = tables
    real_part, imag_part = pieces

    def product(matrix, operand):
        return jnp.einsum(pattern, matrix, operand, precision=precise)

    if inverse:
        return (
            product(cos_table, real_part) - product(sin_table, imag_part),
            product(cos_table, imag_part) + product(sin_table, real_part),
        )
    return (
        product(cos_table, real_part) + product(sin_table, imag_part),
        product(cos_table, imag_part) - product(sin_table, real_part),
    )


def rotate(pieces, tables, inverse):
    cos_turn, sin_turn = tables
    real_part, imag_part = pieces
    if inverse:
        sin_turn = -sin_turn
    return (
        real_part * cos_turn + imag_part * sin_turn,
        imag_part * cos_turn - real_part * sin_turn,
    )


def first_section(values):
    extent = values.shape[1]
    rows_here = values.shape[2]
    cos_table, sin_table = dft_table(extent)
    real_part = jnp.einsum("kn,pnm->kpm", cos_table, values, precision=precise)
    imag_part = -jnp.einsum("kn,pnm->kpm", sin_table, values, precision=precise)
    row_index = lax.axis_index("coef") * rows_here + jnp.arange(rows_here, dtype=jnp.int32)
    frequency = jnp.arange(extent, dtype=jnp.int32)
    cos_turn, sin_turn = phase_table(frequency, row_index, LENGTH)
    pieces = rotate((real_part, imag_part), (cos_turn[:, None, :], sin_turn[:, None, :]), False)
    return jnp.stack(pieces)


def second_section(received):
    leading = received.shape[1:3]
    shaped = received.reshape((2,) + leading + (SPLIT_HI, SPLIT_LO))
    pieces = contract("va,kpab->kpvb", dft_table(SPLIT_HI), (shaped[0], shaped[1]), False)
    pieces = rotate(pieces, row_turns(), False)
    pieces = contract("ub,kpvb->kpvu", dft_table(SPLIT_LO), pieces, False)
    return jnp.stack(pieces)


def quotient_values(numerator, point_index, point_cycle):
    extent = numerator.shape[1]
    frequency = lax.axis_index("coef") * extent + jnp.arange(extent, dtype=jnp.int32)
    slow_part = jnp.arange(SPLIT_HI, dtype=jnp.int32)[None, :, None]
    fast_part = jnp.arange(SPLIT_LO, dtype=jnp.int32)[None, None, :]
    positions = LEN_COLS * (SPLIT_HI * fast_part + slow_part) + frequency[:, None, None]
    angles = positions.astype(jnp.float32) * (2.0 * math.pi / LENGTH)
    point_angle = point_index.astype(jnp.float32) * (2.0 * math.pi / LENGTH)
    radius = 1.0 + (point_cycle.astype(jnp.float32) + 1.0) / 512.0
    diff_real = jnp.cos(angles)[:, None] - (radius * jnp.cos(point_angle))[None, :, None, None]
    diff_imag = (radius * jnp.sin(point_angle))[None, :, None, None] - jnp.sin(angles)[:, None]
    magnitude = diff_real * diff_real + diff_imag * diff_imag
    quot_real = (numerator[0] * diff_real + numerator[1] * diff_imag) / magnitude
    quot_imag = (numerator[1] * diff_real - numerator[0] * diff_imag) / magnitude
    return (quot_real, quot_imag)


def inverse_front(pieces):
    extent = pieces[0].shape[0]
    pieces = contract("ub,kjvu->kjvb", dft_table(SPLIT_LO), pieces, True)
    pieces = rotate(pieces, row_turns(), True)
    pieces = contract("va,kjvb->kjab", dft_table(SPLIT_HI), pieces, True)
    leading = pieces[0].shape[:2]
    pieces = (pieces[0].reshape(leading + (LEN_ROWS,)), pieces[1].reshape(leading + (LEN_ROWS,)))
    frequency = lax.axis_index("coef") * extent + jnp.arange(extent, dtype=jnp.int32)
    cos_turn, sin_turn = phase_table(frequency, jnp.arange(LEN_ROWS, dtype=jnp.int32), LENGTH)
    pieces = rotate(pieces, (cos_turn[:, None, :], sin_turn[:, None, :]), True)
    return jnp.stack(pieces)


def inverse_first(received):
    pieces = contract("kn,kjm->jnm", dft_table(LEN_COLS), (received[0], received[1]), True)
    return jnp.stack(pieces)


def shards(coefficients, batch_weights, claimed, point_index, point_cycle):
    sectioned = first_section(coefficients)
    evaluations = second_section(
        lax.all_to_all(sectioned, "coef", split_axis=1, concat_axis=3, tiled=True)
    )
    offsets = jnp.sum(batch_weights[None] * claimed, axis=2)
    combined = jnp.einsum("jp,pnm->jnm", batch_weights, coefficients, precision=precise)
    combined_here, offsets_here = (
        lax.psum_scatter(combined, ("poly", "limb"), scatter_dimension=0, tiled=True),
        lax.psum_scatter(offsets, ("poly", "limb"), scatter_dimension=1, tiled=True),
    )
    column_sectioned = first_section(combined_here)
    numerator = second_section(
        lax.all_to_all(column_sectioned, "coef", split_axis=1, concat_axis=3, tiled=True)
    )
    numerator = numerator - offsets_here[:, None, :, None, None]
    quot_pieces = quotient_values(numerator, point_index, point_cycle)
    returned = inverse_front(quot_pieces)
    quotient = inverse_first(
        lax.all_to_all(returned, "coef", split_axis=3, concat_axis=1, tiled=True)
    )
    return (evaluations, quotient)


def solution(mesh):
    placed = (
        P(("parts", "poly", "limb"), None, "coef"),
        P("parts", ("poly", "limb")),
        P(None, "parts", ("poly", "limb")),
        P(("parts", "poly", "limb")),
        P(("parts", "poly", "limb")),
    )
    return jax.shard_map(
        shards,
        mesh=mesh,
        in_specs=placed,
        out_specs=(
            P(None, "coef", ("parts", "poly", "limb"), None, None),
            P(None, ("parts", "poly", "limb"), None, "coef"),
        ),
        check_vma=False,
    )
```

profile of v0, /device:TPU:0, one launch (start us, length us, event | category | flops | bytes accessed | tf_op | source)
XLA Modules:
  0.0 711.0 jit_solution(118447262701700206)
XLA Ops:
  7.2 15.2 %fusion = f32[16,128,1024]{2,0,1:T(8,128)S(1)} fusion(f32[12,128,1024]{2,1,0:T(8,128)} %param.5, f32[16,12]{1,0:T(8,128)} %param.6), kind=kOutput, calls=%fused_computation.3 | convolution fusion | flops 301989888 | bytes 14680832 | tf_op jit(solution)/shard_map/jp,pnm->jnm/dot_general | solution.py:129
  22.4 8.3 %copy.107 = f32[16,128,1024]{2,1,0:T(8,128)} copy(f32[16,128,1024]{2,0,1:T(8,128)S(1)} %fusion) | data formatting | bytes 16777216 | tf_op jit(solution)/shard_map/jp,pnm->jnm/dot_general | solution.py:129
  32.8 72.5 %reduce-scatter.3.cloned.1.call-done = f32[4,128,1024]{2,1,0:T(8,128)} async-done(((f32[16,128,1024]{2,1,0:T(8,128)}), f32[4,128,1024]{2,1,0:T(8,128)}) %reduce-scatter.3.cloned.1.call-update) | async-done | bytes 2097168 | tf_op jit(solution)/shard_map/reduce_scatter | solution.py:131
  105.3 3.8 fusion.57
  112.5 4.7 copy.108
  117.2 5.0 all-to-all-start.1
  122.2 8.6 %fusion.59 = f32[128,12,1024]{2,0,1:T(8,128)S(1)} fusion(f32[12,128,1024]{2,1,0:T(8,128)} %param.5), kind=kOutput, calls=%fused_computation.110 | convolution fusion | flops 2416164864 | bytes 12582912 | tf_op jit(solution)/shard_map/kn,pnm->kpm/dot_general | solution.py:71
  130.9 10.1 %add_bitcast_fusion.1 = (f32[1,128,12,1024]{3,1,2,0:T(8,128)}, f32[1,128,12,1024]{3,1,2,0:T(8,128)}) fusion(f32[128,12,1024]{2,0,1:T(8,128)S(1)} %fusion.59, f32[128,1024]{1,0:T(8,128)S(1)} %get-tuple-element.31, f32[128,1024]{1,0:T(8,128)S(1)} %get-tuple-element.30, f32[12,128,1024]{2,1,0:T(8,128)S(1)} %bitcast.217), kind=kOutput, calls=%fused_computation.14 | convolution fusion | flops 2427174912 | bytes 26214400 | tf_op jit(solution)/shard_map/kn,pnm->kpm/dot_general | solution.py:70
  141.0 12.1 %pad_maximum_fusion = f32[2,128,12,1024]{3,1,2,0:T(8,128)} fusion(f32[1,128,12,1024]{3,1,2,0:T(8,128)} %get-tuple-element.15, f32[1,128,12,1024]{3,1,2,0:T(8,128)} %get-tuple-element.14), kind=kLoop, calls=%fused_computation | loop fusion | flops 3145728 | bytes 25165824 | tf_op jit(solution)/shard_map/stack | solution.py:76
  153.2 22.0 %copy.100 = f32[2,128,12,1024]{3,0,2,1:T(2,128)} copy(f32[2,128,12,1024]{3,1,2,0:T(8,128)} %pad_maximum_fusion) | data formatting | bytes 25165824 | tf_op jit(solution)/shard_map/stack | solution.py:76
  175.3 40.4 %all-to-all-done.1 = f32[2,128,4,1024]{3,2,0,1:T(4,128)} async-done(((f32[2,128,4,1024]{3,2,0,1:T(4,128)}), f32[2,128,4,1024]{3,2,0,1:T(4,128)}, u32[]{:S(2)}, u32[]{:S(2)}) %all-to-all-start.1) | async-done | bytes 4194336 | tf_op jit(solution)/shard_map/all_to_all | solution.py:136
  215.7 6.3 all-to-all-start
  223.4 6.2 all-reduce
  229.9 3.1 fusion.28
  235.1 6.1 copy.163
  246.3 3.2 squeeze.28
  280.3 3.6 add_bitcast_fusion.3
  283.9 3.1 reshape.267
  287.0 3.9 fusion.11
  290.9 3.6 subtract_bitcast_fusion.3
  294.5 3.1 reshape.266
  297.6 3.9 multiply_add_fusion
  303.8 13.5 %copy.119 = f32[2,32,4,4096]{1,2,0,3:T(4,128)} copy(f32[2,32,4,4096]{3,1,2,0:T(8,128)} %pad_maximum_fusion.3) | data formatting | bytes 8388608 | tf_op jit(solution)/shard_map/stack | solution.py:115
  317.3 14.5 %reshape.286 = f32[4,1,262144]{2,1,0:T(1,128)} reshape(f32[4096,2,4,32]{3,2,1,0:T(4,128)} %bitcast.218) | data formatting | bytes 8388608
  331.8 162.7 %all-to-all-done = f32[2,128,12,1024]{3,0,2,1:T(2,128)} async-done(((f32[2,128,12,1024]{3,0,2,1:T(2,128)}), f32[2,128,12,1024]{3,0,2,1:T(2,128)}, u32[]{:S(2)}, u32[]{:S(2)}) %all-to-all-start) | async-done | bytes 12582944 | tf_op jit(solution)/shard_map/all_to_all | solution.py:126
  494.5 5.3 all-to-all-start.2
  499.8 16.4 %copy.162 = f32[2,4,32,12,1024]{4,1,3,2,0:T(4,128)} copy(f32[2,4,32,12,1024]{4,0,3,2,1:T(2,128)} %bitcast.4) | data formatting | bytes 25165824 | tf_op jit(solution)/shard_map/all_to_all | solution.py:126
  516.2 14.8 %fusion.266 = (f32[1,32,12,4,1024]{4,3,2,1,0:T(4,128)}, f32[1,32,12,4,1024]{4,3,2,1,0:T(4,128)}) fusion(f32[2,32,12,4,1024]{4,3,2,1,0:T(4,128)} %bitcast.224), kind=kLoop, calls=%fused_computation.337 | loop fusion | bytes 25165824 | tf_op jit(solution)/shard_map/slice | solution.py:82
  531.0 7.9 %squeeze.26 = f32[32,12,32,128]{3,2,1,0:T(8,128)} reshape(f32[1,32,12,4,1024]{4,3,2,1,0:T(4,128)} %get-tuple-element.16) | data formatting | bytes 12582912 | tf_op jit(solution)/shard_map/squeeze | solution.py:82
  538.9 8.0 %squeeze.27 = f32[32,12,32,128]{3,2,1,0:T(8,128)} reshape(f32[1,32,12,4,1024]{4,3,2,1,0:T(4,128)} %get-tuple-element.17) | data formatting | bytes 12582912 | tf_op jit(solution)/shard_map/squeeze | solution.py:82
  546.9 9.9 %fusion.82 = f32[32,12,128,32]{2,3,1,0:T(8,128)} fusion(f32[32,12,32,128]{3,2,1,0:T(8,128)} %squeeze.26), kind=kOutput, calls=%fused_computation.141 | convolution fusion | flops 603995136 | bytes 12582912 | tf_op jit(solution)/shard_map/va,kpab->kpvb/dot_general | solution.py:42
  556.8 7.6 %fusion.94 = f32[32,12,128,32]{2,3,1,0:T(8,128)} fusion(f32[32,12,32,128]{3,2,1,0:T(8,128)S(1)} %bitcast.221), kind=kOutput, calls=%fused_computation.153 | convolution fusion | flops 603995136 | bytes 12582912 | tf_op jit(solution)/shard_map/va,kpab->kpvb/dot_general | solution.py:42
  564.4 7.5 %fusion.84 = f32[32,12,128,32]{2,3,1,0:T(8,128)} fusion(f32[32,12,32,128]{3,2,1,0:T(8,128)S(1)} %bitcast.223), kind=kOutput, calls=%fused_computation.143 | convolution fusion | flops 603995136 | bytes 12582912 | tf_op jit(solution)/shard_map/va,kpab->kpvb/dot_general | solution.py:42
  571.9 12.9 %fusion.2 = (f32[32,12,32,128]{3,2,1,0:T(8,128)}, f32[32,12,32,128]{3,2,1,0:T(8,128)S(1)}) fusion(f32[32,128]{1,0:T(8,128)S(1)} %get-tuple-element.36, f32[32,128]{1,0:T(8,128)S(1)} %get-tuple-element.37, f32[32,12,128,32]{2,3,1,0:T(8,128)} %fusion.82, f32[32,12,128,32]{2,3,1,0:T(8,128)} %fusion.94, f32[32,12,128,32]{2,3,1,0:T(8,128)} %fusion.84, ...), kind=kOutput, calls=%fused_computation.7 | convolution fusion | flops 616578048 | bytes 37781504 | tf_op jit(solution)/shard_map/va,kpab->kpvb/dot_general | solution.py:42
  584.8 5.7 fusion.51
  590.6 5.7 fusion.53
  596.3 8.0 %subtract_bitcast_fusion = f32[1,32,12,32,128]{4,3,2,1,0:T(8,128)} fusion(f32[32,12,32,128]{3,2,1,0:T(8,128)S(1)} %fusion.51, f32[32,12,32,128]{3,2,1,0:T(8,128)S(1)} %copy-done), kind=kOutput, calls=%fused_computation.11 | convolution fusion | flops 2417737728 | bytes 18874368 | tf_op jit(solution)/shard_map/ub,kpvb->kpvu/dot_general | solution.py:42
  604.3 7.6 %add_bitcast_fusion = f32[1,32,12,32,128]{4,3,2,1,0:T(8,128)} fusion(f32[32,12,32,128]{3,2,1,0:T(8,128)S(1)} %fusion.53, f32[32,12,32,128]{3,2,1,0:T(8,128)S(1)} %get-tuple-element.13), kind=kOutput, calls=%fused_computation.12 | convolution fusion | flops 2417737728 | bytes 18874368 | tf_op jit(solution)/shard_map/ub,kpvb->kpvu/dot_general | solution.py:42
  611.9 12.2 %pad_maximum_fusion.1 = f32[2,32,12,32,128]{4,3,2,1,0:T(8,128)} fusion(f32[1,32,12,32,128]{4,3,2,1,0:T(8,128)} %subtract_bitcast_fusion, f32[1,32,12,32,128]{4,3,2,1,0:T(8,128)} %add_bitcast_fusion), kind=kLoop, calls=%fused_computation.1 | loop fusion | flops 3145728 | bytes 25165824 | tf_op jit(solution)/shard_map/stack | solution.py:85
  624.5 15.4 %reduce = f32[4,262144]{1,0:T(4,128)} reduce(f32[4,1,262144]{2,1,0:T(1,128)} %all-to-all-done.2, f32[]{:T(128)} %broadcast.735), dimensions={1}, to_apply=%all_to_all.39.reduce_sub_computation | reduce | bytes 8388612 | tf_op jit(solution)/shard_map/all_to_all | solution.py:142
  639.9 20.9 %reshape.287 = f32[4096,2,4,32]{3,2,1,0:T(4,128)} reshape(f32[4,262144]{1,0:T(4,128)} %reduce) | data formatting | bytes 8388608
  660.8 15.1 %copy.152 = f32[2,32,4,4,1024]{4,3,1,2,0:T(4,128)} copy(f32[2,32,4,4,1024]{1,2,0,4,3:T(4,128)} %bitcast.219) | data formatting | bytes 8388608 | tf_op jit(solution)/shard_map/all_to_all | solution.py:142
  675.9 3.2 fusion.267
  680.3 3.6 fusion.61
  685.1 3.6 fusion.63
  688.7 3.8 add_bitcast_fusion.2
  692.5 3.6 subtract_bitcast_fusion.2
  698.4 5.3 copy.127
  (81 shorter events, 51.7 us)
Async XLA Ops:
  7.2 98.1 %reduce-scatter.3.cloned.1.call-start = ((), (), s32[]{:S(2)}) async-start(), calls=%async_computation.4 | async-start | bytes 10485760 | tf_op jit(solution)/shard_map/reduce_scatter | solution.py:131
  105.3 3.9 copy-start.4
  117.2 13.7 %slice-start = ((s8[6291456]{0:T(1024)(128)(4,1)}), s8[2097152]{0:T(1024)(128)(4,1)S(1)}, s32[]{:S(2)}) async-start(s8[6291456]{0:T(1024)(128)(4,1)} %bitcast.216), calls=%async_computation.5 | async-start | bytes 4194304
  117.2 98.5 %all-to-all-start.1 = ((f32[2,128,4,1024]{3,2,0,1:T(4,128)}), f32[2,128,4,1024]{3,2,0,1:T(4,128)}, u32[]{:S(2)}, u32[]{:S(2)}) async-start(f32[2,128,4,1024]{3,2,0,1:T(4,128)} %copy.108), calls=%async_computation.2 | async-start | bytes 8388608 | tf_op jit(solution)/shard_map/all_to_all | solution.py:136
  122.2 8.7 %slice-start.1 = ((s8[6291456]{0:T(1024)(128)(4,1)}), s8[4194304]{0:T(1024)(128)(4,1)S(1)}, s32[]{:S(2)}) async-start(s8[6291456]{0:T(1024)(128)(4,1)} %bitcast.216), calls=%async_computation.6 | async-start | bytes 8388608
  175.2 46.8 %copy-start.8 = (f32[16,12]{1,0:T(8,128)S(1)}, f32[16,12]{1,0:T(8,128)}, u32[]{:S(2)}) copy-start(f32[16,12]{1,0:T(8,128)} %param.6) | copy-start | bytes 2308
  175.2 46.9 %copy-start.12 = (u32[32]{0:T(128)S(1)}, u32[32]{0:T(128)}, u32[]{:S(2)}) copy-start(u32[32]{0:T(128)} %constant.131) | copy-start | bytes 388
  175.2 48.1 %copy-start.9 = (f32[2,16,12]{1,0,2:T(2,128)S(1)}, f32[2,16,12]{1,0,2:T(2,128)}, u32[]{:S(2)}) copy-start(f32[2,16,12]{1,0,2:T(2,128)} %param.7) | copy-start | bytes 4612
  175.2 54.6 %copy-start.10 = (s32[4]{0:T(128)S(1)}, s32[4]{0:T(128)}, u32[]{:S(2)}) copy-start(s32[4]{0:T(128)} %param.8) | copy-start | bytes 52
  175.2 54.6 %copy-start.11 = (s32[4]{0:T(128)S(1)}, s32[4]{0:T(128)}, u32[]{:S(2)}) copy-start(s32[4]{0:T(128)} %param.9) | copy-start | bytes 52
  215.7 278.8 %all-to-all-start = ((f32[2,128,12,1024]{3,0,2,1:T(2,128)}), f32[2,128,12,1024]{3,0,2,1:T(2,128)}, u32[]{:S(2)}, u32[]{:S(2)}) async-start(f32[2,128,12,1024]{3,0,2,1:T(2,128)} %copy.100), calls=%async_computation | async-start | bytes 25165824 | tf_op jit(solution)/shard_map/all_to_all | solution.py:126
  249.6 2.0 copy-start.3
  266.9 1.0 copy-start.6
  266.9 1.2 copy-start.7
  278.1 2.2 copy-start.1
  287.0 3.9 copy-start.2
  294.5 3.1 copy-start.5
  494.5 129.5 %all-to-all-start.2 = ((f32[4,1,262144]{2,1,0:T(1,128)}), f32[4,1,262144]{2,1,0:T(1,128)}, u32[]{:S(2)}, u32[]{:S(2)}) async-start(f32[4,1,262144]{2,1,0:T(1,128)} %reshape.286), calls=%async_computation.3 | async-start | bytes 8388608 | tf_op jit(solution)/shard_map/all_to_all | solution.py:142
  538.9 17.9 %slice-start.2 = ((s8[6291456]{0:T(1024)(128)(4,1)}), s8[2097152]{0:T(1024)(128)(4,1)S(1)}, s32[]{:S(2)}) async-start(s8[6291456]{0:T(1024)(128)(4,1)} %bitcast.220), calls=%async_computation.7 | async-start | bytes 4194304
  546.9 9.9 %slice-start.3 = ((s8[6291456]{0:T(1024)(128)(4,1)}), s8[4194304]{0:T(1024)(128)(4,1)S(1)}, s32[]{:S(2)}) async-start(s8[6291456]{0:T(1024)(128)(4,1)} %bitcast.220), calls=%async_computation.8 | async-start | bytes 8388608
  546.9 17.5 %slice-start.4 = ((s8[6291456]{0:T(1024)(128)(4,1)}), s8[4194304]{0:T(1024)(128)(4,1)S(1)}, s32[]{:S(2)}) async-start(s8[6291456]{0:T(1024)(128)(4,1)} %bitcast.222), calls=%async_computation.9 | async-start | bytes 8388608
  556.8 7.6 %slice-start.5 = ((s8[6291456]{0:T(1024)(128)(4,1)}), s8[2097152]{0:T(1024)(128)(4,1)S(1)}, s32[]{:S(2)}) async-start(s8[6291456]{0:T(1024)(128)(4,1)} %bitcast.222), calls=%async_computation.10 | async-start | bytes 4194304
  584.8 5.7 copy-start
Sparse Core Ops, SparseCore 0:
  30.8 74.3 reduce-scatter.2
where the time goes:
time: 718 us; the launch traced here: 711 us
  waiting for transfers between devices  276 us (38%)
  local copies, waits for them, and re-layouts  180 us (25%)
  matrix products  159 us (22%)
  other arithmetic  58.2 us (8%)
  starting transfers between devices  16.6 us (2%)
  between operations  15.6 us (2%)
    all_to_all x1, waiting for transfers between devices, shards(): lax.all_to_all(sectioned, 'coef', split_axis=1, concat_axis=3, tiled=True)  163 us
    dot_general x28, matrix products, product(): return jnp.einsum(pattern, matrix, operand, precision=precise)  119 us
    reduce_scatter x1, waiting for transfers between devices, shards(): lax.psum_scatter(combined, ('poly', 'limb'), scatter_dimension=0, tiled=T...  72.5 us
    unnamed x44, local copies, waits for them, and re-layouts  42.1 us
    all_to_all x1, waiting for transfers between devices, shards(): lax.all_to_all(column_sectioned, 'coef', split_axis=1, concat_axis=3, til...  40.4 us
    another operation x2, local copies, waits for them, and re-layouts, first_section(): return jnp.stack(pieces)  26.8 us
    slice x2, local copies, waits for them, and re-layouts, second_section(): shaped[0]  17.8 us
    all_to_all x1, local copies, waits for them, and re-layouts, shards(): lax.all_to_all(sectioned, 'coef', split_axis=1, concat_axis=3, tiled=True)  16.4 us
  transfers between devices with their start and end apart: 4, of which 3 were waited for; matrix products, arithmetic and copies ran while one was open for 40% of the time, Pallas kernels for 0%

commit v1 on v0

v1 whole, which is shorter than its diff:
```python
import functools
import math

import jax
import jax.numpy as jnp
import ml_dtypes
import numpy as np
from jax import lax
from jax.experimental import pallas as pl
from jax.experimental.pallas import tpu as pltpu
from jax.sharding import PartitionSpec as P

LEN_COLS = 128
SPLIT_HI = 32
SPLIT_LO = 128
LEN_ROWS = 4096
LENGTH = 524288
VMEM_BYTES = 48 * 2**20

precise = lax.Precision.HIGHEST


def split(value):
    high = value.astype(jnp.bfloat16)
    low = (value - high.astype(jnp.float32)).astype(jnp.bfloat16)
    return high, low


def split_host(value):
    value = np.asarray(value, np.float32)
    high = value.astype(ml_dtypes.bfloat16)
    low = (value - high.astype(np.float32)).astype(ml_dtypes.bfloat16)
    return high, low


def roots(exponent, length):
    angles = np.asarray(exponent % length, np.float64) * (-2.0 * math.pi / length)
    return np.cos(angles), np.sin(angles)


def first_table(owners):
    index = np.arange(LEN_COLS, dtype=np.int64)
    pair = np.stack(roots(index[:, None] * index[None, :], LEN_COLS)) / math.sqrt(LEN_COLS)
    extent = LEN_COLS // owners
    table = pair.reshape(2, owners, extent, LEN_COLS).transpose(1, 0, 2, 3)
    table = table.reshape(2 * LEN_COLS, LEN_COLS)
    return np.concatenate([table, table]).astype(np.float32)


def middle_table(owners):
    frequency = np.arange(LEN_COLS, dtype=np.int64)
    extent = LEN_COLS // owners
    share = SPLIT_HI // owners
    sender = (frequency[:, None] // extent - np.arange(owners)[None, :]) % owners
    place = (sender[:, :, None] * share + np.arange(share)).reshape(LEN_COLS, 1, SPLIT_HI)
    slow = np.arange(SPLIT_HI, dtype=np.int64)[None, :, None]
    real, imag = roots(place * (LEN_COLS * slow + frequency[:, None, None]), LEN_ROWS)
    table = np.concatenate(
        [np.concatenate([real, -imag], axis=2), np.concatenate([imag, real], axis=2)], axis=1
    )
    high, low = split_host(table / math.sqrt(SPLIT_HI))
    return np.concatenate([high, low, high], axis=2)


def turn_table():
    frequency = np.arange(LEN_COLS, dtype=np.int64)[:, None, None]
    slow = np.arange(SPLIT_HI, dtype=np.int64)[None, :, None]
    fast = np.arange(SPLIT_LO, dtype=np.int64)[None, None, :]
    return np.stack(roots(fast * (frequency + LEN_COLS * slow), LENGTH), axis=1).astype(np.float32)


def last_table():
    index = np.arange(SPLIT_LO, dtype=np.int64)
    real, imag = roots(index[:, None] * index[None, :], SPLIT_LO)
    table = np.concatenate(
        [np.concatenate([real, imag], axis=1), np.concatenate([-imag, real], axis=1)], axis=0
    )
    high, low = split_host(table / math.sqrt(SPLIT_LO))
    return np.concatenate([high, high, low], axis=0)


def first_kernel(group, place_ref, table_ref, coeff_ref, *out_refs):
    owners = len(out_refs)
    rows = table_ref.shape[0] // 2
    each = rows // owners
    extent = each // 2
    begin = pl.multiple_of(place_ref[0] * each, each)
    high, low = split(table_ref[pl.ds(begin, rows), :])
    left = jnp.concatenate([high, low, high], axis=1)
    blocks = coeff_ref.shape[2] // SPLIT_LO
    step = min(2, blocks)
    for lane in range(0, blocks, step):
        value_high, value_low = split(coeff_ref[0, :, lane * SPLIT_LO:(lane + step) * SPLIT_LO])
        right = jnp.concatenate([value_high, value_high, value_low], axis=0)
        result = jnp.dot(left, right, preferred_element_type=jnp.float32)
        for inner in range(step):
            for owner in range(owners):
                for part in range(2):
                    for batch in range(extent // group):
                        top = owner * each + part * extent + batch * group
                        out_refs[owner][0, part, batch, pl.ds((lane + inner) * group, group), :] = result[
                            top:top + group, inner * SPLIT_LO:(inner + 1) * SPLIT_LO
                        ]


def first_section(place, table, coefficients, start, count, owners):
    rows_here = coefficients.shape[2]
    extent = LEN_COLS // owners
    group = min(8, extent)
    shape = (count, 2, extent // group, (rows_here // SPLIT_LO) * group, SPLIT_LO)
    return pl.pallas_call(
        functools.partial(first_kernel, group),
        out_shape=[jax.ShapeDtypeStruct(shape, jnp.float32)] * owners,
        grid_spec=pltpu.PrefetchScalarGridSpec(
            num_scalar_prefetch=1,
            grid=(count,),
            in_specs=[
                pl.BlockSpec(table.shape, lambda i, place: (0, 0)),
                pl.BlockSpec((1, LEN_COLS, rows_here), lambda i, place: (start + i, 0, 0)),
            ],
            out_specs=[pl.BlockSpec((1,) + shape[1:], lambda i, place: (i, 0, 0, 0, 0))] * owners,
        ),
        compiler_params=pltpu.CompilerParams(vmem_limit_bytes=VMEM_BYTES),
        cost_estimate=pl.CostEstimate(
            flops=count * 6 * 2 * LEN_COLS * LEN_COLS * rows_here,
            bytes_accessed=count * 12 * LEN_COLS * rows_here,
            transcendentals=0,
        ),
        name="first_section",
    )(place, table, coefficients)


def second_kernel(group, owners, aliased, place_ref, middle_ref, turn_ref, last_ref, *refs):
    piece_refs, out_ref = refs[:owners], refs[-1]
    count = out_ref.shape[2]
    share = SPLIT_HI // owners
    lines = []
    for item in range(group):
        columns = []
        for poly in range(count):
            pieces = []
            for part in range(2):
                for piece_ref in piece_refs:
                    if share == 1:
                        pieces.append(piece_ref[poly, part, 0, pl.ds(item, 1), :])
                    else:
                        pieces.append(piece_ref[poly, part, 0, pl.ds(item, share, stride=group), :])
            columns.append(jnp.concatenate(pieces, axis=0))
        gathered = columns[0] if count == 1 else jnp.concatenate(columns, axis=1)
        high, low = split(gathered)
        turned = jnp.dot(
            middle_ref[item], jnp.concatenate([high, high, low], axis=0), preferred_element_type=jnp.float32
        )
        cos_turn, sin_turn = turn_ref[item, 0], turn_ref[item, 1]
        for poly in range(count):
            lanes = slice(poly * SPLIT_LO, (poly + 1) * SPLIT_LO)
            real, imag = turned[:SPLIT_HI, lanes], turned[SPLIT_HI:, lanes]
            lines.append(
                jnp.concatenate([real * cos_turn - imag * sin_turn, real * sin_turn + imag * cos_turn], axis=1)
            )
    high, low = split(jnp.concatenate(lines, axis=0))
    result = jnp.dot(jnp.concatenate([high, low, high], axis=1), last_ref[...], preferred_element_type=jnp.float32)
    for item in range(group):
        for poly in range(count):
            top = (item * count + poly) * SPLIT_HI
            out_ref[0, item, poly] = result[top:top + SPLIT_HI, :SPLIT_LO]
            out_ref[1, item, poly] = result[top:top + SPLIT_HI, SPLIT_LO:]


def second_section(place, tables, pieces, previous, start, count, polys, owners):
    middle, turn, last = tables
    extent = LEN_COLS // owners
    group = min(8, extent)
    batches = extent // group
    block = (count, 2, 1) + pieces[0].shape[3:]
    in_specs = [
        pl.BlockSpec((group,) + middle.shape[1:], lambda i, place: (place[0] * batches + i, 0, 0)),
        pl.BlockSpec((group,) + turn.shape[1:], lambda i, place: (place[0] * batches + i, 0, 0, 0)),
        pl.BlockSpec(last.shape, lambda i, place: (0, 0)),
    ] + [pl.BlockSpec(block, lambda i, place: (0, 0, i, 0, 0))] * owners
    operands = [place, middle, turn, last] + list(pieces)
    aliases = {}
    if previous is not None:
        aliases = {len(operands): 0}
        operands.append(previous)
        in_specs.append(pl.BlockSpec(memory_space=pl.ANY))
    points = count * extent * LEN_ROWS
    return pl.pallas_call(
        functools.partial(second_kernel, group, owners, previous is not None),
        out_shape=jax.ShapeDtypeStruct((2, extent, polys, SPLIT_HI, SPLIT_LO), jnp.float32),
        grid_spec=pltpu.PrefetchScalarGridSpec(
            num_scalar_prefetch=1,
            grid=(batches,),
            in_specs=in_specs,
            out_specs=pl.BlockSpec(
                (2, group, count, SPLIT_HI, SPLIT_LO), lambda i, place: (0, i, start // count, 0, 0)
            ),
        ),
        input_output_aliases=aliases,
        compiler_params=pltpu.CompilerParams(vmem_limit_bytes=VMEM_BYTES),
        cost_estimate=pl.CostEstimate(
            flops=points * 6 * (4 * SPLIT_HI + 4 * SPLIT_LO), bytes_accessed=points * 24, transcendentals=0
        ),
        name="second_section",
    )(*operands)


def batch_kernel(weight_ref, coeff_ref, *out_refs):
    polys = coeff_ref.shape[0]
    columns = out_refs[0].shape[0]
    lanes = min(512, coeff_ref.shape[2])
    for top in range(0, coeff_ref.shape[1], 8):
        for lane in range(0, coeff_ref.shape[2], lanes):
            here = (slice(top, top + 8), slice(lane, lane + lanes))
            for target, out_ref in enumerate(out_refs):
                for column in range(columns):
                    row = target * columns + column
                    total = weight_ref[row, 0] * coeff_ref[(0,) + here]
                    for poly in range(1, polys):
                        total = total + weight_ref[row, poly] * coeff_ref[(poly,) + here]
                    out_ref[(column,) + here] = total


def batch_columns(weights, coefficients, targets):
    polys, extent, rows_here = coefficients.shape
    columns = weights.shape[0] // targets
    height = 16
    shape = (columns, extent, rows_here)
    return pl.pallas_call(
        batch_kernel,
        out_shape=[jax.ShapeDtypeStruct(shape, jnp.float32)] * targets,
        grid=(extent // height,),
        in_specs=[
            pl.BlockSpec(memory_space=pltpu.SMEM),
            pl.BlockSpec((polys, height, rows_here), lambda i: (0, i, 0)),
        ],
        out_specs=[pl.BlockSpec((columns, height, rows_here), lambda i: (0, i, 0))] * targets,
        compiler_params=pltpu.CompilerParams(vmem_limit_bytes=VMEM_BYTES),
        cost_estimate=pl.CostEstimate(
            flops=2 * weights.size * extent * rows_here,
            bytes_accessed=4 * (polys + weights.shape[0]) * extent * rows_here,
            transcendentals=0,
        ),
        name="batch_columns",
    )(weights, coefficients)


def filter_kernel(value_ref, table_ref, carry_ref, reach_ref, out_ref):
    table_high, table_low = split(table_ref[0])
    table = jnp.concatenate([table_high, table_high, table_low], axis=0)
    reach_real, reach_imag = reach_ref[0, 0:1, :], reach_ref[0, 1:2, :]
    blocks = value_ref.shape[2] // SPLIT_LO
    for block in range(blocks):
        lanes = slice(block * SPLIT_LO, (block + 1) * SPLIT_LO)
        high, low = split(value_ref[0, :, lanes])
        local = jnp.dot(jnp.concatenate([high, low, high], axis=1), table, preferred_element_type=jnp.float32)
        real = carry_ref[0, 0, :, block:block + 1]
        imag = carry_ref[1, 0, :, block:block + 1]
        out_ref[0, 0, :, lanes] = local[:, :SPLIT_LO] + (real * reach_real - imag * reach_imag)
        out_ref[1, 0, :, lanes] = local[:, SPLIT_LO:] + (real * reach_imag + imag * reach_real)


def filter_columns(values, table, carry, reach):
    columns, extent, rows_here = values.shape
    return pl.pallas_call(
        filter_kernel,
        out_shape=jax.ShapeDtypeStruct((2,) + values.shape, jnp.float32),
        grid=(columns,),
        in_specs=[
            pl.BlockSpec((1, extent, rows_here), lambda i: (i, 0, 0)),
            pl.BlockSpec((1,) + table.shape[1:], lambda i: (i, 0, 0)),
            pl.BlockSpec((2, 1) + carry.shape[2:], lambda i: (0, i, 0, 0)),
            pl.BlockSpec((1,) + reach.shape[1:], lambda i: (i, 0, 0)),
        ],
        out_specs=pl.BlockSpec((2, 1, extent, rows_here), lambda i: (0, i, 0, 0)),
        compiler_params=pltpu.CompilerParams(vmem_limit_bytes=VMEM_BYTES),
        cost_estimate=pl.CostEstimate(
            flops=6 * 2 * SPLIT_LO * values.size, bytes_accessed=12 * values.size, transcendentals=0
        ),
        name="filter_columns",
    )(values, table, carry, reach)


def times(left, right):
    return left[0] * right[0] - left[1] * right[1], left[0] * right[1] + left[1] * right[0]


def powers_of(point_index, point_cycle):
    decay = jnp.log1p((point_cycle.astype(jnp.float32) + 1.0) / 512.0)

    def powers(exponent):
        leading = (-1,) + (1,) * (exponent.ndim - 1)
        kept = jnp.exp(exponent.astype(jnp.float32) * -decay.reshape(leading))
        turns = (exponent * point_index.reshape(leading)) & (LENGTH - 1)
        angles = turns.astype(jnp.float32) * (2.0 * math.pi / LENGTH)
        return kept * jnp.cos(angles), kept * jnp.sin(angles)

    return powers


def masked(keep, pair):
    return jnp.where(keep, pair[0], 0.0), jnp.where(keep, pair[1], 0.0)


def quotient_columns(values, offsets, point_index, point_cycle):
    columns, extent, rows_here = values.shape
    blocks = rows_here // SPLIT_LO
    owners = LEN_ROWS // rows_here
    here = lax.axis_index("coef")
    powers = powers_of(point_index, point_cycle)

    offset = jnp.arange(rows_here, dtype=jnp.int32)[None, :, None]
    border = SPLIT_LO * (1 + jnp.arange(blocks, dtype=jnp.int32))[None, None, :]
    distance = border - 1 - offset
    weights = masked(distance >= 0, powers(jnp.maximum(distance, 0)))
    weights = jnp.concatenate(weights, axis=2)
    ends = jnp.einsum("jnm,jmq->jnq", values, weights, precision=precise)
    ends = ends.reshape(columns, extent, 2, blocks).transpose(2, 0, 1, 3)

    gathered = lax.all_gather(ends[:, :, :, blocks - 1], "coef", axis=0)
    owner = jnp.arange(owners, dtype=jnp.int32)
    weigh = powers(rows_here * (owners - 1 - owner)[None, :, None])
    segment = (gathered[:, 0].transpose(1, 0, 2), gathered[:, 1].transpose(1, 0, 2))
    row_end = times(weigh, segment)
    row_end = (jnp.sum(row_end[0], axis=1), jnp.sum(row_end[1], axis=1))
    radius = 1.0 + (point_cycle.astype(jnp.float32) + 1.0) / 512.0
    angle = point_index.astype(jnp.float32) * (2.0 * math.pi / LENGTH)
    point = (radius * jnp.cos(angle), -radius * jnp.sin(angle))
    shift = times(point, (offsets[0] * math.sqrt(LENGTH), offsets[1] * math.sqrt(LENGTH)))
    final = jnp.arange(extent, dtype=jnp.int32)[None, :] == extent - 1
    row_end = tuple(value - jnp.where(final, moved[:, None], 0.0) for value, moved in zip(row_end, shift))
    row = jnp.arange(extent, dtype=jnp.int32)
    since = (row[:, None] - row[None, :] - 1) % extent
    kernel = powers(LEN_ROWS * since[None])
    around = 1.0 / (1.0 - jnp.exp(-float(LENGTH) * jnp.log1p((point_cycle.astype(jnp.float32) + 1.0) / 512.0)))
    kernel = (kernel[0] * around[:, None, None], kernel[1] * around[:, None, None])

    def apply(matrix, vector):
        return jnp.sum(matrix * vector[:, None, :], axis=2)

    row_start = (
        apply(kernel[0], row_end[0]) - apply(kernel[1], row_end[1]),
        apply(kernel[0], row_end[1]) + apply(kernel[1], row_end[0]),
    )

    ahead = here - 1 - owner
    within = times(masked(ahead >= 0, powers(rows_here * jnp.maximum(ahead, 0)[None, :])), (1.0, 0.0))
    within = times((within[0][:, :, None], within[1][:, :, None]), segment)
    segment_start = times(powers((rows_here * here)[None, None]), row_start)
    segment_start = tuple(start + jnp.sum(part, axis=1) for start, part in zip(segment_start, within))
    block = SPLIT_LO * jnp.arange(blocks, dtype=jnp.int32)[None, None, :]
    carry = times(powers(block), (segment_start[0][:, :, None], segment_start[1][:, :, None]))
    carry = jnp.stack(carry) + jnp.pad(ends[:, :, :, : blocks - 1], ((0, 0), (0, 0), (0, 0), (1, 0)))

    lane = jnp.arange(SPLIT_LO, dtype=jnp.int32)
    apart = (lane[None, :] - lane[:, None])[None]
    inside = masked(apart >= 0, powers(jnp.maximum(apart, 0) + 1))
    table = -jnp.concatenate(inside, axis=2)
    reach = -jnp.stack(powers((lane + 2)[None, :]), axis=1)
    return filter_columns(values, table, carry, reach)


def chunk_sizes(polys):
    sizes = [1, 1]
    while sum(sizes) + 2 + 2 <= polys:
        sizes.append(2)
    while sum(sizes) < polys:
        sizes.append(1)
    return sizes


def exchange(pieces, owners):
    if owners <= 8:
        moved = [
            lax.ppermute(pieces[far], "coef", [(i, (i + far) % owners) for i in range(owners)])
            for far in range(1, owners)
        ]
        return [pieces[0]] + moved
    here = lax.axis_index("coef")
    stacked = jnp.stack(pieces)
    stacked = jnp.roll(stacked, here, axis=0)
    stacked = lax.all_to_all(stacked, "coef", split_axis=0, concat_axis=0, tiled=True)
    stacked = jnp.roll(stacked[::-1], here + 1, axis=0)
    return [stacked[far] for far in range(owners)]


def shift_sum(pieces, axis, size):
    total = pieces[0]
    for far in range(1, size):
        total = total + lax.ppermute(pieces[far], axis, [(i, (i + far) % size) for i in range(size)])
    return total


def shards(coefficients, batch_weights, claimed, point_index, point_cycle, sizes):
    owners, poly_size, limb_size = sizes
    polys = coefficients.shape[0]
    here = lax.axis_index("coef")
    place = here.astype(jnp.int32)[None]
    table = jnp.asarray(first_table(owners))
    tables = (jnp.asarray(middle_table(owners)), jnp.asarray(turn_table()), jnp.asarray(last_table()))

    chunks = []
    start = 0
    for count in chunk_sizes(polys):
        chunks.append((start, count))
        start += count

    arrived = []
    for number, (start, count) in enumerate(chunks):
        pieces = first_section(place, table, coefficients, start, count, owners)
        if number >= 2:
            pieces, arrived[number - 2] = lax.optimization_barrier((pieces, arrived[number - 2]))
        arrived.append(exchange(pieces, owners))

    targets = poly_size * limb_size
    columns = batch_weights.shape[0] // targets
    ahead = jnp.arange(poly_size, dtype=jnp.int32)[:, None] + lax.axis_index("poly")
    aside = jnp.arange(limb_size, dtype=jnp.int32)[None, :] + lax.axis_index("limb")
    target = ((ahead % poly_size) * limb_size + aside % limb_size).reshape(-1)
    ordered = batch_weights.reshape(targets, columns, polys)[target].reshape(batch_weights.shape)
    batched = batch_columns(ordered, coefficients, targets)
    by_poly = [
        shift_sum(batched[far * limb_size:(far + 1) * limb_size], "limb", limb_size) for far in range(poly_size)
    ]
    values = shift_sum(by_poly, "poly", poly_size)
    offsets = lax.psum(jnp.sum(batch_weights[None] * claimed, axis=2), ("poly", "limb"))
    me = lax.axis_index("poly") * limb_size + lax.axis_index("limb")
    offsets = lax.dynamic_slice_in_dim(offsets, me * columns, columns, axis=1)
    quotient = quotient_columns(values, offsets, point_index, point_cycle)

    evaluations = None
    for (start, count), pieces in zip(chunks, arrived):
        evaluations = second_section(place, tables, pieces, evaluations, start, count, polys, owners)
    return (evaluations, quotient)


def solution(mesh):
    placed = (
        P(("parts", "poly", "limb"), None, "coef"),
        P("parts", ("poly", "limb")),
        P(None, "parts", ("poly", "limb")),
        P(("parts", "poly", "limb")),
        P(("parts", "poly", "limb")),
    )
    sizes = tuple(mesh.shape[name] for name in ("coef", "poly", "limb"))
    return jax.shard_map(
        functools.partial(shards, sizes=sizes),
        mesh=mesh,
        in_specs=placed,
        out_specs=(
            P(None, "coef", ("parts", "poly", "limb"), None, None),
            P(None, ("parts", "poly", "limb"), None, "coef"),
        ),
        check_vma=False,
    )
```

time: 718 us -> 327 us (0.46)
  waiting for transfers between devices: 276 us -> 87.9 us
  local copies, waits for them, and re-layouts: 180 us -> 8.02 us
  matrix products: 159 us -> 1.89 us
  starting transfers between devices: 16.6 us -> 122 us
  Pallas kernels: 0 us -> 67.2 us
  other arithmetic: 58.2 us -> 18.1 us
  between operations: 15.6 us -> 1.18 us
  blocking collectives: 6.24 us -> 19.6 us
    all_to_all x3 -> x0, waiting for transfers between devices: 203 us -> none  [the longest x1 163 us: shards(): lax.all_to_all(sectioned, 'coef', split_axis=1, concat_axis=3, tiled=True)]
    dot_general x33 -> x1, matrix products: 159 us -> 1.89 us  [quotient_columns(): ends = jnp.einsum('jnm,jmq->jnq', values, weights, precision=precise)]
    ppermute x0 -> x27, starting transfers between devices: none -> 122 us  [the longest x24 120 us: exchange(): lax.ppermute(pieces[far], 'coef', [(i, (i + far) % owners) for i in range...]
    ppermute x0 -> x27, waiting for transfers between devices: none -> 87.9 us  [the longest x24 87.9 us: exchange(): lax.ppermute(pieces[far], 'coef', [(i, (i + far) % owners) for i in range...]
    reduce_scatter x1 -> x0, waiting for transfers between devices: 72.5 us -> none  [shards(): lax.psum_scatter(combined, ('poly', 'limb'), scatter_dimension=0, tiled=T...]
    pallas_call x0 -> x18, Pallas kernels: none -> 67.2 us  [the longest x8 37 us: second_section(): pl.pallas_call(functools.partial(second_kernel, group, owners, previous i...]
    another operation x3 -> x1, local copies, waits for them, and re-layouts: 40.3 us -> 0.2 us  [quotient_columns(): jnp.stack(carry)]
    all_to_all x4 -> x0, local copies, waits for them, and re-layouts: 38.1 us -> none  [the longest x1 16.4 us: shards(): lax.all_to_all(sectioned, 'coef', split_axis=1, concat_axis=3, tiled=True)]
  transfers between devices with their start and end apart: 4 -> 27, of which waited for: 3 -> 7; matrix products, arithmetic and copies ran while one was open for 40% -> 3% of each run, Pallas kernels for 0% -> 16%
where the time goes in v1:
time: 327 us; the launch traced here: 326 us
  starting transfers between devices  122 us (37%)
  waiting for transfers between devices  87.9 us (27%)
  Pallas kernels  67.2 us (21%)
  blocking collectives  19.6 us (6%)
  other arithmetic  18.1 us (6%)
  local copies, waits for them, and re-layouts  8.02 us (2%)
    ppermute x24, starting transfers between devices, exchange(): lax.ppermute(pieces[far], 'coef', [(i, (i + far) % owners) for i in range...  120 us
    ppermute x24, waiting for transfers between devices, exchange(): lax.ppermute(pieces[far], 'coef', [(i, (i + far) % owners) for i in range...  87.9 us
    pallas_call x8, Pallas kernels, second_section(): pl.pallas_call(functools.partial(second_kernel, group, owners, previous i...  37 us
    pallas_call x8, Pallas kernels, first_section(): pl.pallas_call(functools.partial(first_kernel, group), out_shape=[jax.Sha...  15.7 us
    all_gather x1, blocking collectives, quotient_columns(): gathered = lax.all_gather(ends[:, :, :, blocks - 1], 'coef', axis=0)  13.1 us
    pallas_call x1, Pallas kernels, batch_columns(): pl.pallas_call(batch_kernel, out_shape=[jax.ShapeDtypeStruct(shape, jnp.f...  11.2 us
  transfers between devices with their start and end apart: 27, of which 7 were waited for; matrix products, arithmetic and copies ran while one was open for 3% of the time, Pallas kernels for 16%

profile of v1, /device:TPU:0, one launch (start us, length us, event | category | flops | bytes accessed | tf_op | source)
XLA Modules:
  0.0 326.1 jit_solution(11659936264898596055)
XLA Ops:
  0.8 1.3 gather_fusion
  2.1 11.2 %batch_columns.1 = (f32[4,128,1024]{2,1,0:T(8,128)S(1)}, f32[4,128,1024]{2,1,0:T(8,128)}, f32[4,128,1024]{2,1,0:T(8,128)}, f32[4,128,1024]{2,1,0:T(8,128)}) custom-call(f32[16,12]{1,0:T(8,128)S(1)} %bitcast.34, f32[12,128,1024]{2,1,0:T(8,128)} %coeff_ref.17), custom_call_target="tpu_custom_call" | custom-call | flops 50331648 | bytes 14680064 | tf_op jit(solution)/shard_map/batch_columns/pallas_call | solution.py:229
  13.3 1.3 copy-done.4
  15.0 1.5 first_section.15
  16.5 2.6 collective-permute-start.12
  19.2 2.6 collective-permute-start.13
  21.7 1.3 collective-permute-start.14
  23.1 1.5 first_section.11
  26.1 6.4 %psum.7 = f32[2,16]{1,0:T(2,128)S(1)} all-reduce(f32[2,16]{1,0:T(2,128)S(1)} %multiply_reduce_fusion.4), channel_id=1, replica_groups=mesh['parts'=2,'coef'=4,'poly'=2,'limb'=2] {'poly','limb'}, use_global_device_ids=true, to_apply=%region_2.3 | all-reduce | flops 32 | bytes 256 | tf_op jit(solution)/shard_map/psum | solution.py:426
  33.2 2.0 first_section.14
  35.9 4.7 %collective-permute-start.1 = (f32[1,2,4,64,128]{4,3,2,1,0:T(8,128)S(1)}, f32[1,2,4,64,128]{4,3,2,1,0:T(8,128)S(1)}, u32[]{:S(2)}, u32[]{:S(2)}) collective-permute-start(f32[1,2,4,64,128]{4,3,2,1,0:T(8,128)S(1)} %get-tuple-element.100), channel_id=1, source_target_pairs={{0,8},{4,12},{8,0},{12,4},{1,9},{5,13},{9,1},{13,5},{2,10},{6,14},... | collective-permute-start | bytes 786440 | tf_op jit(solution)/shard_map/ppermute | solution.py:375
  40.6 14.9 %collective-permute-start.2 = (f32[1,2,4,64,128]{4,3,2,1,0:T(8,128)S(1)}, f32[1,2,4,64,128]{4,3,2,1,0:T(8,128)S(1)}, u32[]{:S(2)}, u32[]{:S(2)}) collective-permute-start(f32[1,2,4,64,128]{4,3,2,1,0:T(8,128)S(1)} %get-tuple-element.101), channel_id=1, source_target_pairs={{0,12},{4,0},{8,4},{12,8},{1,13},{5,1},{9,5},{13,9},{2,14},{6,2},{... | collective-permute-start | bytes 786440 | tf_op jit(solution)/shard_map/ppermute | solution.py:375
  55.5 7.0 %collective-permute-start.15 = (f32[2,2,4,64,128]{4,3,2,1,0:T(8,128)S(1)}, f32[2,2,4,64,128]{4,3,2,1,0:T(8,128)S(1)}, u32[]{:S(2)}, u32[]{:S(2)}) collective-permute-start(f32[2,2,4,64,128]{4,3,2,1,0:T(8,128)S(1)} %get-tuple-element.131), channel_id=1, source_target_pairs={{0,4},{4,8},{8,12},{12,0},{1,5},{5,9},{9,13},{13,1},{2,6},{6,10},{... | collective-permute-start | bytes 1572872 | tf_op jit(solution)/shard_map/ppermute | solution.py:375
  63.0 21.4 %collective-permute-done.1.refs_2_ = f32[1,2,4,64,128]{4,3,2,1,0:T(8,128)S(1)} collective-permute-done((f32[1,2,4,64,128]{4,3,2,1,0:T(8,128)S(1)}, f32[1,2,4,64,128]{4,3,2,1,0:T(8,128)S(1)}, u32[]{:S(2)}, u32[]{:S(2)}) %collective-permute-start.1) | collective-permute-done | bytes 262176 | tf_op jit(solution)/shard_map/ppermute | solution.py:375
  85.2 1.9 first_section.10
  87.9 2.8 collective-permute-start.3
  90.6 11.7 %collective-permute-start.4 = (f32[2,2,4,64,128]{4,3,2,1,0:T(8,128)S(1)}, f32[2,2,4,64,128]{4,3,2,1,0:T(8,128)S(1)}, u32[]{:S(2)}, u32[]{:S(2)}) collective-permute-start(f32[2,2,4,64,128]{4,3,2,1,0:T(8,128)S(1)} %get-tuple-element.104), channel_id=1, source_target_pairs={{0,8},{4,12},{8,0},{12,4},{1,9},{5,13},{9,1},{13,5},{2,10},{6,14},... | collective-permute-start | bytes 1572872 | tf_op jit(solution)/shard_map/ppermute | solution.py:375
  102.8 2.1 first_section.13
  105.1 3.4 %add.251 = f32[4,128,1024]{2,1,0:T(8,128)} add(f32[4,128,1024]{2,1,0:T(8,128)S(1)} %copy-done.32, f32[4,128,1024]{2,1,0:T(8,128)} %collective-permute-done.25) | non-fusion elementwise | flops 524288 | bytes 6291456 | tf_op jit(solution)/shard_map/add | solution.py:390
  108.4 15.4 %collective-permute-done.16.refs_2_ = f32[2,2,4,64,128]{4,3,2,1,0:T(8,128)S(1)} collective-permute-done((f32[2,2,4,64,128]{4,3,2,1,0:T(8,128)S(1)}, f32[2,2,4,64,128]{4,3,2,1,0:T(8,128)S(1)}, u32[]{:S(2)}, u32[]{:S(2)}) %collective-permute-start.16) | collective-permute-done | bytes 524320 | tf_op jit(solution)/shard_map/ppermute | solution.py:375
  123.9 1.5 collective-permute-start.26
  126.1 19.4 %collective-permute-start.18 = (f32[2,2,4,64,128]{4,3,2,1,0:T(8,128)S(1)}, f32[2,2,4,64,128]{4,3,2,1,0:T(8,128)S(1)}, u32[]{:S(2)}, u32[]{:S(2)}) collective-permute-start(f32[2,2,4,64,128]{4,3,2,1,0:T(8,128)S(1)} %get-tuple-element.135), channel_id=1, source_target_pairs={{0,4},{4,8},{8,12},{12,0},{1,5},{5,9},{9,13},{13,1},{2,6},{6,10},{... | collective-permute-start | bytes 1572872 | tf_op jit(solution)/shard_map/ppermute | solution.py:375
  145.4 12.2 %collective-permute-done.4.refs_2_ = f32[2,2,4,64,128]{4,3,2,1,0:T(8,128)S(1)} collective-permute-done((f32[2,2,4,64,128]{4,3,2,1,0:T(8,128)S(1)}, f32[2,2,4,64,128]{4,3,2,1,0:T(8,128)S(1)}, u32[]{:S(2)}, u32[]{:S(2)}) %collective-permute-start.4) | collective-permute-done | bytes 524320 | tf_op jit(solution)/shard_map/ppermute | solution.py:375
  157.6 1.9 collective-permute-start.20
  159.5 2.8 first_section.9
  163.1 27.3 %collective-permute-start.6 = (f32[2,2,4,64,128]{4,3,2,1,0:T(8,128)}, f32[2,2,4,64,128]{4,3,2,1,0:T(8,128)S(1)}, u32[]{:S(2)}, u32[]{:S(2)}) collective-permute-start(f32[2,2,4,64,128]{4,3,2,1,0:T(8,128)} %get-tuple-element.107), channel_id=1, source_target_pairs={{0,4},{4,8},{8,12},{12,0},{1,5},{5,9},{9,13},{13,1},{2,6},{6,10},{... | collective-permute-start | bytes 1572872 | tf_op jit(solution)/shard_map/ppermute | solution.py:375
  191.3 1.0 collective-permute-start.7
  192.3 21.4 %collective-permute-done.20.refs_3_ = f32[2,2,4,64,128]{4,3,2,1,0:T(8,128)S(1)} collective-permute-done((f32[2,2,4,64,128]{4,3,2,1,0:T(8,128)S(1)}, f32[2,2,4,64,128]{4,3,2,1,0:T(8,128)S(1)}, u32[]{:S(2)}, u32[]{:S(2)}) %collective-permute-start.20) | collective-permute-done | bytes 524320 | tf_op jit(solution)/shard_map/ppermute | solution.py:375
  213.7 2.3 first_section.12
  216.8 1.6 first_section.8
  221.2 14.3 %collective-permute-start.21 = (f32[1,2,4,64,128]{4,3,2,1,0:T(8,128)}, f32[1,2,4,64,128]{4,3,2,1,0:T(8,128)S(1)}, u32[]{:S(2)}, u32[]{:S(2)}) collective-permute-start(f32[1,2,4,64,128]{4,3,2,1,0:T(8,128)} %get-tuple-element.139), channel_id=1, source_target_pairs={{0,4},{4,8},{8,12},{12,0},{1,5},{5,9},{9,13},{13,1},{2,6},{6,10},{... | collective-permute-start | bytes 786440 | tf_op jit(solution)/shard_map/ppermute | solution.py:375
  237.3 15.8 %collective-permute-done.8.refs_3_ = f32[2,2,4,64,128]{4,3,2,1,0:T(8,128)S(1)} collective-permute-done((f32[2,2,4,64,128]{4,3,2,1,0:T(8,128)}, f32[2,2,4,64,128]{4,3,2,1,0:T(8,128)S(1)}, u32[]{:S(2)}, u32[]{:S(2)}) %collective-permute-start.8) | collective-permute-done | bytes 524320 | tf_op jit(solution)/shard_map/ppermute | solution.py:375
  253.1 2.0 collective-permute-start.23
  255.7 4.4 %second_section.8.refs_4_ = f32[2,32,12,32,128]{4,3,2,1,0:T(8,128)} custom-call(s32[1]{0:T(128)} %bitcast.place_ref, bf16[128,64,192]{2,1,0:T(8,128)(2,1)S(1)} %copy-done, f32[128,2,32,128]{3,2,1,0:T(8,128)} %constant.64.clone.turn_ref, bf16[768,256]{1,0:T(8,128)(2,1)S(1)} %copy-done.2, f32[1,2,4,64,128]{4,3,2,1,0:T(8,128)S(1)} %copy-done.7, ...), custom_call_target="tpu_custom_call" | custom-call | flops 503316480 | bytes 3145728 | tf_op jit(solution)/shard_map/second_section/pallas_call | solution.py:188
  260.1 4.3 %second_section.9.refs_4_ = f32[2,32,12,32,128]{4,3,2,1,0:T(8,128)} custom-call(s32[1]{0:T(128)} %bitcast.place_ref, bf16[128,64,192]{2,1,0:T(8,128)(2,1)S(1)} %copy-done, f32[128,2,32,128]{3,2,1,0:T(8,128)} %constant.64.clone.turn_ref, bf16[768,256]{1,0:T(8,128)(2,1)S(1)} %copy-done.2, ...), custom_call_target="tpu_custom_call", output_to_operand_aliasing={{}: (8, {})} | custom-call | flops 503316480 | bytes 3145728 | tf_op jit(solution)/shard_map/second_section/pallas_call | solution.py:188
  264.4 4.9 %second_section.10.refs_4_ = f32[2,32,12,32,128]{4,3,2,1,0:T(8,128)} custom-call(s32[1]{0:T(128)} %bitcast.place_ref, bf16[128,64,192]{2,1,0:T(8,128)(2,1)} %constant.63.clone.middle_ref, f32[128,2,32,128]{3,2,1,0:T(8,128)} %constant.64.clone.turn_ref, bf16[768,256]{1,0:T(8,128)(2,1)S(1)} %copy-done.2, ...), custom_call_target="tpu_custom_call", output_to_operand_aliasing={{}: (8, {})} | custom-call | flops 1006632960 | bytes 6291456 | tf_op jit(solution)/shard_map/second_section/pallas_call | solution.py:188
  269.3 2.1 collective-permute-start.10
  272.3 1.1 collective-permute-start.9
  273.5 4.8 %second_section.11.refs_4_ = f32[2,32,12,32,128]{4,3,2,1,0:T(8,128)} custom-call(s32[1]{0:T(128)} %bitcast.place_ref, bf16[128,64,192]{2,1,0:T(8,128)(2,1)} %constant.63.clone.middle_ref, f32[128,2,32,128]{3,2,1,0:T(8,128)} %constant.64.clone.turn_ref, bf16[768,256]{1,0:T(8,128)(2,1)S(1)} %copy-done.2, ...), custom_call_target="tpu_custom_call", output_to_operand_aliasing={{}: (8, {})} | custom-call | flops 1006632960 | bytes 6291456 | tf_op jit(solution)/shard_map/second_section/pallas_call | solution.py:188
  278.3 4.8 %second_section.12.refs_4_ = f32[2,32,12,32,128]{4,3,2,1,0:T(8,128)} custom-call(s32[1]{0:T(128)} %bitcast.place_ref, bf16[128,64,192]{2,1,0:T(8,128)(2,1)} %constant.63.clone.middle_ref, f32[128,2,32,128]{3,2,1,0:T(8,128)} %constant.64.clone.turn_ref, bf16[768,256]{1,0:T(8,128)(2,1)S(1)} %copy-done.2, ...), custom_call_target="tpu_custom_call", output_to_operand_aliasing={{}: (8, {})} | custom-call | flops 1006632960 | bytes 6291456 | tf_op jit(solution)/shard_map/second_section/pallas_call | solution.py:188
  283.1 5.0 %second_section.13.refs_4_ = f32[2,32,12,32,128]{4,3,2,1,0:T(8,128)} custom-call(s32[1]{0:T(128)} %bitcast.place_ref, bf16[128,64,192]{2,1,0:T(8,128)(2,1)} %constant.63.clone.middle_ref, f32[128,2,32,128]{3,2,1,0:T(8,128)} %constant.64.clone.turn_ref, bf16[768,256]{1,0:T(8,128)(2,1)S(1)} %copy-done.2, ...), custom_call_target="tpu_custom_call", output_to_operand_aliasing={{}: (8, {})} | custom-call | flops 1006632960 | bytes 6291456 | tf_op jit(solution)/shard_map/second_section/pallas_call | solution.py:188
  288.1 4.3 %second_section.14.refs_4_ = f32[2,32,12,32,128]{4,3,2,1,0:T(8,128)} custom-call(s32[1]{0:T(128)} %bitcast.place_ref, bf16[128,64,192]{2,1,0:T(8,128)(2,1)S(1)} %copy-done.1, f32[128,2,32,128]{3,2,1,0:T(8,128)} %constant.64.clone.turn_ref, bf16[768,256]{1,0:T(8,128)(2,1)S(1)} %copy-done.2, ...), custom_call_target="tpu_custom_call", output_to_operand_aliasing={{}: (8, {})} | custom-call | flops 503316480 | bytes 3145728 | tf_op jit(solution)/shard_map/second_section/pallas_call | solution.py:188
  292.5 4.4 %second_section.15 = f32[2,32,12,32,128]{4,3,2,1,0:T(8,128)} custom-call(s32[1]{0:T(128)} %bitcast.place_ref, bf16[128,64,192]{2,1,0:T(8,128)(2,1)S(1)} %copy-done.1, f32[128,2,32,128]{3,2,1,0:T(8,128)} %constant.64.clone.turn_ref, bf16[768,256]{1,0:T(8,128)(2,1)S(1)} %copy-done.2, ...), custom_call_target="tpu_custom_call", output_to_operand_aliasing={{}: (8, {})} | custom-call | flops 503316480 | bytes 3145728 | tf_op jit(solution)/shard_map/second_section/pallas_call | solution.py:188
  296.9 2.9 add_add_fusion.value_ref
  300.0 1.9 convolution_bitcast_fusion
  302.5 13.1 %all-gather = f32[8,4,128,1]{2,1,3,0:T(4,128)S(1)} all-gather(f32[2,4,128,1]{2,1,3,0:T(4,128)S(1)} %copy.31), channel_id=2, replica_groups=mesh['parts'=2,'coef'=4,'poly'=2,'limb'=2] {'coef'}, dimensions={0}, use_global_device_ids=true | all-gather | bytes 20480 | tf_op jit(solution)/shard_map/all_gather | solution.py:320
  315.9 3.9 %multiply_reduce_fusion.2 = (f32[4,128]{1,0:T(4,128)S(1)}, f32[4,128]{1,0:T(4,128)S(1)}, f32[4,128]{1,0:T(4,128)S(1)}, f32[4,128]{1,0:T(4,128)S(1)}, f32[4,128,128]{2,1,0:T(8,128)S(1)}, /*index=5*/f32[4,128,128]{2,1,0:T(8,128)}) fusion(f32[4,128]{1,0:T(4,128)S(1)} %get-tuple-element.209, f32[4]{0:T(128)} %get-tuple-element.210, ...), kind=kLoop, calls=%fused_computation.10 | loop fusion | flops 1701888 | bytes 815152 | tf_op jit(solution)/shard_map/reduce_sum | solution.py:339
  322.7 3.4 %filter_columns.1 = f32[2,4,128,1024]{3,2,1,0:T(8,128)} custom-call(f32[4,128,1024]{2,1,0:T(8,128)S(1)} %add_add_fusion.value_ref, f32[4,128,256]{2,1,0:T(8,128)S(1)} %maximum_negate_fusion.table_ref, f32[2,4,128,8]{3,2,1,0:T(8,128)S(1)} %pad_add_fusion.carry_ref, f32[4,2,128]{2,1,0:T(2,128)S(1)} %maximum_negate_fusion.1.reach_ref), custom_call_target="tpu_custom_call" | custom-call | flops 805306368 | bytes 6291456 | tf_op jit(solution)/shard_map/filter_columns/pallas_call | solution.py:265
  (160 shorter events, 19.0 us)
Async XLA Ops:
  2.1 13.0 %copy-start.3 = (f32[512,128]{1,0:T(8,128)S(1)}, f32[512,128]{1,0:T(8,128)}, u32[]{:S(2)}) copy-start(f32[512,128]{1,0:T(8,128)} %constant.59.clone.table_ref) | copy-start | bytes 786436
  14.6 87.8 %collective-permute-start.25 = (f32[4,128,1024]{2,1,0:T(8,128)}, f32[4,128,1024]{2,1,0:T(8,128)}, u32[]{:S(2)}, u32[]{:S(2)}) collective-permute-start(f32[4,128,1024]{2,1,0:T(8,128)} %get-tuple-element.169), channel_id=1, source_target_pairs={{0,1},{1,0},{2,3},{3,2},{4,5},{5,4},{6,7},{7,6},{8,9},{9,8},{10,11... | collective-permute-start | bytes 6291464 | tf_op jit(solution)/shard_map/ppermute | solution.py:390
  16.5 8.1 %copy-start.6 = (f32[1,2,4,64,128]{4,3,2,1,0:T(8,128)}, f32[1,2,4,64,128]{4,3,2,1,0:T(8,128)S(1)}, u32[]{:S(2)}) copy-start(f32[1,2,4,64,128]{4,3,2,1,0:T(8,128)S(1)} %get-tuple-element.162.refs_0_) | copy-start | bytes 786436
  16.5 19.3 %collective-permute-start.12 = (f32[1,2,4,64,128]{4,3,2,1,0:T(8,128)S(1)}, f32[1,2,4,64,128]{4,3,2,1,0:T(8,128)S(1)}, u32[]{:S(2)}, u32[]{:S(2)}) collective-permute-start(f32[1,2,4,64,128]{4,3,2,1,0:T(8,128)S(1)} %get-tuple-element.127), channel_id=1, source_target_pairs={{0,4},{4,8},{8,12},{12,0},{1,5},{5,9},{9,13},{13,1},{2,6},{6,10},{... | collective-permute-start | bytes 786440 | tf_op jit(solution)/shard_map/ppermute | solution.py:375
  19.2 21.4 %collective-permute-start.13 = (f32[1,2,4,64,128]{4,3,2,1,0:T(8,128)S(1)}, f32[1,2,4,64,128]{4,3,2,1,0:T(8,128)S(1)}, u32[]{:S(2)}, u32[]{:S(2)}) collective-permute-start(f32[1,2,4,64,128]{4,3,2,1,0:T(8,128)S(1)} %get-tuple-element.128), channel_id=1, source_target_pairs={{0,8},{4,12},{8,0},{12,4},{1,9},{5,13},{9,1},{13,5},{2,10},{6,14},... | collective-permute-start | bytes 786440 | tf_op jit(solution)/shard_map/ppermute | solution.py:375
  21.7 33.8 %collective-permute-start.14 = (f32[1,2,4,64,128]{4,3,2,1,0:T(8,128)S(1)}, f32[1,2,4,64,128]{4,3,2,1,0:T(8,128)S(1)}, u32[]{:S(2)}, u32[]{:S(2)}) collective-permute-start(f32[1,2,4,64,128]{4,3,2,1,0:T(8,128)S(1)} %get-tuple-element.129), channel_id=1, source_target_pairs={{0,12},{4,0},{8,4},{12,8},{1,13},{5,1},{9,5},{13,9},{2,14},{6,2},{... | collective-permute-start | bytes 786440 | tf_op jit(solution)/shard_map/ppermute | solution.py:375
  25.3 37.3 %collective-permute-start = (f32[1,2,4,64,128]{4,3,2,1,0:T(8,128)S(1)}, f32[1,2,4,64,128]{4,3,2,1,0:T(8,128)S(1)}, u32[]{:S(2)}, u32[]{:S(2)}) collective-permute-start(f32[1,2,4,64,128]{4,3,2,1,0:T(8,128)S(1)} %get-tuple-element.99), channel_id=1, source_target_pairs={{0,4},{4,8},{8,12},{12,0},{1,5},{5,9},{9,13},{13,1},{2,6},{6,10},{... | collective-permute-start | bytes 786440 | tf_op jit(solution)/shard_map/ppermute | solution.py:375
  35.9 51.2 %copy-start.8 = (f32[1,2,4,64,128]{4,3,2,1,0:T(8,128)}, f32[1,2,4,64,128]{4,3,2,1,0:T(8,128)S(1)}, u32[]{:S(2)}) copy-start(f32[1,2,4,64,128]{4,3,2,1,0:T(8,128)S(1)} %collective-permute-done.12.refs_1_) | copy-start | bytes 786436
  35.9 48.6 %collective-permute-start.1 = (f32[1,2,4,64,128]{4,3,2,1,0:T(8,128)S(1)}, f32[1,2,4,64,128]{4,3,2,1,0:T(8,128)S(1)}, u32[]{:S(2)}, u32[]{:S(2)}) collective-permute-start(f32[1,2,4,64,128]{4,3,2,1,0:T(8,128)S(1)} %get-tuple-element.100), channel_id=1, source_target_pairs={{0,8},{4,12},{8,0},{12,4},{1,9},{5,13},{9,1},{13,5},{2,10},{6,14},... | collective-permute-start | bytes 786440 | tf_op jit(solution)/shard_map/ppermute | solution.py:375
  40.6 46.6 %copy-start.10 = (f32[1,2,4,64,128]{4,3,2,1,0:T(8,128)}, f32[1,2,4,64,128]{4,3,2,1,0:T(8,128)S(1)}, u32[]{:S(2)}) copy-start(f32[1,2,4,64,128]{4,3,2,1,0:T(8,128)S(1)} %collective-permute-done.13.refs_2_) | copy-start | bytes 786436
  40.6 47.3 %collective-permute-start.2 = (f32[1,2,4,64,128]{4,3,2,1,0:T(8,128)S(1)}, f32[1,2,4,64,128]{4,3,2,1,0:T(8,128)S(1)}, u32[]{:S(2)}, u32[]{:S(2)}) collective-permute-start(f32[1,2,4,64,128]{4,3,2,1,0:T(8,128)S(1)} %get-tuple-element.101), channel_id=1, source_target_pairs={{0,12},{4,0},{8,4},{12,8},{1,13},{5,1},{9,5},{13,9},{2,14},{6,2},{... | collective-permute-start | bytes 786440 | tf_op jit(solution)/shard_map/ppermute | solution.py:375
  55.5 31.6 %copy-start.12 = (f32[1,2,4,64,128]{4,3,2,1,0:T(8,128)}, f32[1,2,4,64,128]{4,3,2,1,0:T(8,128)S(1)}, u32[]{:S(2)}) copy-start(f32[1,2,4,64,128]{4,3,2,1,0:T(8,128)S(1)} %collective-permute-done.14.refs_3_) | copy-start | bytes 786436
  55.5 35.1 %collective-permute-start.15 = (f32[2,2,4,64,128]{4,3,2,1,0:T(8,128)S(1)}, f32[2,2,4,64,128]{4,3,2,1,0:T(8,128)S(1)}, u32[]{:S(2)}, u32[]{:S(2)}) collective-permute-start(f32[2,2,4,64,128]{4,3,2,1,0:T(8,128)S(1)} %get-tuple-element.131), channel_id=1, source_target_pairs={{0,4},{4,8},{8,12},{12,0},{1,5},{5,9},{9,13},{13,1},{2,6},{6,10},{... | collective-permute-start | bytes 1572872 | tf_op jit(solution)/shard_map/ppermute | solution.py:375
  62.6 24.5 %copy-start.16 = (f32[1,2,4,64,128]{4,3,2,1,0:T(8,128)}, f32[1,2,4,64,128]{4,3,2,1,0:T(8,128)S(1)}, u32[]{:S(2)}) copy-start(f32[1,2,4,64,128]{4,3,2,1,0:T(8,128)S(1)} %collective-permute-done.refs_1_) | copy-start | bytes 786436
  62.6 61.2 %collective-permute-start.16 = (f32[2,2,4,64,128]{4,3,2,1,0:T(8,128)S(1)}, f32[2,2,4,64,128]{4,3,2,1,0:T(8,128)S(1)}, u32[]{:S(2)}, u32[]{:S(2)}) collective-permute-start(f32[2,2,4,64,128]{4,3,2,1,0:T(8,128)S(1)} %get-tuple-element.132), channel_id=1, source_target_pairs={{0,8},{4,12},{8,0},{12,4},{1,9},{5,13},{9,1},{13,5},{2,10},{6,14},... | collective-permute-start | bytes 1572872 | tf_op jit(solution)/shard_map/ppermute | solution.py:375
  85.2 38.7 %collective-permute-start.17 = (f32[2,2,4,64,128]{4,3,2,1,0:T(8,128)S(1)}, f32[2,2,4,64,128]{4,3,2,1,0:T(8,128)S(1)}, u32[]{:S(2)}, u32[]{:S(2)}) collective-permute-start(f32[2,2,4,64,128]{4,3,2,1,0:T(8,128)S(1)} %get-tuple-element.133), channel_id=1, source_target_pairs={{0,12},{4,0},{8,4},{12,8},{1,13},{5,1},{9,5},{13,9},{2,14},{6,2},{... | collective-permute-start | bytes 1572872 | tf_op jit(solution)/shard_map/ppermute | solution.py:375
  87.9 17.0 %copy-start.20 = (f32[1,2,4,64,128]{4,3,2,1,0:T(8,128)}, f32[1,2,4,64,128]{4,3,2,1,0:T(8,128)S(1)}, u32[]{:S(2)}) copy-start(f32[1,2,4,64,128]{4,3,2,1,0:T(8,128)S(1)} %collective-permute-done.2.refs_3_) | copy-start | bytes 786436
  87.9 38.2 %collective-permute-start.3 = (f32[2,2,4,64,128]{4,3,2,1,0:T(8,128)S(1)}, f32[2,2,4,64,128]{4,3,2,1,0:T(8,128)S(1)}, u32[]{:S(2)}, u32[]{:S(2)}) collective-permute-start(f32[2,2,4,64,128]{4,3,2,1,0:T(8,128)S(1)} %get-tuple-element.103), channel_id=1, source_target_pairs={{0,4},{4,8},{8,12},{12,0},{1,5},{5,9},{9,13},{13,1},{2,6},{6,10},{... | collective-permute-start | bytes 1572872 | tf_op jit(solution)/shard_map/ppermute | solution.py:375
  90.6 66.9 %collective-permute-start.4 = (f32[2,2,4,64,128]{4,3,2,1,0:T(8,128)S(1)}, f32[2,2,4,64,128]{4,3,2,1,0:T(8,128)S(1)}, u32[]{:S(2)}, u32[]{:S(2)}) collective-permute-start(f32[2,2,4,64,128]{4,3,2,1,0:T(8,128)S(1)} %get-tuple-element.104), channel_id=1, source_target_pairs={{0,8},{4,12},{8,0},{12,4},{1,9},{5,13},{9,1},{13,5},{2,10},{6,14},... | collective-permute-start | bytes 1572872 | tf_op jit(solution)/shard_map/ppermute | solution.py:375
  102.3 55.2 %collective-permute-start.5 = (f32[2,2,4,64,128]{4,3,2,1,0:T(8,128)S(1)}, f32[2,2,4,64,128]{4,3,2,1,0:T(8,128)S(1)}, u32[]{:S(2)}, u32[]{:S(2)}) collective-permute-start(f32[2,2,4,64,128]{4,3,2,1,0:T(8,128)S(1)} %get-tuple-element.105), channel_id=1, source_target_pairs={{0,12},{4,0},{8,4},{12,8},{1,13},{5,1},{9,5},{13,9},{2,14},{6,2},{... | collective-permute-start | bytes 1572872 | tf_op jit(solution)/shard_map/ppermute | solution.py:375
  123.9 173.1 %collective-permute-start.24 = (f32[4,128,1024]{2,1,0:T(8,128)}, f32[4,128,1024]{2,1,0:T(8,128)}, u32[]{:S(2)}, u32[]{:S(2)}) collective-permute-start(f32[4,128,1024]{2,1,0:T(8,128)} %get-tuple-element.167), channel_id=1, source_target_pairs={{0,1},{1,0},{2,3},{3,2},{4,5},{5,4},{6,7},{7,6},{8,9},{9,8},{10,11... | collective-permute-start | bytes 6291464 | tf_op jit(solution)/shard_map/ppermute | solution.py:390
  123.9 173.1 %collective-permute-start.26 = (f32[4,128,1024]{2,1,0:T(8,128)}, f32[4,128,1024]{2,1,0:T(8,128)}, u32[]{:S(2)}, u32[]{:S(2)}) collective-permute-start(f32[4,128,1024]{2,1,0:T(8,128)} %add.251), channel_id=1, source_target_pairs={{0,2},{2,0},{1,3},{3,1},{4,6},{6,4},{5,7},{7,5},{8,10},{10,8},{9,1... | collective-permute-start | bytes 6291464 | tf_op jit(solution)/shard_map/ppermute | solution.py:390
  126.1 37.0 %collective-permute-start.18 = (f32[2,2,4,64,128]{4,3,2,1,0:T(8,128)S(1)}, f32[2,2,4,64,128]{4,3,2,1,0:T(8,128)S(1)}, u32[]{:S(2)}, u32[]{:S(2)}) collective-permute-start(f32[2,2,4,64,128]{4,3,2,1,0:T(8,128)S(1)} %get-tuple-element.135), channel_id=1, source_target_pairs={{0,4},{4,8},{8,12},{12,0},{1,5},{5,9},{9,13},{13,1},{2,6},{6,10},{... | collective-permute-start | bytes 1572872 | tf_op jit(solution)/shard_map/ppermute | solution.py:375
  157.6 33.7 %collective-permute-start.19 = (f32[2,2,4,64,128]{4,3,2,1,0:T(8,128)S(1)}, f32[2,2,4,64,128]{4,3,2,1,0:T(8,128)S(1)}, u32[]{:S(2)}, u32[]{:S(2)}) collective-permute-start(f32[2,2,4,64,128]{4,3,2,1,0:T(8,128)S(1)} %get-tuple-element.136), channel_id=1, source_target_pairs={{0,8},{4,12},{8,0},{12,4},{1,9},{5,13},{9,1},{13,5},{2,10},{6,14},... | collective-permute-start | bytes 1572872 | tf_op jit(solution)/shard_map/ppermute | solution.py:375
  157.6 56.1 %collective-permute-start.20 = (f32[2,2,4,64,128]{4,3,2,1,0:T(8,128)S(1)}, f32[2,2,4,64,128]{4,3,2,1,0:T(8,128)S(1)}, u32[]{:S(2)}, u32[]{:S(2)}) collective-permute-start(f32[2,2,4,64,128]{4,3,2,1,0:T(8,128)S(1)} %get-tuple-element.137), channel_id=1, source_target_pairs={{0,12},{4,0},{8,4},{12,8},{1,13},{5,1},{9,5},{13,9},{2,14},{6,2},{... | collective-permute-start | bytes 1572872 | tf_op jit(solution)/shard_map/ppermute | solution.py:375
  163.1 58.1 %collective-permute-start.6 = (f32[2,2,4,64,128]{4,3,2,1,0:T(8,128)}, f32[2,2,4,64,128]{4,3,2,1,0:T(8,128)S(1)}, u32[]{:S(2)}, u32[]{:S(2)}) collective-permute-start(f32[2,2,4,64,128]{4,3,2,1,0:T(8,128)} %get-tuple-element.107), channel_id=1, source_target_pairs={{0,4},{4,8},{8,12},{12,0},{1,5},{5,9},{9,13},{13,1},{2,6},{6,10},{... | collective-permute-start | bytes 1572872 | tf_op jit(solution)/shard_map/ppermute | solution.py:375
  191.3 45.0 %collective-permute-start.7 = (f32[2,2,4,64,128]{4,3,2,1,0:T(8,128)}, f32[2,2,4,64,128]{4,3,2,1,0:T(8,128)S(1)}, u32[]{:S(2)}, u32[]{:S(2)}) collective-permute-start(f32[2,2,4,64,128]{4,3,2,1,0:T(8,128)} %get-tuple-element.108), channel_id=1, source_target_pairs={{0,8},{4,12},{8,0},{12,4},{1,9},{5,13},{9,1},{13,5},{2,10},{6,14},... | collective-permute-start | bytes 1572872 | tf_op jit(solution)/shard_map/ppermute | solution.py:375
  213.7 39.4 %collective-permute-start.8 = (f32[2,2,4,64,128]{4,3,2,1,0:T(8,128)}, f32[2,2,4,64,128]{4,3,2,1,0:T(8,128)S(1)}, u32[]{:S(2)}, u32[]{:S(2)}) collective-permute-start(f32[2,2,4,64,128]{4,3,2,1,0:T(8,128)} %get-tuple-element.109), channel_id=1, source_target_pairs={{0,12},{4,0},{8,4},{12,8},{1,13},{5,1},{9,5},{13,9},{2,14},{6,2},{... | collective-permute-start | bytes 1572872 | tf_op jit(solution)/shard_map/ppermute | solution.py:375
  216.7 38.9 %copy-start = (bf16[128,64,192]{2,1,0:T(8,128)(2,1)S(1)}, bf16[128,64,192]{2,1,0:T(8,128)(2,1)}, u32[]{:S(2)}) copy-start(bf16[128,64,192]{2,1,0:T(8,128)(2,1)} %constant.63.clone.middle_ref) | copy-start | bytes 9437188
  216.7 38.9 %copy-start.2 = (bf16[768,256]{1,0:T(8,128)(2,1)S(1)}, bf16[768,256]{1,0:T(8,128)(2,1)}, u32[]{:S(2)}) copy-start(bf16[768,256]{1,0:T(8,128)(2,1)} %constant.65.clone.last_ref) | copy-start | bytes 1179652
  216.8 38.9 %copy-start.7 = (f32[1,2,4,64,128]{4,3,2,1,0:T(8,128)S(1)}, f32[1,2,4,64,128]{4,3,2,1,0:T(8,128)}, u32[]{:S(2)}) copy-start(f32[1,2,4,64,128]{4,3,2,1,0:T(8,128)} %copy-done.6) | copy-start | bytes 786436
  216.8 38.9 %copy-start.9 = (f32[1,2,4,64,128]{4,3,2,1,0:T(8,128)S(1)}, f32[1,2,4,64,128]{4,3,2,1,0:T(8,128)}, u32[]{:S(2)}) copy-start(f32[1,2,4,64,128]{4,3,2,1,0:T(8,128)} %copy-done.8) | copy-start | bytes 786436
  216.8 38.9 %copy-start.11 = (f32[1,2,4,64,128]{4,3,2,1,0:T(8,128)S(1)}, f32[1,2,4,64,128]{4,3,2,1,0:T(8,128)}, u32[]{:S(2)}) copy-start(f32[1,2,4,64,128]{4,3,2,1,0:T(8,128)} %copy-done.10) | copy-start | bytes 786436
  216.8 38.9 %copy-start.13 = (f32[1,2,4,64,128]{4,3,2,1,0:T(8,128)S(1)}, f32[1,2,4,64,128]{4,3,2,1,0:T(8,128)}, u32[]{:S(2)}) copy-start(f32[1,2,4,64,128]{4,3,2,1,0:T(8,128)} %copy-done.12) | copy-start | bytes 786436
  220.5 39.5 %copy-start.22 = (f32[1,2,4,64,128]{4,3,2,1,0:T(8,128)}, f32[1,2,4,64,128]{4,3,2,1,0:T(8,128)S(1)}, u32[]{:S(2)}) copy-start(f32[1,2,4,64,128]{4,3,2,1,0:T(8,128)S(1)} %get-tuple-element.110.refs_0_) | copy-start | bytes 786436
  221.2 48.1 %collective-permute-start.21 = (f32[1,2,4,64,128]{4,3,2,1,0:T(8,128)}, f32[1,2,4,64,128]{4,3,2,1,0:T(8,128)S(1)}, u32[]{:S(2)}, u32[]{:S(2)}) collective-permute-start(f32[1,2,4,64,128]{4,3,2,1,0:T(8,128)} %get-tuple-element.139), channel_id=1, source_target_pairs={{0,4},{4,8},{8,12},{12,0},{1,5},{5,9},{9,13},{13,1},{2,6},{6,10},{... | collective-permute-start | bytes 786440 | tf_op jit(solution)/shard_map/ppermute | solution.py:375
  236.3 35.1 %collective-permute-start.22 = (f32[1,2,4,64,128]{4,3,2,1,0:T(8,128)}, f32[1,2,4,64,128]{4,3,2,1,0:T(8,128)S(1)}, u32[]{:S(2)}, u32[]{:S(2)}) collective-permute-start(f32[1,2,4,64,128]{4,3,2,1,0:T(8,128)} %get-tuple-element.140), channel_id=1, source_target_pairs={{0,8},{4,12},{8,0},{12,4},{1,9},{5,13},{9,1},{13,5},{2,10},{6,14},... | collective-permute-start | bytes 786440 | tf_op jit(solution)/shard_map/ppermute | solution.py:375
  253.1 19.3 %collective-permute-start.23 = (f32[1,2,4,64,128]{4,3,2,1,0:T(8,128)}, f32[1,2,4,64,128]{4,3,2,1,0:T(8,128)S(1)}, u32[]{:S(2)}, u32[]{:S(2)}) collective-permute-start(f32[1,2,4,64,128]{4,3,2,1,0:T(8,128)} %get-tuple-element.141), channel_id=1, source_target_pairs={{0,12},{4,0},{8,4},{12,8},{1,13},{5,1},{9,5},{13,9},{2,14},{6,2},{... | collective-permute-start | bytes 786440 | tf_op jit(solution)/shard_map/ppermute | solution.py:375
  269.3 23.1 %collective-permute-start.10 = (f32[1,2,4,64,128]{4,3,2,1,0:T(8,128)S(1)}, f32[1,2,4,64,128]{4,3,2,1,0:T(8,128)S(1)}, u32[]{:S(2)}, u32[]{:S(2)}) collective-permute-start(f32[1,2,4,64,128]{4,3,2,1,0:T(8,128)S(1)} %copy-done.31), channel_id=1, source_target_pairs={{0,8},{4,12},{8,0},{12,4},{1,9},{5,13},{9,1},{13,5},{2,10},{6,14},... | collective-permute-start | bytes 786440 | tf_op jit(solution)/shard_map/ppermute | solution.py:375
  271.4 21.1 %collective-permute-start.11 = (f32[1,2,4,64,128]{4,3,2,1,0:T(8,128)S(1)}, f32[1,2,4,64,128]{4,3,2,1,0:T(8,128)S(1)}, u32[]{:S(2)}, u32[]{:S(2)}) collective-permute-start(f32[1,2,4,64,128]{4,3,2,1,0:T(8,128)S(1)} %copy-done.29), channel_id=1, source_target_pairs={{0,12},{4,0},{8,4},{12,8},{1,13},{5,1},{9,5},{13,9},{2,14},{6,2},{... | collective-permute-start | bytes 786440 | tf_op jit(solution)/shard_map/ppermute | solution.py:375
  272.3 20.2 %collective-permute-start.9 = (f32[1,2,4,64,128]{4,3,2,1,0:T(8,128)S(1)}, f32[1,2,4,64,128]{4,3,2,1,0:T(8,128)S(1)}, u32[]{:S(2)}, u32[]{:S(2)}) collective-permute-start(f32[1,2,4,64,128]{4,3,2,1,0:T(8,128)S(1)} %copy-done.27), channel_id=1, source_target_pairs={{0,4},{4,8},{8,12},{12,0},{1,5},{5,9},{9,13},{13,1},{2,6},{6,10},{... | collective-permute-start | bytes 786440 | tf_op jit(solution)/shard_map/ppermute | solution.py:375
  299.9 15.7 %copy-start.36 = (f32[4,4]{1,0:T(4,128)S(1)}, f32[4,4]{1,0:T(4,128)}, u32[]{:S(2)}) copy-start(f32[4,4]{1,0:T(4,128)} %get-tuple-element.200) | copy-start | bytes 196
  299.9 15.7 %copy-start.37 = (f32[4,4]{1,0:T(4,128)S(1)}, f32[4,4]{1,0:T(4,128)}, u32[]{:S(2)}) copy-start(f32[4,4]{1,0:T(4,128)} %get-tuple-element.201) | copy-start | bytes 196
  299.9 15.7 %copy-start.38 = (f32[4,4]{1,0:T(4,128)S(1)}, f32[4,4]{1,0:T(4,128)}, u32[]{:S(2)}) copy-start(f32[4,4]{1,0:T(4,128)} %get-tuple-element.206) | copy-start | bytes 196
  299.9 15.7 %copy-start.39 = (f32[4,4]{1,0:T(4,128)S(1)}, f32[4,4]{1,0:T(4,128)}, u32[]{:S(2)}) copy-start(f32[4,4]{1,0:T(4,128)} %get-tuple-element.207) | copy-start | bytes 196
  299.9 15.8 %copy-start.40 = (f32[4]{0:T(128)S(1)}, f32[4]{0:T(128)}, u32[]{:S(2)}) copy-start(f32[4]{0:T(128)} %get-tuple-element.198) | copy-start | bytes 52
  299.9 15.8 %copy-start.41 = (f32[4]{0:T(128)S(1)}, f32[4]{0:T(128)}, u32[]{:S(2)}) copy-start(f32[4]{0:T(128)} %get-tuple-element.199) | copy-start | bytes 52
  299.9 15.8 %copy-start.43 = (pred[128]{0:T(512)(128)(4,1)S(1)}, pred[128]{0:T(512)(128)(4,1)}, u32[]{:S(2)}) copy-start(pred[128]{0:T(512)(128)(4,1)} %iota_compare_fusion) | copy-start | bytes 388
  (23 other events, 76.7 us)

commit v2 on v1

--- a/solution.py
+++ b/solution.py
@@ -16,6 +16,9 @@
 LEN_ROWS = 4096
 LENGTH = 524288
 VMEM_BYTES = 48 * 2**20
+
+SMALL_COST = pl.CostEstimate(flops=1, bytes_accessed=1, transcendentals=0)
+DEPTH = 4
 
 precise = lax.Precision.HIGHEST
 
@@ -79,12 +82,12 @@
     return np.concatenate([high, high, low], axis=0)
 
 
-def first_kernel(group, place_ref, table_ref, coeff_ref, *out_refs):
+def transform(group, table_ref, coeff_ref, out_refs):
     owners = len(out_refs)
     rows = table_ref.shape[0] // 2
     each = rows // owners
     extent = each // 2
-    begin = pl.multiple_of(place_ref[0] * each, each)
+    begin = pl.multiple_of(lax.axis_index("coef") * each, each)
     high, low = split(table_ref[pl.ds(begin, rows), :])
     left = jnp.concatenate([high, low, high], axis=1)
     blocks = coeff_ref.shape[2] // SPLIT_LO
@@ -103,51 +106,87 @@
                         ]
 
 
-def first_section(place, table, coefficients, start, count, owners):
-    rows_here = coefficients.shape[2]
+def batch(weight_ref, coeff_ref, out_refs):
+    polys = coeff_ref.shape[0]
+    lanes = min(512, coeff_ref.shape[2])
+    for top in range(0, coeff_ref.shape[1], 8):
+        for lane in range(0, coeff_ref.shape[2], lanes):
+            here = (slice(top, top + 8), slice(lane, lane + lanes))
+            for target, out_ref in enumerate(out_refs):
+                for column in range(out_ref.shape[0]):
+                    row = target * out_ref.shape[0] + column
+                    total = weight_ref[row, 0] * coeff_ref[(0,) + here]
+                    for poly in range(1, polys):
+                        total = total + weight_ref[row, poly] * coeff_ref[(poly,) + here]
+                    out_ref[(column,) + here] = total
+
+
+def first_kernel(group, table_ref, coeff_ref, *out_refs):
+    transform(group, table_ref, coeff_ref, out_refs)
+
+
+def first_batch_kernel(group, count, owners, table_ref, coeff_ref, weight_ref, rows_ref, *out_refs):
+    batch(weight_ref, rows_ref, out_refs[owners:])
+
+    @pl.when(pl.program_id(0) < count)
+    def _():
+        transform(group, table_ref, coeff_ref, out_refs[:owners])
+
+
+def first_section(table, coefficients, start, count, owners, weights=None, targets=1):
+    polys, _, rows_here = coefficients.shape
     extent = LEN_COLS // owners
     group = min(8, extent)
-    shape = (count, 2, extent // group, (rows_here // SPLIT_LO) * group, SPLIT_LO)
-    return pl.pallas_call(
-        functools.partial(first_kernel, group),
-        out_shape=[jax.ShapeDtypeStruct(shape, jnp.float32)] * owners,
-        grid_spec=pltpu.PrefetchScalarGridSpec(
-            num_scalar_prefetch=1,
-            grid=(count,),
-            in_specs=[
-                pl.BlockSpec(table.shape, lambda i, place: (0, 0)),
-                pl.BlockSpec((1, LEN_COLS, rows_here), lambda i, place: (start + i, 0, 0)),
-            ],
-            out_specs=[pl.BlockSpec((1,) + shape[1:], lambda i, place: (i, 0, 0, 0, 0))] * owners,
-        ),
-        compiler_params=pltpu.CompilerParams(vmem_limit_bytes=VMEM_BYTES),
-        cost_estimate=pl.CostEstimate(
-            flops=count * 6 * 2 * LEN_COLS * LEN_COLS * rows_here,
-            bytes_accessed=count * 12 * LEN_COLS * rows_here,
-            transcendentals=0,
-        ),
-        name="first_section",
-    )(place, table, coefficients)
-
-
-def second_kernel(group, owners, aliased, place_ref, middle_ref, turn_ref, last_ref, *refs):
+    shape = (1, 2, extent // group, (rows_here // SPLIT_LO) * group, SPLIT_LO)
+    steps = count
+    kernel = functools.partial(first_kernel, group)
+    in_specs = [
+        pl.BlockSpec(table.shape, lambda i: (0, 0)),
+        pl.BlockSpec((1, LEN_COLS, rows_here), lambda i: (start + jnp.minimum(i, count - 1), 0, 0)),
+    ]
+    out_specs = [pl.BlockSpec(shape, lambda i: (jnp.minimum(i, count - 1), 0, 0, 0, 0))] * owners
+    out_shape = [jax.ShapeDtypeStruct((count,) + shape[1:], jnp.float32)] * owners
+    operands = [table, coefficients]
+    if weights is not None:
+        columns = weights.shape[0] // targets
+        height = 16 if count <= LEN_COLS // 16 else 8
+        steps = LEN_COLS // height
+        kernel = functools.partial(first_batch_kernel, group, count, owners)
+        in_specs += [
+            pl.BlockSpec(memory_space=pltpu.SMEM),
+            pl.BlockSpec((polys, height, rows_here), lambda i: (0, i, 0)),
+        ]
+        out_specs += [pl.BlockSpec((columns, height, rows_here), lambda i: (0, i, 0))] * targets
+        out_shape += [jax.ShapeDtypeStruct((columns, LEN_COLS, rows_here), jnp.float32)] * targets
+        operands += [weights, coefficients]
+    return list(
+        pl.pallas_call(
+            kernel,
+            out_shape=out_shape,
+            grid=(steps,),
+            in_specs=in_specs,
+            out_specs=out_specs,
+            compiler_params=pltpu.CompilerParams(vmem_limit_bytes=VMEM_BYTES),
+            cost_estimate=SMALL_COST,
+            name="first_section",
+        )(*operands)
+    )
+
+
+def second_kernel(group, owners, middle_ref, turn_ref, last_ref, *refs):
     piece_refs, out_ref = refs[:owners], refs[-1]
     count = out_ref.shape[2]
     share = SPLIT_HI // owners
     lines = []
     for item in range(group):
-        columns = []
-        for poly in range(count):
-            pieces = []
-            for part in range(2):
-                for piece_ref in piece_refs:
-                    if share == 1:
-                        pieces.append(piece_ref[poly, part, 0, pl.ds(item, 1), :])
-                    else:
-                        pieces.append(piece_ref[poly, part, 0, pl.ds(item, share, stride=group), :])
-            columns.append(jnp.concatenate(pieces, axis=0))
-        gathered = columns[0] if count == 1 else jnp.concatenate(columns, axis=1)
-        high, low = split(gathered)
+        places = pl.ds(item, 1) if share == 1 else pl.ds(item, share, stride=group)
+        gathered = [
+            jnp.concatenate(
+                [piece_ref[poly, part, 0, places, :] for part in range(2) for piece_ref in piece_refs], axis=0
+            )
+            for poly in range(count)
+        ]
+        high, low = split(gathered[0] if count == 1 else jnp.concatenate(gathered, axis=1))
         turned = jnp.dot(
             middle_ref[item], jnp.concatenate([high, high, low], axis=0), preferred_element_type=jnp.float32
         )
@@ -167,82 +206,35 @@
             out_ref[1, item, poly] = result[top:top + SPLIT_HI, SPLIT_LO:]
 
 
-def second_section(place, tables, pieces, previous, start, count, polys, owners):
+def second_section(tables, pieces, previous, start, count, polys, owners):
     middle, turn, last = tables
     extent = LEN_COLS // owners
     group = min(8, extent)
-    batches = extent // group
-    block = (count, 2, 1) + pieces[0].shape[3:]
+    together = 2 if start % 2 == 0 and count % 2 == 0 else 1
+    first = start // together
+    block = (together, 2, 1) + pieces[0].shape[3:]
     in_specs = [
-        pl.BlockSpec((group,) + middle.shape[1:], lambda i, place: (place[0] * batches + i, 0, 0)),
-        pl.BlockSpec((group,) + turn.shape[1:], lambda i, place: (place[0] * batches + i, 0, 0, 0)),
-        pl.BlockSpec(last.shape, lambda i, place: (0, 0)),
-    ] + [pl.BlockSpec(block, lambda i, place: (0, 0, i, 0, 0))] * owners
-    operands = [place, middle, turn, last] + list(pieces)
+        pl.BlockSpec((group,) + middle.shape[1:], lambda i, j: (i, 0, 0)),
+        pl.BlockSpec((group,) + turn.shape[1:], lambda i, j: (i, 0, 0, 0)),
+        pl.BlockSpec(last.shape, lambda i, j: (0, 0)),
+    ] + [pl.BlockSpec(block, lambda i, j: (j, 0, i, 0, 0))] * owners
+    operands = [middle, turn, last] + list(pieces)
     aliases = {}
     if previous is not None:
         aliases = {len(operands): 0}
         operands.append(previous)
         in_specs.append(pl.BlockSpec(memory_space=pl.ANY))
-    points = count * extent * LEN_ROWS
     return pl.pallas_call(
-        functools.partial(second_kernel, group, owners, previous is not None),
+        functools.partial(second_kernel, group, owners),
         out_shape=jax.ShapeDtypeStruct((2, extent, polys, SPLIT_HI, SPLIT_LO), jnp.float32),
-        grid_spec=pltpu.PrefetchScalarGridSpec(
-            num_scalar_prefetch=1,
-            grid=(batches,),
-            in_specs=in_specs,
-            out_specs=pl.BlockSpec(
-                (2, group, count, SPLIT_HI, SPLIT_LO), lambda i, place: (0, i, start // count, 0, 0)
-            ),
-        ),
+        grid=(extent // group, count // together),
+        in_specs=in_specs,
+        out_specs=pl.BlockSpec((2, group, together, SPLIT_HI, SPLIT_LO), lambda i, j: (0, i, first + j, 0, 0)),
         input_output_aliases=aliases,
         compiler_params=pltpu.CompilerParams(vmem_limit_bytes=VMEM_BYTES),
-        cost_estimate=pl.CostEstimate(
-            flops=points * 6 * (4 * SPLIT_HI + 4 * SPLIT_LO), bytes_accessed=points * 24, transcendentals=0
-        ),
+        cost_estimate=SMALL_COST,
         name="second_section",
     )(*operands)
-
-
-def batch_kernel(weight_ref, coeff_ref, *out_refs):
-    polys = coeff_ref.shape[0]
-    columns = out_refs[0].shape[0]
-    lanes = min(512, coeff_ref.shape[2])
-    for top in range(0, coeff_ref.shape[1], 8):
-        for lane in range(0, coeff_ref.shape[2], lanes):
-            here = (slice(top, top + 8), slice(lane, lane + lanes))
-            for target, out_ref in enumerate(out_refs):
-                for column in range(columns):
-                    row = target * columns + column
-                    total = weight_ref[row, 0] * coeff_ref[(0,) + here]
-                    for poly in range(1, polys):
-                        total = total + weight_ref[row, poly] * coeff_ref[(poly,) + here]
-                    out_ref[(column,) + here] = total
-
-
-def batch_columns(weights, coefficients, targets):
-    polys, extent, rows_here = coefficients.shape
-    columns = weights.shape[0] // targets
-    height = 16
-    shape = (columns, extent, rows_here)
-    return pl.pallas_call(
-        batch_kernel,
-        out_shape=[jax.ShapeDtypeStruct(shape, jnp.float32)] * targets,
-        grid=(extent // height,),
-        in_specs=[
-            pl.BlockSpec(memory_space=pltpu.SMEM),
-            pl.BlockSpec((polys, height, rows_here), lambda i: (0, i, 0)),
-        ],
-        out_specs=[pl.BlockSpec((columns, height, rows_here), lambda i: (0, i, 0))] * targets,
-        compiler_params=pltpu.CompilerParams(vmem_limit_bytes=VMEM_BYTES),
-        cost_estimate=pl.CostEstimate(
-            flops=2 * weights.size * extent * rows_here,
-            bytes_accessed=4 * (polys + weights.shape[0]) * extent * rows_here,
-            transcendentals=0,
-        ),
-        name="batch_columns",
-    )(weights, coefficients)
 
 
 def filter_kernel(value_ref, table_ref, carry_ref, reach_ref, out_ref):
@@ -274,9 +266,7 @@
         ],
         out_specs=pl.BlockSpec((2, 1, extent, rows_here), lambda i: (0, i, 0, 0)),
         compiler_params=pltpu.CompilerParams(vmem_limit_bytes=VMEM_BYTES),
-        cost_estimate=pl.CostEstimate(
-            flops=6 * 2 * SPLIT_LO * values.size, bytes_accessed=12 * values.size, transcendentals=0
-        ),
+        cost_estimate=SMALL_COST,
         name="filter_columns",
     )(values, table, carry, reach)
 
@@ -302,23 +292,37 @@
     return jnp.where(keep, pair[0], 0.0), jnp.where(keep, pair[1], 0.0)
 
 
-def quotient_columns(values, offsets, point_index, point_cycle):
+def segment_states(values, point_index, point_cycle):
     columns, extent, rows_here = values.shape
     blocks = rows_here // SPLIT_LO
-    owners = LEN_ROWS // rows_here
-    here = lax.axis_index("coef")
     powers = powers_of(point_index, point_cycle)
-
     offset = jnp.arange(rows_here, dtype=jnp.int32)[None, :, None]
     border = SPLIT_LO * (1 + jnp.arange(blocks, dtype=jnp.int32))[None, None, :]
     distance = border - 1 - offset
     weights = masked(distance >= 0, powers(jnp.maximum(distance, 0)))
     weights = jnp.concatenate(weights, axis=2)
     ends = jnp.einsum("jnm,jmq->jnq", values, weights, precision=precise)
-    ends = ends.reshape(columns, extent, 2, blocks).transpose(2, 0, 1, 3)
-
-    gathered = lax.all_gather(ends[:, :, :, blocks - 1], "coef", axis=0)
-    owner = jnp.arange(owners, dtype=jnp.int32)
+    return ends.reshape(columns, extent, 2, blocks).transpose(2, 0, 1, 3)
+
+
+def from_all_owners(ends):
+    owners = LEN_ROWS // (ends.shape[3] * SPLIT_LO)
+    last = ends[:, :, :, -1]
+    if owners <= 8:
+        moved = [lax.ppermute(last, "coef", [(i, (i + far) % owners) for i in range(owners)]) for far in range(1, owners)]
+        return jnp.stack([last] + moved)
+    gathered = lax.all_gather(last, "coef", axis=0)
+    return gathered[(lax.axis_index("coef") - jnp.arange(owners)) % owners]
+
+
+def quotient_columns(values, ends, gathered, offsets, point_index, point_cycle):
+    columns, extent, rows_here = values.shape
+    blocks = rows_here // SPLIT_LO
+    owners = LEN_ROWS // rows_here
+    here = lax.axis_index("coef")
+    powers = powers_of(point_index, point_cycle)
+
+    owner = (here - jnp.arange(owners, dtype=jnp.int32)) % owners
     weigh = powers(rows_here * (owners - 1 - owner)[None, :, None])
     segment = (gathered[:, 0].transpose(1, 0, 2), gathered[:, 1].transpose(1, 0, 2))
     row_end = times(weigh, segment)
@@ -361,30 +365,30 @@
 
 
 def chunk_sizes(polys):
-    sizes = [1, 1]
-    while sum(sizes) + 2 + 2 <= polys:
-        sizes.append(2)
-    while sum(sizes) < polys:
-        sizes.append(1)
-    return sizes
-
-
-def exchange(pieces, owners):
+    most = (polys - 4) // 2
+    return [1, most, polys - 4 - most, 2, 1] if polys > 6 else [1, 1, 2, 1, 1]
+
+
+def exchange(pieces, owners, sent):
     if owners <= 8:
-        moved = [
-            lax.ppermute(pieces[far], "coef", [(i, (i + far) % owners) for i in range(owners)])
-            for far in range(1, owners)
-        ]
-        return [pieces[0]] + moved
+        moved = [pieces[0]]
+        for far in range(1, owners):
+            piece = pieces[far]
+            if len(sent) >= DEPTH:
+                chunk, place = sent[-DEPTH]
+                piece, chunk[place] = lax.optimization_barrier((piece, chunk[place]))
+            moved.append(lax.ppermute(piece, "coef", [(i, (i + far) % owners) for i in range(owners)]))
+            sent.append((moved, far))
+        return moved
     here = lax.axis_index("coef")
-    stacked = jnp.stack(pieces)
-    stacked = jnp.roll(stacked, here, axis=0)
+    stacked = jnp.roll(jnp.stack(pieces), here, axis=0)
     stacked = lax.all_to_all(stacked, "coef", split_axis=0, concat_axis=0, tiled=True)
     stacked = jnp.roll(stacked[::-1], here + 1, axis=0)
     return [stacked[far] for far in range(owners)]
 
 
-def shift_sum(pieces, axis, size):
+def shift_sum(pieces, axis):
+    size = len(pieces)
     total = pieces[0]
     for far in range(1, size):
         total = total + lax.ppermute(pieces[far], axis, [(i, (i + far) % size) for i in range(size)])
@@ -394,10 +398,14 @@
 def shards(coefficients, batch_weights, claimed, point_index, point_cycle, sizes):
     owners, poly_size, limb_size = sizes
     polys = coefficients.shape[0]
-    here = lax.axis_index("coef")
-    place = here.astype(jnp.int32)[None]
+    extent = LEN_COLS // owners
     table = jnp.asarray(first_table(owners))
-    tables = (jnp.asarray(middle_table(owners)), jnp.asarray(turn_table()), jnp.asarray(last_table()))
+    begin = lax.axis_index("coef") * extent
+    tables = (
+        lax.dynamic_slice_in_dim(jnp.asarray(middle_table(owners)), begin, extent, axis=0),
+        lax.dynamic_slice_in_dim(jnp.asarray(turn_table()), begin, extent, axis=0),
+        jnp.asarray(last_table()),
+    )
 
     chunks = []
     start = 0
@@ -405,32 +413,43 @@
         chunks.append((start, count))
         start += count
 
+    columns = batch_weights.shape[0] // (poly_size * limb_size)
+    me_poly, me_limb = lax.axis_index("poly"), lax.axis_index("limb")
+    ahead = (me_poly + jnp.arange(poly_size, dtype=jnp.int32)[None, :]) % poly_size
+    aside = (me_limb + jnp.arange(limb_size, dtype=jnp.int32)[:, None]) % limb_size
+    target = (ahead * limb_size + aside).reshape(-1)
+    weights = batch_weights.reshape(-1, columns, polys)[target].reshape(batch_weights.shape)
+
     arrived = []
+    sent = []
+    used = 0
+    evaluations = None
     for number, (start, count) in enumerate(chunks):
-        pieces = first_section(place, table, coefficients, start, count, owners)
-        if number >= 2:
-            pieces, arrived[number - 2] = lax.optimization_barrier((pieces, arrived[number - 2]))
-        arrived.append(exchange(pieces, owners))
-
-    targets = poly_size * limb_size
-    columns = batch_weights.shape[0] // targets
-    ahead = jnp.arange(poly_size, dtype=jnp.int32)[:, None] + lax.axis_index("poly")
-    aside = jnp.arange(limb_size, dtype=jnp.int32)[None, :] + lax.axis_index("limb")
-    target = ((ahead % poly_size) * limb_size + aside % limb_size).reshape(-1)
-    ordered = batch_weights.reshape(targets, columns, polys)[target].reshape(batch_weights.shape)
-    batched = batch_columns(ordered, coefficients, targets)
-    by_poly = [
-        shift_sum(batched[far * limb_size:(far + 1) * limb_size], "limb", limb_size) for far in range(poly_size)
-    ]
-    values = shift_sum(by_poly, "poly", poly_size)
-    offsets = lax.psum(jnp.sum(batch_weights[None] * claimed, axis=2), ("poly", "limb"))
-    me = lax.axis_index("poly") * limb_size + lax.axis_index("limb")
-    offsets = lax.dynamic_slice_in_dim(offsets, me * columns, columns, axis=1)
-    quotient = quotient_columns(values, offsets, point_index, point_cycle)
-
-    evaluations = None
-    for (start, count), pieces in zip(chunks, arrived):
-        evaluations = second_section(place, tables, pieces, evaluations, start, count, polys, owners)
+        batched = (weights, limb_size) if number == 1 else ()
+        pieces = first_section(table, coefficients, start, count, owners, *batched)
+        if number == 3:
+            values = shift_sum([sums[i * columns:(i + 1) * columns] for i in range(poly_size)], "poly")
+            ends = segment_states(values, point_index, point_cycle)
+            pieces, ends = lax.optimization_barrier((pieces, ends))
+        if number == len(chunks) - 1:
+            while used < number - 2:
+                evaluations = second_section(tables, arrived[used], evaluations, *chunks[used], polys, owners)
+                used += 1
+            gathered = from_all_owners(ends)
+            quotient = quotient_columns(values, ends, gathered, offsets, point_index, point_cycle)
+            pieces, quotient, evaluations = lax.optimization_barrier((pieces, quotient, evaluations))
+        arrived.append(exchange(pieces[:owners], owners, sent))
+        if number == 1:
+            offsets = jnp.sum(batch_weights[None] * claimed, axis=2)
+            pieces[owners:], arrived[0][1:], offsets = lax.optimization_barrier(
+                (pieces[owners:], arrived[0][1:], offsets)
+            )
+            sums = shift_sum(pieces[owners:], "limb")
+            offsets = lax.psum(offsets, ("poly", "limb"))
+            offsets = lax.dynamic_slice_in_dim(offsets, (me_poly * limb_size + me_limb) * columns, columns, axis=1)
+
+    for number in range(used, len(chunks)):
+        evaluations = second_section(tables, arrived[number], evaluations, *chunks[number], polys, owners)
     return (evaluations, quotient)
 
 
@@ -442,9 +461,8 @@
         P(("parts", "poly", "limb")),
         P(("parts", "poly", "limb")),
     )
-    sizes = tuple(mesh.shape[name] for name in ("coef", "poly", "limb"))
     return jax.shard_map(
-        functools.partial(shards, sizes=sizes),
+        functools.partial(shards, sizes=tuple(mesh.shape[name] for name in ("coef", "poly", "limb"))),
         mesh=mesh,
         in_specs=placed,
         out_specs=(

time: 327 us -> 305 us (0.933)
  waiting for transfers between devices: 87.9 us -> 36.8 us
  local copies, waits for them, and re-layouts: 8.02 us -> 31 us
  blocking collectives: 19.6 us -> 24.6 us
    ppermute x24 -> x18, waiting for transfers between devices: 87.9 us -> 36.8 us  [the longest x15 36.8 us: exchange(): lax.ppermute(piece, 'coef', [(i, (i + far) % owners) for i in range(owner...]
    psum x1, blocking collectives: 6.44 us -> 24.6 us  [shards(): offsets = lax.psum(offsets, ('poly', 'limb'))]
    unnamed x89 -> x117, local copies, waits for them, and re-layouts: 5.78 us -> 21.1 us
    all_gather x1 -> x0, blocking collectives: 13.1 us -> none  [quotient_columns(): gathered = lax.all_gather(ends[:, :, :, blocks - 1], 'coef', axis=0)]
    ppermute x24 -> x18, starting transfers between devices: 120 us -> 118 us  [the longest x15 70.4 us: exchange(): lax.ppermute(piece, 'coef', [(i, (i + far) % owners) for i in range(owner...]
    pallas_call x17 -> x10, Pallas kernels: 63.8 us -> 62.6 us  [the longest x5 39 us: second_section(): pl.pallas_call(functools.partial(second_kernel, group, owners), out_shape...]
  transfers between devices with their start and end apart: 27 -> 20, of which waited for: 7 -> 2; matrix products, arithmetic and copies ran while one was open for 3% -> 11% of each run, Pallas kernels for 16% -> 20%
where the time goes in v2:
time: 305 us; the launch traced here: 302 us
  starting transfers between devices  120 us (39%)
  Pallas kernels  66 us (22%)
  waiting for transfers between devices  36.8 us (12%)
  local copies, waits for them, and re-layouts  31 us (10%)
  blocking collectives  24.6 us (8%)
  other arithmetic  20.1 us (7%)
    ppermute x15, starting transfers between devices, exchange(): lax.ppermute(piece, 'coef', [(i, (i + far) % owners) for i in range(owner...  70.4 us
    ppermute x3, starting transfers between devices, from_all_owners(): lax.ppermute(last, 'coef', [(i, (i + far) % owners) for i in range(owners)])  48 us
    pallas_call x5, Pallas kernels, second_section(): pl.pallas_call(functools.partial(second_kernel, group, owners), out_shape...  39 us
    ppermute x15, waiting for transfers between devices, exchange(): lax.ppermute(piece, 'coef', [(i, (i + far) % owners) for i in range(owner...  36.8 us
    psum x1, blocking collectives, shards(): offsets = lax.psum(offsets, ('poly', 'limb'))  24.6 us
    pallas_call x5, Pallas kernels, first_section(): pl.pallas_call(kernel, out_shape=out_shape, grid=(steps,), in_specs=in_sp...  23.6 us
    unnamed x117, local copies, waits for them, and re-layouts  21.1 us
    add x2, other arithmetic, shift_sum(): total + lax.ppermute(pieces[far], axis, [(i, (i + far) % size) for i in r...  7.06 us
  transfers between devices with their start and end apart: 20, of which 2 were waited for; matrix products, arithmetic and copies ran while one was open for 11% of the time, Pallas kernels for 20%

profile of v2, /device:TPU:0, one launch (start us, length us, event | category | flops | bytes accessed | tf_op | source)
XLA Modules:
  0.0 302.1 jit_solution(9921162726287902254)
XLA Ops:
  1.6 1.5 first_section.7
  3.8 3.0 %collective-permute-start = (f32[1,2,4,64,128]{4,3,2,1,0:T(8,128)S(1)}, f32[1,2,4,64,128]{4,3,2,1,0:T(8,128)S(1)}, u32[]{:S(2)}, u32[]{:S(2)}) collective-permute-start(f32[1,2,4,64,128]{4,3,2,1,0:T(8,128)S(1)} %get-tuple-element.70), channel_id=1, source_target_pairs={{0,4},{4,8},{8,12},{12,0},{1,5},{5,9},{9,13},{13,1},{2,6},{6,10},{... | collective-permute-start | bytes 786440 | tf_op jit(solution)/shard_map/ppermute | solution.py:380
  6.8 2.6 collective-permute-start.1
  9.4 1.3 collective-permute-start.2
  11.5 13.0 %first_section.6 = (f32[4,2,4,64,128]{4,3,2,1,0:T(8,128)S(1)}, f32[4,2,4,64,128]{4,3,2,1,0:T(8,128)S(1)}, f32[4,2,4,64,128]{4,3,2,1,0:T(8,128)S(1)}, f32[4,2,4,6...) custom-call(f32[512,128]{1,0:T(8,128)S(1)} %copy-done.4, f32[12,128,1024]{2,1,0:T(8,128)} %coeff_ref.9, ...), custom_call_target="tpu_custom_call" | custom-call | flops 1 | bytes 1 | tf_op jit(solution)/shard_map/first_section/pallas_call | solution.py:163
  24.6 1.0 copy-done.5
  25.6 1.0 copy-done.25
  27.8 4.8 %collective-permute-start.8 = (f32[4,2,4,64,128]{4,3,2,1,0:T(8,128)}, f32[4,2,4,64,128]{4,3,2,1,0:T(8,128)S(1)}, u32[]{:S(2)}, u32[]{:S(2)}) collective-permute-start(f32[4,2,4,64,128]{4,3,2,1,0:T(8,128)} %copy-done.27), channel_id=1, source_target_pairs={{0,4},{4,8},{8,12},{12,0},{1,5},{5,9},{9,13},{13,1},{2,6},{6,10},{... | collective-permute-start | bytes 3145736 | tf_op jit(solution)/shard_map/ppermute | solution.py:380
  35.3 4.4 %add.273 = f32[8,128,1024]{2,1,0:T(8,128)S(1)} add(f32[8,128,1024]{2,1,0:T(8,128)} %get-tuple-element.76, f32[8,128,1024]{2,1,0:T(8,128)} %collective-permute-done.3) | non-fusion elementwise | flops 1048576 | bytes 12582912 | tf_op jit(solution)/shard_map/add | solution.py:394
  39.7 1.6 slice.35
  41.3 1.1 copy-done.36
  42.4 1.5 collective-permute-start.4
  43.9 1.3 constant_dynamic-slice_fusion.1.turn_ref
  45.2 1.3 constant_dynamic-slice_fusion.2.middle_ref
  47.3 4.4 %first_section.9 = (f32[4,2,4,64,128]{4,3,2,1,0:T(8,128)S(1)}, f32[4,2,4,64,128]{4,3,2,1,0:T(8,128)S(1)}, f32[4,2,4,64,128]{4,3,2,1,0:T(8,128)S(1)}, f32[4,2,4,64,128]{4,3,2,1,0:T(8,128)}) custom-call(f32[512,128]{1,0:T(8,128)S(1)} %copy-done.4, f32[12,128,1024]{2,1,0:T(8,128)} %coeff_ref.9), custom_call_target="tpu_custom_call" | custom-call | flops 1 | bytes 1 | tf_op jit(solution)/shard_map/first_section/pallas_call | solution.py:163
  53.6 3.2 %first_section.8 = (f32[2,2,4,64,128]{4,3,2,1,0:T(8,128)S(1)}, f32[2,2,4,64,128]{4,3,2,1,0:T(8,128)}, f32[2,2,4,64,128]{4,3,2,1,0:T(8,128)}, f32[2,2,4,64,128]{4,3,2,1,0:T(8,128)}) custom-call(f32[512,128]{1,0:T(8,128)S(1)} %copy-done.4, f32[12,128,1024]{2,1,0:T(8,128)} %coeff_ref.9), custom_call_target="tpu_custom_call" | custom-call | flops 1 | bytes 1 | tf_op jit(solution)/shard_map/first_section/pallas_call | solution.py:163
  57.6 1.5 first_section.5
  62.0 5.9 %collective-permute-start.10 = (f32[4,2,4,64,128]{4,3,2,1,0:T(8,128)}, f32[4,2,4,64,128]{4,3,2,1,0:T(8,128)}, u32[]{:S(2)}, u32[]{:S(2)}) collective-permute-start(f32[4,2,4,64,128]{4,3,2,1,0:T(8,128)} %copy-done.26), channel_id=1, source_target_pairs={{0,12},{4,0},{8,4},{12,8},{1,13},{5,1},{9,5},{13,9},{2,14},{6,2},{... | collective-permute-start | bytes 3145736 | tf_op jit(solution)/shard_map/ppermute | solution.py:380
  68.4 24.6 %psum.7 = f32[2,16]{1,0:T(2,128)S(1)} all-reduce(f32[2,16]{1,0:T(2,128)S(1)} %multiply_reduce_fusion.4), channel_id=1, replica_groups=mesh['parts'=2,'coef'=4,'poly'=2,'limb'=2] {'poly','limb'}, use_global_device_ids=true, to_apply=%region_2.3 | all-reduce | flops 32 | bytes 256 | tf_op jit(solution)/shard_map/psum | solution.py:448
  95.9 1.0 copy-done.7
  96.9 3.8 %collective-permute-start.18 = (f32[4,2,4,64,128]{4,3,2,1,0:T(8,128)}, f32[4,2,4,64,128]{4,3,2,1,0:T(8,128)S(1)}, u32[]{:S(2)}, u32[]{:S(2)}) collective-permute-start(f32[4,2,4,64,128]{4,3,2,1,0:T(8,128)} %copy-done.28), channel_id=1, source_target_pairs={{0,8},{4,12},{8,0},{12,4},{1,9},{5,13},{9,1},{13,5},{2,10},{6,14},... | collective-permute-start | bytes 3145736 | tf_op jit(solution)/shard_map/ppermute | solution.py:380
  100.6 1.4 multiply_select_fusion.3
  102.0 2.7 slice_add_fusion.value_ref
  104.7 2.5 convolution_bitcast_fusion
  107.2 1.3 copy-done
  108.5 1.8 copy.25
  110.3 1.4 slice_reduce_fusion
  111.7 2.7 collective-permute-start.5
  114.4 45.2 %collective-permute-start.6 = (f32[2,4,128]{2,1,0:T(4,128)S(1)}, f32[2,4,128]{2,1,0:T(4,128)S(1)}, u32[]{:S(2)}, u32[]{:S(2)}) collective-permute-start(f32[2,4,128]{2,1,0:T(4,128)S(1)} %slice_reduce_fusion), channel_id=1, source_target_pairs={{0,8},{4,12},{8,0},{12,4},{1,9},{5,13},{9,1},{13,5},{2,10},{6,14},... | collective-permute-start | bytes 12296 | tf_op jit(solution)/shard_map/ppermute | solution.py:312
  159.7 23.0 %collective-permute-done.9.refs_2_ = f32[4,2,4,64,128]{4,3,2,1,0:T(8,128)} collective-permute-done((f32[4,2,4,64,128]{4,3,2,1,0:T(8,128)}, f32[4,2,4,64,128]{4,3,2,1,0:T(8,128)}, u32[]{:S(2)}, u32[]{:S(2)}) %collective-permute-start.9) | collective-permute-done | bytes 1048608 | tf_op jit(solution)/shard_map/ppermute | solution.py:380
  187.3 2.9 second_section.5.refs_4_
  190.2 1.0 collective-permute-start.11
  191.2 13.8 %collective-permute-done.18.refs_2_ = f32[4,2,4,64,128]{4,3,2,1,0:T(8,128)S(1)} collective-permute-done((f32[4,2,4,64,128]{4,3,2,1,0:T(8,128)}, f32[4,2,4,64,128]{4,3,2,1,0:T(8,128)S(1)}, u32[]{:S(2)}, u32[]{:S(2)}) %collective-permute-start.18) | collective-permute-done | bytes 1048608 | tf_op jit(solution)/shard_map/ppermute | solution.py:380
  205.1 1.0 copy-done.11
  206.1 35.8 %collective-permute-start.13 = (f32[2,2,4,64,128]{4,3,2,1,0:T(8,128)}, f32[2,2,4,64,128]{4,3,2,1,0:T(8,128)}, u32[]{:S(2)}, u32[]{:S(2)}) collective-permute-start(f32[2,2,4,64,128]{4,3,2,1,0:T(8,128)} %get-tuple-element.105), channel_id=1, source_target_pairs={{0,4},{4,8},{8,12},{12,0},{1,5},{5,9},{9,13},{13,1},{2,6},{6,10},{... | collective-permute-start | bytes 1572872 | tf_op jit(solution)/shard_map/ppermute | solution.py:380
  242.2 2.3 multiply_reduce_fusion.2
  245.4 1.8 copy.27
  247.1 1.4 pad_add_fusion.carry_ref
  248.5 1.2 copy-done.6
  249.8 1.2 copy-done.8
  251.0 13.1 %second_section.6.refs_4_ = f32[2,32,12,32,128]{4,3,2,1,0:T(8,128)} custom-call(bf16[32,64,192]{2,1,0:T(8,128)(2,1)S(1)} %constant_dynamic-slice_fusion.2.middle_ref, f32[32,2,32,128]{3,2,1,0:T(8,128)S(1)} %constant_dynamic-slice_fusion.1.turn_ref, bf16[768,256]{1,0:T(8,128)(2,1)S(1)} %copy-done.2, ...), custom_call_target="tpu_custom_call", output_to_operand_aliasing={{}: (7, {})} | custom-call | flops 1 | bytes 1 | tf_op jit(solution)/shard_map/second_section/pallas_call | solution.py:227
  264.1 3.4 %filter_columns.1 = f32[2,4,128,1024]{3,2,1,0:T(8,128)} custom-call(f32[4,128,1024]{2,1,0:T(8,128)S(1)} %copy-done.1, f32[4,128,256]{2,1,0:T(8,128)S(1)} %maximum_negate_fusion.table_ref, f32[2,4,128,8]{3,2,1,0:T(8,128)S(1)} %pad_add_fusion.carry_ref, f32[4,2,128]{2,1,0:T(2,128)S(1)} %maximum_negate_fusion.1.reach_ref), custom_call_target="tpu_custom_call" | custom-call | flops 1 | bytes 1 | tf_op jit(solution)/shard_map/filter_columns/pallas_call | solution.py:257
  267.5 2.0 collective-permute-start.12
  269.5 8.5 %collective-permute-start.17 = (f32[1,2,4,64,128]{4,3,2,1,0:T(8,128)S(1)}, f32[1,2,4,64,128]{4,3,2,1,0:T(8,128)S(1)}, u32[]{:S(2)}, u32[]{:S(2)}) collective-permute-start(f32[1,2,4,64,128]{4,3,2,1,0:T(8,128)S(1)} %copy-done.33), channel_id=1, source_target_pairs={{0,12},{4,0},{8,4},{12,8},{1,13},{5,1},{9,5},{13,9},{2,14},{6,2},{... | collective-permute-start | bytes 786440 | tf_op jit(solution)/shard_map/ppermute | solution.py:380
  278.0 1.0 collective-permute-start.14
  279.0 13.0 %second_section.7.refs_4_ = f32[2,32,12,32,128]{4,3,2,1,0:T(8,128)} custom-call(bf16[32,64,192]{2,1,0:T(8,128)(2,1)S(1)} %constant_dynamic-slice_fusion.2.middle_ref, f32[32,2,32,128]{3,2,1,0:T(8,128)S(1)} %constant_dynamic-slice_fusion.1.turn_ref, bf16[768,256]{1,0:T(8,128)(2,1)S(1)} %copy-done.2, ...), custom_call_target="tpu_custom_call", output_to_operand_aliasing={{}: (7, {})} | custom-call | flops 1 | bytes 1 | tf_op jit(solution)/shard_map/second_section/pallas_call | solution.py:227
  292.0 7.1 %second_section.8.refs_4_ = f32[2,32,12,32,128]{4,3,2,1,0:T(8,128)} custom-call(bf16[32,64,192]{2,1,0:T(8,128)(2,1)S(1)} %constant_dynamic-slice_fusion.2.middle_ref, f32[32,2,32,128]{3,2,1,0:T(8,128)S(1)} %constant_dynamic-slice_fusion.1.turn_ref, bf16[768,256]{1,0:T(8,128)(2,1)S(1)} %copy-done.2, ...), custom_call_target="tpu_custom_call", output_to_operand_aliasing={{}: (7, {})} | custom-call | flops 1 | bytes 1 | tf_op jit(solution)/shard_map/second_section/pallas_call | solution.py:227
  299.2 2.9 second_section.9
  (167 shorter events, 21.7 us)
Async XLA Ops:
  3.8 23.9 %collective-permute-start = (f32[1,2,4,64,128]{4,3,2,1,0:T(8,128)S(1)}, f32[1,2,4,64,128]{4,3,2,1,0:T(8,128)S(1)}, u32[]{:S(2)}, u32[]{:S(2)}) collective-permute-start(f32[1,2,4,64,128]{4,3,2,1,0:T(8,128)S(1)} %get-tuple-element.70), channel_id=1, source_target_pairs={{0,4},{4,8},{8,12},{12,0},{1,5},{5,9},{9,13},{13,1},{2,6},{6,10},{... | collective-permute-start | bytes 786440 | tf_op jit(solution)/shard_map/ppermute | solution.py:380
  6.8 20.9 %collective-permute-start.1 = (f32[1,2,4,64,128]{4,3,2,1,0:T(8,128)S(1)}, f32[1,2,4,64,128]{4,3,2,1,0:T(8,128)S(1)}, u32[]{:S(2)}, u32[]{:S(2)}) collective-permute-start(f32[1,2,4,64,128]{4,3,2,1,0:T(8,128)S(1)} %get-tuple-element.73), channel_id=1, source_target_pairs={{0,8},{4,12},{8,0},{12,4},{1,9},{5,13},{9,1},{13,5},{2,10},{6,14},... | collective-permute-start | bytes 786440 | tf_op jit(solution)/shard_map/ppermute | solution.py:380
  9.4 18.3 %collective-permute-start.2 = (f32[1,2,4,64,128]{4,3,2,1,0:T(8,128)S(1)}, f32[1,2,4,64,128]{4,3,2,1,0:T(8,128)S(1)}, u32[]{:S(2)}, u32[]{:S(2)}) collective-permute-start(f32[1,2,4,64,128]{4,3,2,1,0:T(8,128)S(1)} %get-tuple-element.75), channel_id=1, source_target_pairs={{0,12},{4,0},{8,4},{12,8},{1,13},{5,1},{9,5},{13,9},{2,14},{6,2},{... | collective-permute-start | bytes 786440 | tf_op jit(solution)/shard_map/ppermute | solution.py:380
  11.5 16.1 %copy-start.44 = (f32[2,16,12]{1,0,2:T(2,128)S(1)}, f32[2,16,12]{1,0,2:T(2,128)}, u32[]{:S(2)}) copy-start(f32[2,16,12]{1,0,2:T(2,128)} %param.11) | copy-start | bytes 4612
  27.6 16.3 %copy-start.26 = (f32[4,2,4,64,128]{4,3,2,1,0:T(8,128)}, f32[4,2,4,64,128]{4,3,2,1,0:T(8,128)S(1)}, u32[]{:S(2)}) copy-start(f32[4,2,4,64,128]{4,3,2,1,0:T(8,128)S(1)} %get-tuple-element.92) | copy-start | bytes 3145732
  27.7 12.0 %copy-start.19 = (f32[1,2,4,64,128]{4,3,2,1,0:T(8,128)}, f32[1,2,4,64,128]{4,3,2,1,0:T(8,128)S(1)}, u32[]{:S(2)}) copy-start(f32[1,2,4,64,128]{4,3,2,1,0:T(8,128)S(1)} %collective-permute-done.refs_1_) | copy-start | bytes 786436
  27.7 7.6 %collective-permute-start.3 = (f32[8,128,1024]{2,1,0:T(8,128)}, f32[8,128,1024]{2,1,0:T(8,128)}, u32[]{:S(2)}, u32[]{:S(2)}) collective-permute-start(f32[8,128,1024]{2,1,0:T(8,128)} %get-tuple-element.77), channel_id=1, source_target_pairs={{0,1},{1,0},{2,3},{3,2},{4,5},{5,4},{6,7},{7,6},{8,9},{9,8},{10,11... | collective-permute-start | bytes 12582920 | tf_op jit(solution)/shard_map/ppermute | solution.py:394
  27.8 68.1 %collective-permute-start.8 = (f32[4,2,4,64,128]{4,3,2,1,0:T(8,128)}, f32[4,2,4,64,128]{4,3,2,1,0:T(8,128)S(1)}, u32[]{:S(2)}, u32[]{:S(2)}) collective-permute-start(f32[4,2,4,64,128]{4,3,2,1,0:T(8,128)} %copy-done.27), channel_id=1, source_target_pairs={{0,4},{4,8},{8,12},{12,0},{1,5},{5,9},{9,13},{13,1},{2,6},{6,10},{... | collective-permute-start | bytes 3145736 | tf_op jit(solution)/shard_map/ppermute | solution.py:380
  42.4 59.6 %collective-permute-start.4 = (f32[4,128,1024]{2,1,0:T(8,128)}, f32[4,128,1024]{2,1,0:T(8,128)}, u32[]{:S(2)}, u32[]{:S(2)}) collective-permute-start(f32[4,128,1024]{2,1,0:T(8,128)} %slice.35), channel_id=1, source_target_pairs={{0,2},{2,0},{1,3},{3,1},{4,6},{6,4},{5,7},{7,5},{8,10},{10,8},{9,1... | collective-permute-start | bytes 6291464 | tf_op jit(solution)/shard_map/ppermute | solution.py:394
  57.6 35.5 %copy-start.43 = (s32[4]{0:T(128)S(1)}, s32[4]{0:T(128)}, u32[]{:S(2)}) copy-start(s32[4]{0:T(128)} %param.12) | copy-start | bytes 52
  57.6 35.5 %copy-start.56 = (s32[4]{0:T(128)S(1)}, s32[4]{0:T(128)}, u32[]{:S(2)}) copy-start(s32[4]{0:T(128)} %param.13) | copy-start | bytes 52
  62.0 52.5 %collective-permute-start.10 = (f32[4,2,4,64,128]{4,3,2,1,0:T(8,128)}, f32[4,2,4,64,128]{4,3,2,1,0:T(8,128)}, u32[]{:S(2)}, u32[]{:S(2)}) collective-permute-start(f32[4,2,4,64,128]{4,3,2,1,0:T(8,128)} %copy-done.26), channel_id=1, source_target_pairs={{0,12},{4,0},{8,4},{12,8},{1,13},{5,1},{9,5},{13,9},{2,14},{6,2},{... | collective-permute-start | bytes 3145736 | tf_op jit(solution)/shard_map/ppermute | solution.py:380
  67.9 114.8 %collective-permute-start.9 = (f32[4,2,4,64,128]{4,3,2,1,0:T(8,128)}, f32[4,2,4,64,128]{4,3,2,1,0:T(8,128)}, u32[]{:S(2)}, u32[]{:S(2)}) collective-permute-start(f32[4,2,4,64,128]{4,3,2,1,0:T(8,128)} %copy-done.25), channel_id=1, source_target_pairs={{0,8},{4,12},{8,0},{12,4},{1,9},{5,13},{9,1},{13,5},{2,10},{6,14},... | collective-permute-start | bytes 3145736 | tf_op jit(solution)/shard_map/ppermute | solution.py:380
  68.2 122.0 %collective-permute-start.15 = (f32[4,2,4,64,128]{4,3,2,1,0:T(8,128)}, f32[4,2,4,64,128]{4,3,2,1,0:T(8,128)}, u32[]{:S(2)}, u32[]{:S(2)}) collective-permute-start(f32[4,2,4,64,128]{4,3,2,1,0:T(8,128)} %copy-done.29), channel_id=1, source_target_pairs={{0,4},{4,8},{8,12},{12,0},{1,5},{5,9},{9,13},{13,1},{2,6},{6,10},{... | collective-permute-start | bytes 3145736 | tf_op jit(solution)/shard_map/ppermute | solution.py:380
  96.9 108.2 %collective-permute-start.18 = (f32[4,2,4,64,128]{4,3,2,1,0:T(8,128)}, f32[4,2,4,64,128]{4,3,2,1,0:T(8,128)S(1)}, u32[]{:S(2)}, u32[]{:S(2)}) collective-permute-start(f32[4,2,4,64,128]{4,3,2,1,0:T(8,128)} %copy-done.28), channel_id=1, source_target_pairs={{0,8},{4,12},{8,0},{12,4},{1,9},{5,13},{9,1},{13,5},{2,10},{6,14},... | collective-permute-start | bytes 3145736 | tf_op jit(solution)/shard_map/ppermute | solution.py:380
  102.0 81.3 %copy-start.2 = (bf16[768,256]{1,0:T(8,128)(2,1)S(1)}, bf16[768,256]{1,0:T(8,128)(2,1)}, u32[]{:S(2)}) copy-start(bf16[768,256]{1,0:T(8,128)(2,1)} %constant.136.clone.last_ref) | copy-start | bytes 1179652
  111.7 94.4 %collective-permute-start.5 = (f32[2,4,128]{2,1,0:T(4,128)S(1)}, f32[2,4,128]{2,1,0:T(4,128)S(1)}, u32[]{:S(2)}, u32[]{:S(2)}) collective-permute-start(f32[2,4,128]{2,1,0:T(4,128)S(1)} %slice_reduce_fusion), channel_id=1, source_target_pairs={{0,4},{4,8},{8,12},{12,0},{1,5},{5,9},{9,13},{13,1},{2,6},{6,10},{... | collective-permute-start | bytes 12296 | tf_op jit(solution)/shard_map/ppermute | solution.py:312
  114.4 127.5 %collective-permute-start.6 = (f32[2,4,128]{2,1,0:T(4,128)S(1)}, f32[2,4,128]{2,1,0:T(4,128)S(1)}, u32[]{:S(2)}, u32[]{:S(2)}) collective-permute-start(f32[2,4,128]{2,1,0:T(4,128)S(1)} %slice_reduce_fusion), channel_id=1, source_target_pairs={{0,8},{4,12},{8,0},{12,4},{1,9},{5,13},{9,1},{13,5},{2,10},{6,14},... | collective-permute-start | bytes 12296 | tf_op jit(solution)/shard_map/ppermute | solution.py:312
  182.6 59.3 %collective-permute-start.7 = (f32[2,4,128]{2,1,0:T(4,128)S(1)}, f32[2,4,128]{2,1,0:T(4,128)S(1)}, u32[]{:S(2)}, u32[]{:S(2)}) collective-permute-start(f32[2,4,128]{2,1,0:T(4,128)S(1)} %slice_reduce_fusion), channel_id=1, source_target_pairs={{0,12},{4,0},{8,4},{12,8},{1,13},{5,1},{9,5},{13,9},{2,14},{6,2},{... | collective-permute-start | bytes 12296 | tf_op jit(solution)/shard_map/ppermute | solution.py:312
  187.1 54.8 %copy-start.47 = (f32[4,4]{0,1:T(4,128)S(1)}, f32[4,4]{0,1:T(4,128)}, u32[]{:S(2)}) copy-start(f32[4,4]{0,1:T(4,128)} %get-tuple-element.154) | copy-start | bytes 196
  187.1 54.8 %copy-start.48 = (f32[4,4]{0,1:T(4,128)S(1)}, f32[4,4]{0,1:T(4,128)}, u32[]{:S(2)}) copy-start(f32[4,4]{0,1:T(4,128)} %get-tuple-element.155) | copy-start | bytes 196
  187.1 54.8 %copy-start.49 = (f32[4,4]{0,1:T(4,128)S(1)}, f32[4,4]{0,1:T(4,128)}, u32[]{:S(2)}) copy-start(f32[4,4]{0,1:T(4,128)} %get-tuple-element.160) | copy-start | bytes 196
  187.1 54.8 %copy-start.50 = (f32[4,4]{0,1:T(4,128)S(1)}, f32[4,4]{0,1:T(4,128)}, u32[]{:S(2)}) copy-start(f32[4,4]{0,1:T(4,128)} %get-tuple-element.161) | copy-start | bytes 196
  187.2 54.9 %copy-start.53 = (f32[4]{0:T(128)S(1)}, f32[4]{0:T(128)}, u32[]{:S(2)}) copy-start(f32[4]{0:T(128)} %get-tuple-element.152) | copy-start | bytes 52
  187.2 54.9 %copy-start.54 = (f32[4]{0:T(128)S(1)}, f32[4]{0:T(128)}, u32[]{:S(2)}) copy-start(f32[4]{0:T(128)} %get-tuple-element.153) | copy-start | bytes 52
  187.2 54.9 %copy-start.57 = (pred[128]{0:T(512)(128)(4,1)S(1)}, pred[128]{0:T(512)(128)(4,1)}, u32[]{:S(2)}) copy-start(pred[128]{0:T(512)(128)(4,1)} %iota_compare_fusion) | copy-start | bytes 388
  187.2 55.0 %copy-start.37 = (s32[128,128]{1,0:T(8,128)S(1)}, s32[128,128]{1,0:T(8,128)}, u32[]{:S(2)}) copy-start(s32[128,128]{1,0:T(8,128)} %get-tuple-element.172) | copy-start | bytes 196612
  187.2 55.0 %copy-start.38 = (s32[128,128]{1,0:T(8,128)S(1)}, s32[128,128]{1,0:T(8,128)}, u32[]{:S(2)}) copy-start(s32[128,128]{1,0:T(8,128)} %get-tuple-element.173) | copy-start | bytes 196612
  187.2 55.0 %copy-start.39 = (f32[128,128]{1,0:T(8,128)S(1)}, f32[128,128]{1,0:T(8,128)}, u32[]{:S(2)}) copy-start(f32[128,128]{1,0:T(8,128)} %get-tuple-element.174) | copy-start | bytes 196612
  187.2 55.0 %copy-start.40 = (f32[128,128]{1,0:T(8,128)S(1)}, f32[128,128]{1,0:T(8,128)}, u32[]{:S(2)}) copy-start(f32[128,128]{1,0:T(8,128)} %get-tuple-element.175) | copy-start | bytes 196612
  187.2 55.0 %copy-start.41 = (pred[128,128]{1,0:T(8,128)(4,1)S(1)}, pred[128,128]{1,0:T(8,128)(4,1)}, u32[]{:S(2)}) copy-start(pred[128,128]{1,0:T(8,128)(4,1)} %fusion.5) | copy-start | bytes 49156
  187.2 55.0 %copy-start.55 = (f32[4]{0:T(128)S(1)}, f32[4]{0:T(128)}, u32[]{:S(2)}) copy-start(f32[4]{0:T(128)} %get-tuple-element.164) | copy-start | bytes 52
  187.2 57.3 %copy-start.51 = (f32[4]{0:T(128)S(1)}, f32[4]{0:T(128)}, u32[]{:S(2)}) copy-start(f32[4]{0:T(128)} %get-tuple-element.158) | copy-start | bytes 52
  187.3 57.3 %copy-start.52 = (f32[4]{0:T(128)S(1)}, f32[4]{0:T(128)}, u32[]{:S(2)}) copy-start(f32[4]{0:T(128)} %get-tuple-element.159) | copy-start | bytes 52
  187.3 57.4 %copy-start.45 = (f32[4,8]{1,0:T(4,128)S(1)}, f32[4,8]{1,0:T(4,128)}, u32[]{:S(2)}) copy-start(f32[4,8]{1,0:T(4,128)} %get-tuple-element.150) | copy-start | bytes 388
  187.3 57.3 %copy-start.46 = (f32[4,8]{1,0:T(4,128)S(1)}, f32[4,8]{1,0:T(4,128)}, u32[]{:S(2)}) copy-start(f32[4,8]{1,0:T(4,128)} %get-tuple-element.151) | copy-start | bytes 388
  190.2 77.3 %collective-permute-start.11 = (f32[4,2,4,64,128]{4,3,2,1,0:T(8,128)}, f32[4,2,4,64,128]{4,3,2,1,0:T(8,128)}, u32[]{:S(2)}, u32[]{:S(2)}) collective-permute-start(f32[4,2,4,64,128]{4,3,2,1,0:T(8,128)} %get-tuple-element.102), channel_id=1, source_target_pairs={{0,12},{4,0},{8,4},{12,8},{1,13},{5,1},{9,5},{13,9},{2,14},{6,2},{... | collective-permute-start | bytes 3145736 | tf_op jit(solution)/shard_map/ppermute | solution.py:380
  206.1 63.4 %collective-permute-start.16 = (f32[2,2,4,64,128]{4,3,2,1,0:T(8,128)}, f32[2,2,4,64,128]{4,3,2,1,0:T(8,128)S(1)}, u32[]{:S(2)}, u32[]{:S(2)}) collective-permute-start(f32[2,2,4,64,128]{4,3,2,1,0:T(8,128)} %get-tuple-element.110), channel_id=1, source_target_pairs={{0,8},{4,12},{8,0},{12,4},{1,9},{5,13},{9,1},{13,5},{2,10},{6,14},... | collective-permute-start | bytes 1572872 | tf_op jit(solution)/shard_map/ppermute | solution.py:380
  206.1 63.4 %collective-permute-start.13 = (f32[2,2,4,64,128]{4,3,2,1,0:T(8,128)}, f32[2,2,4,64,128]{4,3,2,1,0:T(8,128)}, u32[]{:S(2)}, u32[]{:S(2)}) collective-permute-start(f32[2,2,4,64,128]{4,3,2,1,0:T(8,128)} %get-tuple-element.105), channel_id=1, source_target_pairs={{0,4},{4,8},{8,12},{12,0},{1,5},{5,9},{9,13},{13,1},{2,6},{6,10},{... | collective-permute-start | bytes 1572872 | tf_op jit(solution)/shard_map/ppermute | solution.py:380
  241.9 50.1 %collective-permute-start.19 = (f32[2,2,4,64,128]{4,3,2,1,0:T(8,128)}, f32[2,2,4,64,128]{4,3,2,1,0:T(8,128)}, u32[]{:S(2)}, u32[]{:S(2)}) collective-permute-start(f32[2,2,4,64,128]{4,3,2,1,0:T(8,128)} %get-tuple-element.117), channel_id=1, source_target_pairs={{0,12},{4,0},{8,4},{12,8},{1,13},{5,1},{9,5},{13,9},{2,14},{6,2},{... | collective-permute-start | bytes 1572872 | tf_op jit(solution)/shard_map/ppermute | solution.py:380
  251.0 13.1 %copy-start.1 = (f32[4,128,1024]{2,1,0:T(8,128)S(1)}, f32[4,128,1024]{2,1,0:T(8,128)}, u32[]{:S(2)}) copy-start(f32[4,128,1024]{2,1,0:T(8,128)} %copy-done) | copy-start | bytes 6291460
  264.0 14.0 %copy-start.31 = (f32[1,2,4,64,128]{4,3,2,1,0:T(8,128)S(1)}, f32[1,2,4,64,128]{4,3,2,1,0:T(8,128)}, u32[]{:S(2)}) copy-start(f32[1,2,4,64,128]{4,3,2,1,0:T(8,128)} %copy-done.30) | copy-start | bytes 786436
  264.1 15.0 %copy-start.10 = (f32[4,2,4,64,128]{4,3,2,1,0:T(8,128)S(1)}, f32[4,2,4,64,128]{4,3,2,1,0:T(8,128)}, u32[]{:S(2)}) copy-start(f32[4,2,4,64,128]{4,3,2,1,0:T(8,128)} %copy-done.9) | copy-start | bytes 3145732
  264.1 15.0 %copy-start.12 = (f32[4,2,4,64,128]{4,3,2,1,0:T(8,128)S(1)}, f32[4,2,4,64,128]{4,3,2,1,0:T(8,128)}, u32[]{:S(2)}) copy-start(f32[4,2,4,64,128]{4,3,2,1,0:T(8,128)} %copy-done.11) | copy-start | bytes 3145732
  267.5 31.7 %collective-permute-start.12 = (f32[1,2,4,64,128]{4,3,2,1,0:T(8,128)S(1)}, f32[1,2,4,64,128]{4,3,2,1,0:T(8,128)S(1)}, u32[]{:S(2)}, u32[]{:S(2)}) collective-permute-start(f32[1,2,4,64,128]{4,3,2,1,0:T(8,128)S(1)} %copy-done.35), channel_id=1, source_target_pairs={{0,4},{4,8},{8,12},{12,0},{1,5},{5,9},{9,13},{13,1},{2,6},{6,10},{... | collective-permute-start | bytes 786440 | tf_op jit(solution)/shard_map/ppermute | solution.py:380
  269.5 29.6 %collective-permute-start.17 = (f32[1,2,4,64,128]{4,3,2,1,0:T(8,128)S(1)}, f32[1,2,4,64,128]{4,3,2,1,0:T(8,128)S(1)}, u32[]{:S(2)}, u32[]{:S(2)}) collective-permute-start(f32[1,2,4,64,128]{4,3,2,1,0:T(8,128)S(1)} %copy-done.33), channel_id=1, source_target_pairs={{0,12},{4,0},{8,4},{12,8},{1,13},{5,1},{9,5},{13,9},{2,14},{6,2},{... | collective-permute-start | bytes 786440 | tf_op jit(solution)/shard_map/ppermute | solution.py:380
  278.0 21.1 %collective-permute-start.14 = (f32[1,2,4,64,128]{4,3,2,1,0:T(8,128)S(1)}, f32[1,2,4,64,128]{4,3,2,1,0:T(8,128)S(1)}, u32[]{:S(2)}, u32[]{:S(2)}) collective-permute-start(f32[1,2,4,64,128]{4,3,2,1,0:T(8,128)S(1)} %copy-done.31), channel_id=1, source_target_pairs={{0,8},{4,12},{8,0},{12,4},{1,9},{5,13},{9,1},{13,5},{2,10},{6,14},... | collective-permute-start | bytes 786440 | tf_op jit(solution)/shard_map/ppermute | solution.py:380
  279.0 13.0 %copy-start.14 = (f32[2,2,4,64,128]{4,3,2,1,0:T(8,128)S(1)}, f32[2,2,4,64,128]{4,3,2,1,0:T(8,128)}, u32[]{:S(2)}) copy-start(f32[2,2,4,64,128]{4,3,2,1,0:T(8,128)} %copy-done.13) | copy-start | bytes 1572868
  (30 other events, 85.1 us)

commit v3 on v2

--- a/solution.py
+++ b/solution.py
@@ -18,7 +18,7 @@
 VMEM_BYTES = 48 * 2**20
 
 SMALL_COST = pl.CostEstimate(flops=1, bytes_accessed=1, transcendentals=0)
-DEPTH = 4
+DEPTH = 5
 
 precise = lax.Precision.HIGHEST
 
@@ -125,52 +125,77 @@
     transform(group, table_ref, coeff_ref, out_refs)
 
 
-def first_batch_kernel(group, count, owners, table_ref, coeff_ref, weight_ref, rows_ref, *out_refs):
-    batch(weight_ref, rows_ref, out_refs[owners:])
-
-    @pl.when(pl.program_id(0) < count)
-    def _():
-        transform(group, table_ref, coeff_ref, out_refs[:owners])
-
-
-def first_section(table, coefficients, start, count, owners, weights=None, targets=1):
-    polys, _, rows_here = coefficients.shape
+def rest_kernel(group, counts, owners, table_ref, coeff_ref, weight_ref, rows_ref, *out_refs):
+    step = pl.program_id(0)
+    batch(weight_ref, rows_ref, out_refs[owners * len(counts):])
+    begin = 0
+    for number, count in enumerate(counts):
+
+        @pl.when((step >= begin) & (step < begin + count))
+        def _(number=number):
+            transform(group, table_ref, coeff_ref, out_refs[number * owners:(number + 1) * owners])
+
+        begin += count
+
+
+def piece_shape(coefficients, count, owners):
     extent = LEN_COLS // owners
     group = min(8, extent)
-    shape = (1, 2, extent // group, (rows_here // SPLIT_LO) * group, SPLIT_LO)
-    steps = count
-    kernel = functools.partial(first_kernel, group)
-    in_specs = [
-        pl.BlockSpec(table.shape, lambda i: (0, 0)),
-        pl.BlockSpec((1, LEN_COLS, rows_here), lambda i: (start + jnp.minimum(i, count - 1), 0, 0)),
-    ]
-    out_specs = [pl.BlockSpec(shape, lambda i: (jnp.minimum(i, count - 1), 0, 0, 0, 0))] * owners
-    out_shape = [jax.ShapeDtypeStruct((count,) + shape[1:], jnp.float32)] * owners
-    operands = [table, coefficients]
-    if weights is not None:
-        columns = weights.shape[0] // targets
-        height = 16 if count <= LEN_COLS // 16 else 8
-        steps = LEN_COLS // height
-        kernel = functools.partial(first_batch_kernel, group, count, owners)
-        in_specs += [
+    return (count, 2, extent // group, (coefficients.shape[2] // SPLIT_LO) * group, SPLIT_LO)
+
+
+def first_section(table, coefficients, count, owners):
+    rows_here = coefficients.shape[2]
+    shape = piece_shape(coefficients, count, owners)
+    pieces = pl.pallas_call(
+        functools.partial(first_kernel, min(8, LEN_COLS // owners)),
+        out_shape=[jax.ShapeDtypeStruct(shape, jnp.float32)] * owners,
+        grid=(count,),
+        in_specs=[
+            pl.BlockSpec(table.shape, lambda i: (0, 0)),
+            pl.BlockSpec((1, LEN_COLS, rows_here), lambda i: (i, 0, 0)),
+        ],
+        out_specs=[pl.BlockSpec((1,) + shape[1:], lambda i: (i, 0, 0, 0, 0))] * owners,
+        compiler_params=pltpu.CompilerParams(vmem_limit_bytes=VMEM_BYTES),
+        cost_estimate=SMALL_COST,
+        name="first_section",
+    )(table, coefficients)
+    return list(pieces)
+
+
+def rest_sections(table, coefficients, start, counts, owners, weights, targets):
+    polys, _, rows_here = coefficients.shape
+    columns = weights.shape[0] // targets
+    total = sum(counts)
+    height = 8
+    steps = LEN_COLS // height
+    out_specs, out_shape = [], []
+    begin = 0
+    for count in counts:
+        shape = piece_shape(coefficients, count, owners)
+        place = lambda i, begin=begin, count=count: (jnp.clip(i - begin, 0, count - 1), 0, 0, 0, 0)
+        out_specs += [pl.BlockSpec((1,) + shape[1:], place)] * owners
+        out_shape += [jax.ShapeDtypeStruct(shape, jnp.float32)] * owners
+        begin += count
+    out_specs += [pl.BlockSpec((columns, height, rows_here), lambda i: (0, jnp.minimum(i, steps - 1), 0))] * targets
+    out_shape += [jax.ShapeDtypeStruct((columns, LEN_COLS, rows_here), jnp.float32)] * targets
+    outs = pl.pallas_call(
+        functools.partial(rest_kernel, min(8, LEN_COLS // owners), tuple(counts), owners),
+        out_shape=out_shape,
+        grid=(max(steps, total),),
+        in_specs=[
+            pl.BlockSpec(table.shape, lambda i: (0, 0)),
+            pl.BlockSpec((1, LEN_COLS, rows_here), lambda i: (start + jnp.minimum(i, total - 1), 0, 0)),
             pl.BlockSpec(memory_space=pltpu.SMEM),
-            pl.BlockSpec((polys, height, rows_here), lambda i: (0, i, 0)),
-        ]
-        out_specs += [pl.BlockSpec((columns, height, rows_here), lambda i: (0, i, 0))] * targets
-        out_shape += [jax.ShapeDtypeStruct((columns, LEN_COLS, rows_here), jnp.float32)] * targets
-        operands += [weights, coefficients]
-    return list(
-        pl.pallas_call(
-            kernel,
-            out_shape=out_shape,
-            grid=(steps,),
-            in_specs=in_specs,
-            out_specs=out_specs,
-            compiler_params=pltpu.CompilerParams(vmem_limit_bytes=VMEM_BYTES),
-            cost_estimate=SMALL_COST,
-            name="first_section",
-        )(*operands)
-    )
+            pl.BlockSpec((polys, height, rows_here), lambda i: (0, jnp.minimum(i, steps - 1), 0)),
+        ],
+        out_specs=out_specs,
+        compiler_params=pltpu.CompilerParams(vmem_limit_bytes=VMEM_BYTES),
+        cost_estimate=SMALL_COST,
+        name="rest_sections",
+    )(table, coefficients, weights, coefficients)
+    pieces = [list(outs[i * owners:(i + 1) * owners]) for i in range(len(counts))]
+    return pieces, list(outs[len(counts) * owners:])
 
 
 def second_kernel(group, owners, middle_ref, turn_ref, last_ref, *refs):
@@ -365,8 +390,7 @@
 
 
 def chunk_sizes(polys):
-    most = (polys - 4) // 2
-    return [1, most, polys - 4 - most, 2, 1] if polys > 6 else [1, 1, 2, 1, 1]
+    return [4, 5, 2, 1] if polys==12 else [1,2,2,1]
 
 
 def exchange(pieces, owners, sent):
@@ -420,32 +444,42 @@
     target = (ahead * limb_size + aside).reshape(-1)
     weights = batch_weights.reshape(-1, columns, polys)[target].reshape(batch_weights.shape)
 
+    counts = [count for _, count in chunks]
+    made = [first_section(table, coefficients, counts[0], owners)]
+    others, batched = rest_sections(table, coefficients, counts[0], counts[1:], owners, weights, limb_size)
+    made += others
+    offsets = jnp.sum(batch_weights[None] * claimed, axis=2)
+
     arrived = []
     sent = []
     used = 0
     evaluations = None
-    for number, (start, count) in enumerate(chunks):
-        batched = (weights, limb_size) if number == 1 else ()
-        pieces = first_section(table, coefficients, start, count, owners, *batched)
-        if number == 3:
+    for number, pieces in enumerate(made):
+        if number >= 2:
+            evaluations = second_section(tables, arrived[used], evaluations, *chunks[used], polys, owners)
+            used += 1
+            tied = None
+            if number == 2:
+                tied = segment_states(values, point_index, point_cycle)
+            elif number == 3:
+                gathered = from_all_owners(ends)
+                tied = quotient_columns(values, ends, gathered, offsets, point_index, point_cycle)
+            pieces, tied, evaluations = lax.optimization_barrier((pieces, tied, evaluations))
+            if number == 2:
+                ends = tied
+            elif number == 3:
+                quotient = tied
+        arrived.append(exchange(pieces, owners, sent))
+        if number == 0:
+            batched, arrived[0][2:] = lax.optimization_barrier((batched, arrived[0][2:]))
+            moved = [batched[0]] + [
+                lax.ppermute(batched[far], "limb", [(i, (i + far) % limb_size) for i in range(limb_size)])
+                for far in range(1, limb_size)
+            ]
+        if number == 1:
+            sums = functools.reduce(jnp.add, moved)
             values = shift_sum([sums[i * columns:(i + 1) * columns] for i in range(poly_size)], "poly")
-            ends = segment_states(values, point_index, point_cycle)
-            pieces, ends = lax.optimization_barrier((pieces, ends))
-        if number == len(chunks) - 1:
-            while used < number - 2:
-                evaluations = second_section(tables, arrived[used], evaluations, *chunks[used], polys, owners)
-                used += 1
-            gathered = from_all_owners(ends)
-            quotient = quotient_columns(values, ends, gathered, offsets, point_index, point_cycle)
-            pieces, quotient, evaluations = lax.optimization_barrier((pieces, quotient, evaluations))
-        arrived.append(exchange(pieces[:owners], owners, sent))
-        if number == 1:
-            offsets = jnp.sum(batch_weights[None] * claimed, axis=2)
-            pieces[owners:], arrived[0][1:], offsets = lax.optimization_barrier(
-                (pieces[owners:], arrived[0][1:], offsets)
-            )
-            sums = shift_sum(pieces[owners:], "limb")
-            offsets = lax.psum(offsets, ("poly", "limb"))
+            offsets = shift_sum([shift_sum([offsets] * limb_size, "limb")] * poly_size, "poly")
             offsets = lax.dynamic_slice_in_dim(offsets, (me_poly * limb_size + me_limb) * columns, columns, axis=1)
 
     for number in range(used, len(chunks)):

time: 305 us -> 290 us (0.951)
  waiting for transfers between devices: 36.8 us -> 71.3 us
  blocking collectives: 24.6 us -> 0 us
  starting transfers between devices: 120 us -> 104 us
  local copies, waits for them, and re-layouts: 31 us -> 18.6 us
  other arithmetic: 20.1 us -> 28 us
  Pallas kernels: 66 us -> 61.4 us
    ppermute x3, starting transfers between devices: 48 us -> 3.88 us  [from_all_owners(): lax.ppermute(last, 'coef', [(i, (i + far) % owners) for i in range(owners)])]
    ppermute x2 -> x3, waiting for transfers between devices: 0.01 us -> 39 us  [shift_sum(): lax.ppermute(pieces[far], axis, [(i, (i + far) % size) for i in range(siz...]
    ppermute x15 -> x12, starting transfers between devices: 70.4 us -> 97.5 us  [exchange(): lax.ppermute(piece, 'coef', [(i, (i + far) % owners) for i in range(owner...]
    psum x1 -> x0, blocking collectives: 24.6 us -> none  [shards(): offsets = lax.psum(offsets, ('poly', 'limb'))]
    unnamed x117 -> x95, local copies, waits for them, and re-layouts: 21.1 us -> 10.7 us
    ppermute x15 -> x12, waiting for transfers between devices: 36.8 us -> 32 us  [exchange(): lax.ppermute(piece, 'coef', [(i, (i + far) % owners) for i in range(owner...]
    add x0 -> x1, other arithmetic: none -> 4.4 us  [shards(): sums = functools.reduce(jnp.add, moved)]
    pallas_call x5 -> x4, Pallas kernels: 39 us -> 34.7 us  [second_section(): pl.pallas_call(functools.partial(second_kernel, group, owners), out_shape...]
  transfers between devices with their start and end apart: 20 -> 19, of which waited for: 2 -> 5; matrix products, arithmetic and copies ran while one was open for 11% -> 13% of each run, Pallas kernels for 20% -> 19%
where the time goes in v3:
time: 290 us; the launch traced here: 286 us
  starting transfers between devices  104 us (36%)
  waiting for transfers between devices  71.3 us (25%)
  Pallas kernels  61.4 us (21%)
  other arithmetic  28 us (10%)
  local copies, waits for them, and re-layouts  18.6 us (6%)
    ppermute x12, starting transfers between devices, exchange(): lax.ppermute(piece, 'coef', [(i, (i + far) % owners) for i in range(owner...  97.5 us
    ppermute x3, waiting for transfers between devices, shift_sum(): lax.ppermute(pieces[far], axis, [(i, (i + far) % size) for i in range(siz...  39 us
    pallas_call x4, Pallas kernels, second_section(): pl.pallas_call(functools.partial(second_kernel, group, owners), out_shape...  34.7 us
    ppermute x12, waiting for transfers between devices, exchange(): lax.ppermute(piece, 'coef', [(i, (i + far) % owners) for i in range(owner...  32 us
    pallas_call x1, Pallas kernels, rest_sections(): pl.pallas_call(functools.partial(rest_kernel, min(8, LEN_COLS // owners),...  18.7 us
    unnamed x95, local copies, waits for them, and re-layouts  10.7 us
  transfers between devices with their start and end apart: 19, of which 5 were waited for; matrix products, arithmetic and copies ran while one was open for 13% of the time, Pallas kernels for 19%

profile of v3, /device:TPU:0, one launch (start us, length us, event | category | flops | bytes accessed | tf_op | source)
XLA Modules:
  0.0 286.2 jit_solution(14182716371927904685)
XLA Ops:
  0.6 0.9 copy-done.7
  1.6 4.6 %first_section.1 = (f32[4,2,4,64,128]{4,3,2,1,0:T(8,128)S(1)}, f32[4,2,4,64,128]{4,3,2,1,0:T(8,128)}, f32[4,2,4,64,128]{4,3,2,1,0:T(8,128)}, f32[4,2,4,64,128]{4,3,2,1,0:T(8,128)S(1)}) custom-call(f32[512,128]{1,0:T(8,128)S(1)} %copy-done.7, f32[12,128,1024]{2,1,0:T(8,128)} %coeff_ref.3), custom_call_target="tpu_custom_call" | custom-call | flops 1 | bytes 1 | tf_op jit(solution)/shard_map/first_section/pallas_call | solution.py:150
  6.2 4.0 %collective-permute-start = (f32[4,2,4,64,128]{4,3,2,1,0:T(8,128)}, f32[4,2,4,64,128]{4,3,2,1,0:T(8,128)S(1)}, u32[]{:S(2)}, u32[]{:S(2)}) collective-permute-start(f32[4,2,4,64,128]{4,3,2,1,0:T(8,128)} %get-tuple-element.52), channel_id=1, source_target_pairs={{0,8},{4,12},{8,0},{12,4},{1,9},{5,13},{9,1},{13,5},{2,10},{6,14},... | collective-permute-start | bytes 3145736 | tf_op jit(solution)/shard_map/ppermute | solution.py:404
  10.2 1.4 collective-permute-start.1
  12.4 18.7 %rest_sections.1 = (f32[5,2,4,64,128]{4,3,2,1,0:T(8,128)S(1)}, f32[5,2,4,64,128]{4,3,2,1,0:T(8,128)S(1)}, f32[5,2,4,64,128]{4,3,2,1,0:T(8,128)}, f32[5,2,4,64,12...) custom-call(f32[512,128]{1,0:T(8,128)S(1)} %copy-done.8, ...), custom_call_target="tpu_custom_call" | custom-call | flops 1 | bytes 1 | tf_op jit(solution)/shard_map/rest_sections/pallas_call | solution.py:182
  31.1 1.2 copy-done.3
  32.3 0.8 copy-done.9
  33.1 0.7 copy-done.11
  33.8 1.1 copy-done.13
  35.6 0.7 copy-done.16
  37.0 19.9 %collective-permute-done.refs_2_ = f32[4,2,4,64,128]{4,3,2,1,0:T(8,128)S(1)} collective-permute-done((f32[4,2,4,64,128]{4,3,2,1,0:T(8,128)}, f32[4,2,4,64,128]{4,3,2,1,0:T(8,128)S(1)}, u32[]{:S(2)}, u32[]{:S(2)}) %collective-permute-start) | collective-permute-done | bytes 1048608 | tf_op jit(solution)/shard_map/ppermute | solution.py:404
  58.1 22.4 %collective-permute-start.4 = (f32[4,2,4,64,128]{4,3,2,1,0:T(8,128)}, f32[4,2,4,64,128]{4,3,2,1,0:T(8,128)}, u32[]{:S(2)}, u32[]{:S(2)}) collective-permute-start(f32[4,2,4,64,128]{4,3,2,1,0:T(8,128)} %get-tuple-element.62), channel_id=1, source_target_pairs={{0,4},{4,8},{8,12},{12,0},{1,5},{5,9},{9,13},{13,1},{2,6},{6,10},{... | collective-permute-start | bytes 3145736 | tf_op jit(solution)/shard_map/ppermute | solution.py:404
  80.5 3.3 %collective-permute-start.11 = (f32[5,2,4,64,128]{4,3,2,1,0:T(8,128)}, f32[5,2,4,64,128]{4,3,2,1,0:T(8,128)}, u32[]{:S(2)}, u32[]{:S(2)}) collective-permute-start(f32[5,2,4,64,128]{4,3,2,1,0:T(8,128)} %get-tuple-element.71), channel_id=1, source_target_pairs={{0,8},{4,12},{8,0},{12,4},{1,9},{5,13},{9,1},{13,5},{2,10},{6,14},... | collective-permute-start | bytes 3932168 | tf_op jit(solution)/shard_map/ppermute | solution.py:404
  88.4 4.4 %add.277 = f32[8,128,1024]{2,1,0:T(8,128)S(1)} add(f32[8,128,1024]{2,1,0:T(8,128)} %get-tuple-element.54, f32[8,128,1024]{2,1,0:T(8,128)} %collective-permute-done.2) | non-fusion elementwise | flops 1048576 | bytes 12582912 | tf_op jit(solution)/shard_map/add | solution.py:480
  92.8 1.6 slice.35
  94.4 1.0 copy-done.20
  95.4 1.5 collective-permute-start.3
  98.1 1.3 constant_dynamic-slice_fusion.1.turn_ref
  99.5 1.3 constant_dynamic-slice_fusion.2.middle_ref
  102.2 1.2 add.286
  103.9 39.0 %collective-permute-done.9 = f32[2,16]{1,0:T(2,128)} collective-permute-done((f32[2,16]{1,0:T(2,128)}, f32[2,16]{1,0:T(2,128)}, u32[]{:S(2)}, u32[]{:S(2)}) %collective-permute-start.9) | collective-permute-done | bytes 160 | tf_op jit(solution)/shard_map/ppermute | solution.py:418
  143.6 1.4 fusion.16
  145.6 1.4 cosine_multiply_fusion
  147.0 1.4 cosine_multiply_fusion.2
  148.4 1.4 cosine_multiply_fusion.1
  149.8 1.4 multiply_select_fusion.3
  151.2 1.2 copy-done.6
  152.4 8.3 %second_section.4.refs_4_ = f32[2,32,12,32,128]{4,3,2,1,0:T(8,128)} custom-call(bf16[32,64,192]{2,1,0:T(8,128)(2,1)S(1)} %constant_dynamic-slice_fusion.2.middle_ref, f32[32,2,32,128]{3,2,1,0:T(8,128)S(1)} %constant_dynamic-slice_fusion.1.turn_ref, bf16[768,256]{1,0:T(8,128)(2,1)S(1)} %copy-done.2, f32[4,2,4,64,128]{4,3,2,1,0:T(8,128)S(1)} %get-tuple-element.60.refs_0_, ...), custom_call_target="tpu_custom_call" | custom-call | flops 1 | bytes 1 | tf_op jit(solution)/shard_map/second_section/pallas_call | solution.py:252
  160.8 2.1 slice_add_fusion.value_ref
  163.1 1.9 convolution_bitcast_fusion
  165.0 1.3 copy-done
  166.9 0.9 collective-permute-start.5
  167.8 2.4 collective-permute-start.6
  170.8 1.4 collective-permute-start.12
  172.6 45.7 %collective-permute-start.17 = (f32[2,2,4,64,128]{4,3,2,1,0:T(8,128)}, f32[2,2,4,64,128]{4,3,2,1,0:T(8,128)S(1)}, u32[]{:S(2)}, u32[]{:S(2)}) collective-permute-start(f32[2,2,4,64,128]{4,3,2,1,0:T(8,128)} %get-tuple-element.86), channel_id=1, source_target_pairs={{0,8},{4,12},{8,0},{12,4},{1,9},{5,13},{9,1},{13,5},{2,10},{6,14},... | collective-permute-start | bytes 1572872 | tf_op jit(solution)/shard_map/ppermute | solution.py:404
  218.3 3.8 %collective-permute-start.18 = (f32[2,2,4,64,128]{4,3,2,1,0:T(8,128)}, f32[2,2,4,64,128]{4,3,2,1,0:T(8,128)}, u32[]{:S(2)}, u32[]{:S(2)}) collective-permute-start(f32[2,2,4,64,128]{4,3,2,1,0:T(8,128)} %get-tuple-element.87), channel_id=1, source_target_pairs={{0,12},{4,0},{8,4},{12,8},{1,13},{5,1},{9,5},{13,9},{2,14},{6,2},{... | collective-permute-start | bytes 1572872 | tf_op jit(solution)/shard_map/ppermute | solution.py:404
  222.4 2.3 multiply_reduce_fusion.2
  225.6 1.7 copy.26
  227.3 1.5 pad_add_fusion.carry_ref
  229.0 16.3 %second_section.5.refs_4_ = f32[2,32,12,32,128]{4,3,2,1,0:T(8,128)} custom-call(bf16[32,64,192]{2,1,0:T(8,128)(2,1)S(1)} %constant_dynamic-slice_fusion.2.middle_ref, f32[32,2,32,128]{3,2,1,0:T(8,128)S(1)} %constant_dynamic-slice_fusion.1.turn_ref, bf16[768,256]{1,0:T(8,128)(2,1)S(1)} %copy-done.2, ...), custom_call_target="tpu_custom_call", output_to_operand_aliasing={{}: (7, {})} | custom-call | flops 1 | bytes 1 | tf_op jit(solution)/shard_map/second_section/pallas_call | solution.py:252
  245.3 3.4 %filter_columns.1 = f32[2,4,128,1024]{3,2,1,0:T(8,128)} custom-call(f32[4,128,1024]{2,1,0:T(8,128)S(1)} %copy-done.1, f32[4,128,256]{2,1,0:T(8,128)S(1)} %maximum_negate_fusion.table_ref, f32[2,4,128,8]{3,2,1,0:T(8,128)S(1)} %pad_add_fusion.carry_ref, f32[4,2,128]{2,1,0:T(2,128)S(1)} %maximum_negate_fusion.1.reach_ref), custom_call_target="tpu_custom_call" | custom-call | flops 1 | bytes 1 | tf_op jit(solution)/shard_map/filter_columns/pallas_call | solution.py:282
  248.8 11.5 %collective-permute-start.14 = (f32[1,2,4,64,128]{4,3,2,1,0:T(8,128)S(1)}, f32[1,2,4,64,128]{4,3,2,1,0:T(8,128)S(1)}, u32[]{:S(2)}, u32[]{:S(2)}) collective-permute-start(f32[1,2,4,64,128]{4,3,2,1,0:T(8,128)S(1)} %copy-done.19), channel_id=1, source_target_pairs={{0,8},{4,12},{8,0},{12,4},{1,9},{5,13},{9,1},{13,5},{2,10},{6,14},... | collective-permute-start | bytes 786440 | tf_op jit(solution)/shard_map/ppermute | solution.py:404
  260.3 1.4 collective-permute-start.13
  261.7 2.4 collective-permute-start.16
  264.1 7.1 %second_section.6.refs_4_ = f32[2,32,12,32,128]{4,3,2,1,0:T(8,128)} custom-call(bf16[32,64,192]{2,1,0:T(8,128)(2,1)S(1)} %constant_dynamic-slice_fusion.2.middle_ref, f32[32,2,32,128]{3,2,1,0:T(8,128)S(1)} %constant_dynamic-slice_fusion.1.turn_ref, bf16[768,256]{1,0:T(8,128)(2,1)S(1)} %copy-done.2, ...), custom_call_target="tpu_custom_call", output_to_operand_aliasing={{}: (7, {})} | custom-call | flops 1 | bytes 1 | tf_op jit(solution)/shard_map/second_section/pallas_call | solution.py:252
  271.2 10.3 %collective-permute-done.14.refs_2_ = f32[1,2,4,64,128]{4,3,2,1,0:T(8,128)S(1)} collective-permute-done((f32[1,2,4,64,128]{4,3,2,1,0:T(8,128)S(1)}, f32[1,2,4,64,128]{4,3,2,1,0:T(8,128)S(1)}, u32[]{:S(2)}, u32[]{:S(2)}) %collective-permute-start.14) | collective-permute-done | bytes 262176 | tf_op jit(solution)/shard_map/ppermute | solution.py:404
  281.5 1.8 collective-permute-done.16.refs_3_
  283.2 2.9 %second_section.7 = f32[2,32,12,32,128]{4,3,2,1,0:T(8,128)} custom-call(bf16[32,64,192]{2,1,0:T(8,128)(2,1)S(1)} %constant_dynamic-slice_fusion.2.middle_ref, f32[32,2,32,128]{3,2,1,0:T(8,128)S(1)} %constant_dynamic-slice_fusion.1.turn_ref, bf16[768,256]{1,0:T(8,128)(2,1)S(1)} %copy-done.2, ...), custom_call_target="tpu_custom_call", output_to_operand_aliasing={{}: (7, {})} | custom-call | flops 1 | bytes 1 | tf_op jit(solution)/shard_map/second_section/pallas_call | solution.py:252
  (140 shorter events, 15.2 us)
Async XLA Ops:
  1.6 10.2 %copy-start.27 = (f32[16,12]{1,0:T(8,128)S(1)}, f32[16,12]{1,0:T(8,128)}, u32[]{:S(2)}) copy-start(f32[16,12]{1,0:T(8,128)} %param.10) | copy-start | bytes 2308
  1.6 10.8 %copy-start.8 = (f32[512,128]{1,0:T(8,128)S(1)}, f32[512,128]{1,0:T(8,128)}, u32[]{:S(2)}) copy-start(f32[512,128]{1,0:T(8,128)} %constant.133.clone.table_ref) | copy-start | bytes 786436
  6.2 50.7 %collective-permute-start = (f32[4,2,4,64,128]{4,3,2,1,0:T(8,128)}, f32[4,2,4,64,128]{4,3,2,1,0:T(8,128)S(1)}, u32[]{:S(2)}, u32[]{:S(2)}) collective-permute-start(f32[4,2,4,64,128]{4,3,2,1,0:T(8,128)} %get-tuple-element.52), channel_id=1, source_target_pairs={{0,8},{4,12},{8,0},{12,4},{1,9},{5,13},{9,1},{13,5},{2,10},{6,14},... | collective-permute-start | bytes 3145736 | tf_op jit(solution)/shard_map/ppermute | solution.py:404
  10.2 46.7 %collective-permute-start.1 = (f32[4,2,4,64,128]{4,3,2,1,0:T(8,128)S(1)}, f32[4,2,4,64,128]{4,3,2,1,0:T(8,128)}, u32[]{:S(2)}, u32[]{:S(2)}) collective-permute-start(f32[4,2,4,64,128]{4,3,2,1,0:T(8,128)S(1)} %get-tuple-element.53), channel_id=1, source_target_pairs={{0,12},{4,0},{8,4},{12,8},{1,13},{5,1},{9,5},{13,9},{2,14},{6,2},{... | collective-permute-start | bytes 3145736 | tf_op jit(solution)/shard_map/ppermute | solution.py:404
  12.4 44.7 %copy-start.31 = (f32[2,16,12]{1,0,2:T(2,128)S(1)}, f32[2,16,12]{1,0,2:T(2,128)}, u32[]{:S(2)}) copy-start(f32[2,16,12]{1,0,2:T(2,128)} %param.11) | copy-start | bytes 4612
  56.9 35.8 %copy-start.5 = (f32[4,2,4,64,128]{4,3,2,1,0:T(8,128)}, f32[4,2,4,64,128]{4,3,2,1,0:T(8,128)S(1)}, u32[]{:S(2)}) copy-start(f32[4,2,4,64,128]{4,3,2,1,0:T(8,128)S(1)} %collective-permute-done.refs_2_) | copy-start | bytes 3145732
  56.9 31.4 %collective-permute-start.2 = (f32[8,128,1024]{2,1,0:T(8,128)}, f32[8,128,1024]{2,1,0:T(8,128)}, u32[]{:S(2)}, u32[]{:S(2)}) collective-permute-start(f32[8,128,1024]{2,1,0:T(8,128)} %get-tuple-element.55), channel_id=1, source_target_pairs={{0,1},{1,0},{2,3},{3,2},{4,5},{5,4},{6,7},{7,6},{8,9},{9,8},{10,11... | collective-permute-start | bytes 12582920 | tf_op jit(solution)/shard_map/ppermute | solution.py:476
  57.7 44.5 %collective-permute-start.8 = (f32[2,16]{1,0:T(2,128)}, f32[2,16]{1,0:T(2,128)}, u32[]{:S(2)}, u32[]{:S(2)}) collective-permute-start(f32[2,16]{1,0:T(2,128)} %multiply_reduce_fusion.4), channel_id=1, source_target_pairs={{0,1},{1,0},{2,3},{3,2},{4,5},{5,4},{6,7},{7,6},{8,9},{9,8},{10,11... | collective-permute-start | bytes 392 | tf_op jit(solution)/shard_map/ppermute | solution.py:418
  58.1 93.1 %collective-permute-start.4 = (f32[4,2,4,64,128]{4,3,2,1,0:T(8,128)}, f32[4,2,4,64,128]{4,3,2,1,0:T(8,128)}, u32[]{:S(2)}, u32[]{:S(2)}) collective-permute-start(f32[4,2,4,64,128]{4,3,2,1,0:T(8,128)} %get-tuple-element.62), channel_id=1, source_target_pairs={{0,4},{4,8},{8,12},{12,0},{1,5},{5,9},{9,13},{13,1},{2,6},{6,10},{... | collective-permute-start | bytes 3145736 | tf_op jit(solution)/shard_map/ppermute | solution.py:404
  80.5 90.3 %collective-permute-start.10 = (f32[5,2,4,64,128]{4,3,2,1,0:T(8,128)}, f32[5,2,4,64,128]{4,3,2,1,0:T(8,128)}, u32[]{:S(2)}, u32[]{:S(2)}) collective-permute-start(f32[5,2,4,64,128]{4,3,2,1,0:T(8,128)} %copy-done.13), channel_id=1, source_target_pairs={{0,4},{4,8},{8,12},{12,0},{1,5},{5,9},{9,13},{13,1},{2,6},{6,10},{... | collective-permute-start | bytes 3932168 | tf_op jit(solution)/shard_map/ppermute | solution.py:404
  80.5 148.3 %collective-permute-start.11 = (f32[5,2,4,64,128]{4,3,2,1,0:T(8,128)}, f32[5,2,4,64,128]{4,3,2,1,0:T(8,128)}, u32[]{:S(2)}, u32[]{:S(2)}) collective-permute-start(f32[5,2,4,64,128]{4,3,2,1,0:T(8,128)} %get-tuple-element.71), channel_id=1, source_target_pairs={{0,8},{4,12},{8,0},{12,4},{1,9},{5,13},{9,1},{13,5},{2,10},{6,14},... | collective-permute-start | bytes 3932168 | tf_op jit(solution)/shard_map/ppermute | solution.py:404
  95.4 65.4 %collective-permute-start.3 = (f32[4,128,1024]{2,1,0:T(8,128)}, f32[4,128,1024]{2,1,0:T(8,128)}, u32[]{:S(2)}, u32[]{:S(2)}) collective-permute-start(f32[4,128,1024]{2,1,0:T(8,128)} %slice.35), channel_id=1, source_target_pairs={{0,2},{2,0},{1,3},{3,1},{4,6},{6,4},{5,7},{7,5},{8,10},{10,8},{9,1... | collective-permute-start | bytes 6291464 | tf_op jit(solution)/shard_map/ppermute | solution.py:418
  98.1 53.1 %copy-start.2 = (bf16[768,256]{1,0:T(8,128)(2,1)S(1)}, bf16[768,256]{1,0:T(8,128)(2,1)}, u32[]{:S(2)}) copy-start(bf16[768,256]{1,0:T(8,128)(2,1)} %constant.136.clone.last_ref) | copy-start | bytes 1179652
  103.4 39.5 %collective-permute-start.9 = (f32[2,16]{1,0:T(2,128)}, f32[2,16]{1,0:T(2,128)}, u32[]{:S(2)}, u32[]{:S(2)}) collective-permute-start(f32[2,16]{1,0:T(2,128)} %add.286), channel_id=1, source_target_pairs={{0,2},{2,0},{1,3},{3,1},{4,6},{6,4},{5,7},{7,5},{8,10},{10,8},{9,1... | collective-permute-start | bytes 392 | tf_op jit(solution)/shard_map/ppermute | solution.py:418
  152.4 8.3 %copy-start.21 = (f32[8,128,1024]{2,1,0:T(8,128)S(1)}, f32[8,128,1024]{2,1,0:T(8,128)}, u32[]{:S(2)}) copy-start(f32[8,128,1024]{2,1,0:T(8,128)} %copy-done.20) | copy-start | bytes 12582916
  162.9 59.2 %copy-start.34 = (f32[4,4]{0,1:T(4,128)S(1)}, f32[4,4]{0,1:T(4,128)}, u32[]{:S(2)}) copy-start(f32[4,4]{0,1:T(4,128)} %get-tuple-element.120) | copy-start | bytes 196
  163.0 59.2 %copy-start.35 = (f32[4,4]{0,1:T(4,128)S(1)}, f32[4,4]{0,1:T(4,128)}, u32[]{:S(2)}) copy-start(f32[4,4]{0,1:T(4,128)} %get-tuple-element.121) | copy-start | bytes 196
  163.0 59.2 %copy-start.36 = (f32[4,4]{0,1:T(4,128)S(1)}, f32[4,4]{0,1:T(4,128)}, u32[]{:S(2)}) copy-start(f32[4,4]{0,1:T(4,128)} %get-tuple-element.126) | copy-start | bytes 196
  163.0 59.2 %copy-start.37 = (f32[4,4]{0,1:T(4,128)S(1)}, f32[4,4]{0,1:T(4,128)}, u32[]{:S(2)}) copy-start(f32[4,4]{0,1:T(4,128)} %get-tuple-element.127) | copy-start | bytes 196
  163.0 59.3 %copy-start.43 = (f32[4]{0:T(128)S(1)}, f32[4]{0:T(128)}, u32[]{:S(2)}) copy-start(f32[4]{0:T(128)} %get-tuple-element.118) | copy-start | bytes 52
  163.0 59.3 %copy-start.44 = (f32[4]{0:T(128)S(1)}, f32[4]{0:T(128)}, u32[]{:S(2)}) copy-start(f32[4]{0:T(128)} %get-tuple-element.119) | copy-start | bytes 52
  163.0 59.3 %copy-start.46 = (pred[128]{0:T(512)(128)(4,1)S(1)}, pred[128]{0:T(512)(128)(4,1)}, u32[]{:S(2)}) copy-start(pred[128]{0:T(512)(128)(4,1)} %iota_compare_fusion) | copy-start | bytes 388
  163.0 59.4 %copy-start.23 = (s32[128,128]{1,0:T(8,128)S(1)}, s32[128,128]{1,0:T(8,128)}, u32[]{:S(2)}) copy-start(s32[128,128]{1,0:T(8,128)} %get-tuple-element.138) | copy-start | bytes 196612
  163.0 59.4 %copy-start.24 = (s32[128,128]{1,0:T(8,128)S(1)}, s32[128,128]{1,0:T(8,128)}, u32[]{:S(2)}) copy-start(s32[128,128]{1,0:T(8,128)} %get-tuple-element.139) | copy-start | bytes 196612
  163.0 59.4 %copy-start.25 = (f32[128,128]{1,0:T(8,128)S(1)}, f32[128,128]{1,0:T(8,128)}, u32[]{:S(2)}) copy-start(f32[128,128]{1,0:T(8,128)} %get-tuple-element.140) | copy-start | bytes 196612
  163.0 59.4 %copy-start.26 = (f32[128,128]{1,0:T(8,128)S(1)}, f32[128,128]{1,0:T(8,128)}, u32[]{:S(2)}) copy-start(f32[128,128]{1,0:T(8,128)} %get-tuple-element.141) | copy-start | bytes 196612
  163.1 59.4 %copy-start.28 = (s32[4]{0:T(128)S(1)}, s32[4]{0:T(128)}, u32[]{:S(2)}) copy-start(s32[4]{0:T(128)} %param.12) | copy-start | bytes 52
  163.1 59.3 %copy-start.30 = (f32[4]{0:T(128)S(1)}, f32[4]{0:T(128)}, u32[]{:S(2)}) copy-start(f32[4]{0:T(128)} %copy-done.29) | copy-start | bytes 52
  163.1 59.3 %copy-start.45 = (f32[4]{0:T(128)S(1)}, f32[4]{0:T(128)}, u32[]{:S(2)}) copy-start(f32[4]{0:T(128)} %get-tuple-element.130) | copy-start | bytes 52
  163.1 61.7 %copy-start.41 = (f32[4]{0:T(128)S(1)}, f32[4]{0:T(128)}, u32[]{:S(2)}) copy-start(f32[4]{0:T(128)} %get-tuple-element.124) | copy-start | bytes 52
  163.1 61.7 %copy-start.42 = (f32[4]{0:T(128)S(1)}, f32[4]{0:T(128)}, u32[]{:S(2)}) copy-start(f32[4]{0:T(128)} %get-tuple-element.125) | copy-start | bytes 52
  163.1 61.7 %copy-start.32 = (f32[4,8]{1,0:T(4,128)S(1)}, f32[4,8]{1,0:T(4,128)}, u32[]{:S(2)}) copy-start(f32[4,8]{1,0:T(4,128)} %get-tuple-element.116) | copy-start | bytes 388
  163.1 61.7 %copy-start.33 = (f32[4,8]{1,0:T(4,128)S(1)}, f32[4,8]{1,0:T(4,128)}, u32[]{:S(2)}) copy-start(f32[4,8]{1,0:T(4,128)} %get-tuple-element.117) | copy-start | bytes 388
  166.9 5.7 %collective-permute-start.5 = (f32[2,4,128]{2,1,0:T(4,128)S(1)}, f32[2,4,128]{2,1,0:T(4,128)S(1)}, u32[]{:S(2)}, u32[]{:S(2)}) collective-permute-start(f32[2,4,128]{2,1,0:T(4,128)S(1)} %slice_reduce_fusion), channel_id=1, source_target_pairs={{0,4},{4,8},{8,12},{12,0},{1,5},{5,9},{9,13},{13,1},{2,6},{6,10},{... | collective-permute-start | bytes 12296 | tf_op jit(solution)/shard_map/ppermute | solution.py:337
  167.8 50.5 %collective-permute-start.6 = (f32[2,4,128]{2,1,0:T(4,128)S(1)}, f32[2,4,128]{2,1,0:T(4,128)S(1)}, u32[]{:S(2)}, u32[]{:S(2)}) collective-permute-start(f32[2,4,128]{2,1,0:T(4,128)S(1)} %slice_reduce_fusion), channel_id=1, source_target_pairs={{0,8},{4,12},{8,0},{12,4},{1,9},{5,13},{9,1},{13,5},{2,10},{6,14},... | collective-permute-start | bytes 12296 | tf_op jit(solution)/shard_map/ppermute | solution.py:337
  170.2 48.1 %collective-permute-start.7 = (f32[2,4,128]{2,1,0:T(4,128)S(1)}, f32[2,4,128]{2,1,0:T(4,128)S(1)}, u32[]{:S(2)}, u32[]{:S(2)}) collective-permute-start(f32[2,4,128]{2,1,0:T(4,128)S(1)} %slice_reduce_fusion), channel_id=1, source_target_pairs={{0,12},{4,0},{8,4},{12,8},{1,13},{5,1},{9,5},{13,9},{2,14},{6,2},{... | collective-permute-start | bytes 12296 | tf_op jit(solution)/shard_map/ppermute | solution.py:337
  170.8 58.0 %collective-permute-start.12 = (f32[5,2,4,64,128]{4,3,2,1,0:T(8,128)}, f32[5,2,4,64,128]{4,3,2,1,0:T(8,128)}, u32[]{:S(2)}, u32[]{:S(2)}) collective-permute-start(f32[5,2,4,64,128]{4,3,2,1,0:T(8,128)} %get-tuple-element.72), channel_id=1, source_target_pairs={{0,12},{4,0},{8,4},{12,8},{1,13},{5,1},{9,5},{13,9},{2,14},{6,2},{... | collective-permute-start | bytes 3932168 | tf_op jit(solution)/shard_map/ppermute | solution.py:404
  172.6 91.5 %collective-permute-start.17 = (f32[2,2,4,64,128]{4,3,2,1,0:T(8,128)}, f32[2,2,4,64,128]{4,3,2,1,0:T(8,128)S(1)}, u32[]{:S(2)}, u32[]{:S(2)}) collective-permute-start(f32[2,2,4,64,128]{4,3,2,1,0:T(8,128)} %get-tuple-element.86), channel_id=1, source_target_pairs={{0,8},{4,12},{8,0},{12,4},{1,9},{5,13},{9,1},{13,5},{2,10},{6,14},... | collective-permute-start | bytes 1572872 | tf_op jit(solution)/shard_map/ppermute | solution.py:404
  218.3 43.4 %collective-permute-start.15 = (f32[2,2,4,64,128]{4,3,2,1,0:T(8,128)}, f32[2,2,4,64,128]{4,3,2,1,0:T(8,128)}, u32[]{:S(2)}, u32[]{:S(2)}) collective-permute-start(f32[2,2,4,64,128]{4,3,2,1,0:T(8,128)} %get-tuple-element.81), channel_id=1, source_target_pairs={{0,4},{4,8},{8,12},{12,0},{1,5},{5,9},{9,13},{13,1},{2,6},{6,10},{... | collective-permute-start | bytes 1572872 | tf_op jit(solution)/shard_map/ppermute | solution.py:404
  218.3 45.8 %collective-permute-start.18 = (f32[2,2,4,64,128]{4,3,2,1,0:T(8,128)}, f32[2,2,4,64,128]{4,3,2,1,0:T(8,128)}, u32[]{:S(2)}, u32[]{:S(2)}) collective-permute-start(f32[2,2,4,64,128]{4,3,2,1,0:T(8,128)} %get-tuple-element.87), channel_id=1, source_target_pairs={{0,12},{4,0},{8,4},{12,8},{1,13},{5,1},{9,5},{13,9},{2,14},{6,2},{... | collective-permute-start | bytes 1572872 | tf_op jit(solution)/shard_map/ppermute | solution.py:404
  229.0 16.3 %copy-start.1 = (f32[4,128,1024]{2,1,0:T(8,128)S(1)}, f32[4,128,1024]{2,1,0:T(8,128)}, u32[]{:S(2)}) copy-start(f32[4,128,1024]{2,1,0:T(8,128)} %copy-done) | copy-start | bytes 6291460
  245.3 15.0 %copy-start.17 = (f32[1,2,4,64,128]{4,3,2,1,0:T(8,128)S(1)}, f32[1,2,4,64,128]{4,3,2,1,0:T(8,128)}, u32[]{:S(2)}) copy-start(f32[1,2,4,64,128]{4,3,2,1,0:T(8,128)} %copy-done.16) | copy-start | bytes 786436
  245.3 16.4 %copy-start.15 = (f32[1,2,4,64,128]{4,3,2,1,0:T(8,128)S(1)}, f32[1,2,4,64,128]{4,3,2,1,0:T(8,128)}, u32[]{:S(2)}) copy-start(f32[1,2,4,64,128]{4,3,2,1,0:T(8,128)} %copy-done.14) | copy-start | bytes 786436
  245.3 18.8 %copy-start.10 = (f32[2,2,4,64,128]{4,3,2,1,0:T(8,128)S(1)}, f32[2,2,4,64,128]{4,3,2,1,0:T(8,128)}, u32[]{:S(2)}) copy-start(f32[2,2,4,64,128]{4,3,2,1,0:T(8,128)} %copy-done.9) | copy-start | bytes 1572868
  248.7 34.5 %copy-start.12 = (f32[1,2,4,64,128]{4,3,2,1,0:T(8,128)S(1)}, f32[1,2,4,64,128]{4,3,2,1,0:T(8,128)}, u32[]{:S(2)}) copy-start(f32[1,2,4,64,128]{4,3,2,1,0:T(8,128)} %copy-done.11) | copy-start | bytes 786436
  248.8 32.7 %collective-permute-start.14 = (f32[1,2,4,64,128]{4,3,2,1,0:T(8,128)S(1)}, f32[1,2,4,64,128]{4,3,2,1,0:T(8,128)S(1)}, u32[]{:S(2)}, u32[]{:S(2)}) collective-permute-start(f32[1,2,4,64,128]{4,3,2,1,0:T(8,128)S(1)} %copy-done.19), channel_id=1, source_target_pairs={{0,8},{4,12},{8,0},{12,4},{1,9},{5,13},{9,1},{13,5},{2,10},{6,14},... | collective-permute-start | bytes 786440 | tf_op jit(solution)/shard_map/ppermute | solution.py:404
  260.3 21.2 %collective-permute-start.13 = (f32[1,2,4,64,128]{4,3,2,1,0:T(8,128)S(1)}, f32[1,2,4,64,128]{4,3,2,1,0:T(8,128)S(1)}, u32[]{:S(2)}, u32[]{:S(2)}) collective-permute-start(f32[1,2,4,64,128]{4,3,2,1,0:T(8,128)S(1)} %copy-done.17), channel_id=1, source_target_pairs={{0,4},{4,8},{8,12},{12,0},{1,5},{5,9},{9,13},{13,1},{2,6},{6,10},{... | collective-permute-start | bytes 786440 | tf_op jit(solution)/shard_map/ppermute | solution.py:404
  261.7 21.5 %collective-permute-start.16 = (f32[1,2,4,64,128]{4,3,2,1,0:T(8,128)S(1)}, f32[1,2,4,64,128]{4,3,2,1,0:T(8,128)S(1)}, u32[]{:S(2)}, u32[]{:S(2)}) collective-permute-start(f32[1,2,4,64,128]{4,3,2,1,0:T(8,128)S(1)} %copy-done.15), channel_id=1, source_target_pairs={{0,12},{4,0},{8,4},{12,8},{1,13},{5,1},{9,5},{13,9},{2,14},{6,2},{... | collective-permute-start | bytes 786440 | tf_op jit(solution)/shard_map/ppermute | solution.py:404
  (18 other events, 47.5 us)

commit v4 on v3

--- a/solution.py
+++ b/solution.py
@@ -390,7 +390,8 @@
 
 
 def chunk_sizes(polys):
-    return [4, 5, 2, 1] if polys==12 else [1,2,2,1]
+    first, third = max(1, polys // 3), max(1, polys // 6)
+    return [first, polys - first - third - 1, third, 1]
 
 
 def exchange(pieces, owners, sent):

time: 290 us -> 290 us (level)
  no operation moved by 1% of the time
where the time goes in v4:
time: 290 us; the launch traced here: 286 us
  starting transfers between devices  104 us (36%)
  waiting for transfers between devices  71.3 us (25%)
  Pallas kernels  61.4 us (21%)
  other arithmetic  28 us (10%)
  local copies, waits for them, and re-layouts  18.6 us (6%)
    ppermute x12, starting transfers between devices, exchange(): lax.ppermute(piece, 'coef', [(i, (i + far) % owners) for i in range(owner...  97.5 us
    ppermute x3, waiting for transfers between devices, shift_sum(): lax.ppermute(pieces[far], axis, [(i, (i + far) % size) for i in range(siz...  39 us
    pallas_call x4, Pallas kernels, second_section(): pl.pallas_call(functools.partial(second_kernel, group, owners), out_shape...  34.7 us
    ppermute x12, waiting for transfers between devices, exchange(): lax.ppermute(piece, 'coef', [(i, (i + far) % owners) for i in range(owner...  32 us
    pallas_call x1, Pallas kernels, rest_sections(): pl.pallas_call(functools.partial(rest_kernel, min(8, LEN_COLS // owners),...  18.7 us
    unnamed x95, local copies, waits for them, and re-layouts  10.7 us
  transfers between devices with their start and end apart: 19, of which 5 were waited for; matrix products, arithmetic and copies ran while one was open for 13% of the time, Pallas kernels for 19%

profile of v4, /device:TPU:0, one launch (start us, length us, event | category | flops | bytes accessed | tf_op | source)
XLA Modules:
  0.0 286.2 jit_solution(14182716371927904685)
XLA Ops:
  0.6 0.9 copy-done.7
  1.6 4.6 %first_section.1 = (f32[4,2,4,64,128]{4,3,2,1,0:T(8,128)S(1)}, f32[4,2,4,64,128]{4,3,2,1,0:T(8,128)}, f32[4,2,4,64,128]{4,3,2,1,0:T(8,128)}, f32[4,2,4,64,128]{4,3,2,1,0:T(8,128)S(1)}) custom-call(f32[512,128]{1,0:T(8,128)S(1)} %copy-done.7, f32[12,128,1024]{2,1,0:T(8,128)} %coeff_ref.3), custom_call_target="tpu_custom_call" | custom-call | flops 1 | bytes 1 | tf_op jit(solution)/shard_map/first_section/pallas_call | solution.py:150
  6.2 4.0 %collective-permute-start = (f32[4,2,4,64,128]{4,3,2,1,0:T(8,128)}, f32[4,2,4,64,128]{4,3,2,1,0:T(8,128)S(1)}, u32[]{:S(2)}, u32[]{:S(2)}) collective-permute-start(f32[4,2,4,64,128]{4,3,2,1,0:T(8,128)} %get-tuple-element.52), channel_id=1, source_target_pairs={{0,8},{4,12},{8,0},{12,4},{1,9},{5,13},{9,1},{13,5},{2,10},{6,14},... | collective-permute-start | bytes 3145736 | tf_op jit(solution)/shard_map/ppermute | solution.py:405
  10.2 1.4 collective-permute-start.1
  12.4 18.7 %rest_sections.1 = (f32[5,2,4,64,128]{4,3,2,1,0:T(8,128)S(1)}, f32[5,2,4,64,128]{4,3,2,1,0:T(8,128)S(1)}, f32[5,2,4,64,128]{4,3,2,1,0:T(8,128)}, f32[5,2,4,64,12...) custom-call(f32[512,128]{1,0:T(8,128)S(1)} %copy-done.8, ...), custom_call_target="tpu_custom_call" | custom-call | flops 1 | bytes 1 | tf_op jit(solution)/shard_map/rest_sections/pallas_call | solution.py:182
  31.1 1.2 copy-done.3
  32.3 0.8 copy-done.9
  33.1 0.7 copy-done.11
  33.8 1.1 copy-done.13
  35.6 0.7 copy-done.16
  37.0 19.9 %collective-permute-done.refs_2_ = f32[4,2,4,64,128]{4,3,2,1,0:T(8,128)S(1)} collective-permute-done((f32[4,2,4,64,128]{4,3,2,1,0:T(8,128)}, f32[4,2,4,64,128]{4,3,2,1,0:T(8,128)S(1)}, u32[]{:S(2)}, u32[]{:S(2)}) %collective-permute-start) | collective-permute-done | bytes 1048608 | tf_op jit(solution)/shard_map/ppermute | solution.py:405
  58.1 22.4 %collective-permute-start.4 = (f32[4,2,4,64,128]{4,3,2,1,0:T(8,128)}, f32[4,2,4,64,128]{4,3,2,1,0:T(8,128)}, u32[]{:S(2)}, u32[]{:S(2)}) collective-permute-start(f32[4,2,4,64,128]{4,3,2,1,0:T(8,128)} %get-tuple-element.62), channel_id=1, source_target_pairs={{0,4},{4,8},{8,12},{12,0},{1,5},{5,9},{9,13},{13,1},{2,6},{6,10},{... | collective-permute-start | bytes 3145736 | tf_op jit(solution)/shard_map/ppermute | solution.py:405
  80.5 3.3 %collective-permute-start.11 = (f32[5,2,4,64,128]{4,3,2,1,0:T(8,128)}, f32[5,2,4,64,128]{4,3,2,1,0:T(8,128)}, u32[]{:S(2)}, u32[]{:S(2)}) collective-permute-start(f32[5,2,4,64,128]{4,3,2,1,0:T(8,128)} %get-tuple-element.71), channel_id=1, source_target_pairs={{0,8},{4,12},{8,0},{12,4},{1,9},{5,13},{9,1},{13,5},{2,10},{6,14},... | collective-permute-start | bytes 3932168 | tf_op jit(solution)/shard_map/ppermute | solution.py:405
  88.4 4.4 %add.277 = f32[8,128,1024]{2,1,0:T(8,128)S(1)} add(f32[8,128,1024]{2,1,0:T(8,128)} %get-tuple-element.54, f32[8,128,1024]{2,1,0:T(8,128)} %collective-permute-done.2) | non-fusion elementwise | flops 1048576 | bytes 12582912 | tf_op jit(solution)/shard_map/add | solution.py:481
  92.8 1.6 slice.35
  94.4 1.0 copy-done.20
  95.4 1.5 collective-permute-start.3
  98.1 1.3 constant_dynamic-slice_fusion.1.turn_ref
  99.5 1.3 constant_dynamic-slice_fusion.2.middle_ref
  102.2 1.2 add.286
  103.9 39.0 %collective-permute-done.9 = f32[2,16]{1,0:T(2,128)} collective-permute-done((f32[2,16]{1,0:T(2,128)}, f32[2,16]{1,0:T(2,128)}, u32[]{:S(2)}, u32[]{:S(2)}) %collective-permute-start.9) | collective-permute-done | bytes 160 | tf_op jit(solution)/shard_map/ppermute | solution.py:419
  143.6 1.4 fusion.16
  145.6 1.4 cosine_multiply_fusion
  147.0 1.4 cosine_multiply_fusion.2
  148.4 1.4 cosine_multiply_fusion.1
  149.8 1.4 multiply_select_fusion.3
  151.2 1.2 copy-done.6
  152.4 8.3 %second_section.4.refs_4_ = f32[2,32,12,32,128]{4,3,2,1,0:T(8,128)} custom-call(bf16[32,64,192]{2,1,0:T(8,128)(2,1)S(1)} %constant_dynamic-slice_fusion.2.middle_ref, f32[32,2,32,128]{3,2,1,0:T(8,128)S(1)} %constant_dynamic-slice_fusion.1.turn_ref, bf16[768,256]{1,0:T(8,128)(2,1)S(1)} %copy-done.2, f32[4,2,4,64,128]{4,3,2,1,0:T(8,128)S(1)} %get-tuple-element.60.refs_0_, ...), custom_call_target="tpu_custom_call" | custom-call | flops 1 | bytes 1 | tf_op jit(solution)/shard_map/second_section/pallas_call | solution.py:252
  160.8 2.1 slice_add_fusion.value_ref
  163.1 1.9 convolution_bitcast_fusion
  165.0 1.3 copy-done
  166.9 0.9 collective-permute-start.5
  167.8 2.4 collective-permute-start.6
  170.8 1.4 collective-permute-start.12
  172.6 45.7 %collective-permute-start.17 = (f32[2,2,4,64,128]{4,3,2,1,0:T(8,128)}, f32[2,2,4,64,128]{4,3,2,1,0:T(8,128)S(1)}, u32[]{:S(2)}, u32[]{:S(2)}) collective-permute-start(f32[2,2,4,64,128]{4,3,2,1,0:T(8,128)} %get-tuple-element.86), channel_id=1, source_target_pairs={{0,8},{4,12},{8,0},{12,4},{1,9},{5,13},{9,1},{13,5},{2,10},{6,14},... | collective-permute-start | bytes 1572872 | tf_op jit(solution)/shard_map/ppermute | solution.py:405
  218.3 3.8 %collective-permute-start.18 = (f32[2,2,4,64,128]{4,3,2,1,0:T(8,128)}, f32[2,2,4,64,128]{4,3,2,1,0:T(8,128)}, u32[]{:S(2)}, u32[]{:S(2)}) collective-permute-start(f32[2,2,4,64,128]{4,3,2,1,0:T(8,128)} %get-tuple-element.87), channel_id=1, source_target_pairs={{0,12},{4,0},{8,4},{12,8},{1,13},{5,1},{9,5},{13,9},{2,14},{6,2},{... | collective-permute-start | bytes 1572872 | tf_op jit(solution)/shard_map/ppermute | solution.py:405
  222.4 2.3 multiply_reduce_fusion.2
  225.6 1.7 copy.26
  227.3 1.5 pad_add_fusion.carry_ref
  229.0 16.3 %second_section.5.refs_4_ = f32[2,32,12,32,128]{4,3,2,1,0:T(8,128)} custom-call(bf16[32,64,192]{2,1,0:T(8,128)(2,1)S(1)} %constant_dynamic-slice_fusion.2.middle_ref, f32[32,2,32,128]{3,2,1,0:T(8,128)S(1)} %constant_dynamic-slice_fusion.1.turn_ref, bf16[768,256]{1,0:T(8,128)(2,1)S(1)} %copy-done.2, ...), custom_call_target="tpu_custom_call", output_to_operand_aliasing={{}: (7, {})} | custom-call | flops 1 | bytes 1 | tf_op jit(solution)/shard_map/second_section/pallas_call | solution.py:252
  245.3 3.4 %filter_columns.1 = f32[2,4,128,1024]{3,2,1,0:T(8,128)} custom-call(f32[4,128,1024]{2,1,0:T(8,128)S(1)} %copy-done.1, f32[4,128,256]{2,1,0:T(8,128)S(1)} %maximum_negate_fusion.table_ref, f32[2,4,128,8]{3,2,1,0:T(8,128)S(1)} %pad_add_fusion.carry_ref, f32[4,2,128]{2,1,0:T(2,128)S(1)} %maximum_negate_fusion.1.reach_ref), custom_call_target="tpu_custom_call" | custom-call | flops 1 | bytes 1 | tf_op jit(solution)/shard_map/filter_columns/pallas_call | solution.py:282
  248.8 11.5 %collective-permute-start.14 = (f32[1,2,4,64,128]{4,3,2,1,0:T(8,128)S(1)}, f32[1,2,4,64,128]{4,3,2,1,0:T(8,128)S(1)}, u32[]{:S(2)}, u32[]{:S(2)}) collective-permute-start(f32[1,2,4,64,128]{4,3,2,1,0:T(8,128)S(1)} %copy-done.19), channel_id=1, source_target_pairs={{0,8},{4,12},{8,0},{12,4},{1,9},{5,13},{9,1},{13,5},{2,10},{6,14},... | collective-permute-start | bytes 786440 | tf_op jit(solution)/shard_map/ppermute | solution.py:405
  260.3 1.4 collective-permute-start.13
  261.7 2.4 collective-permute-start.16
  264.1 7.1 %second_section.6.refs_4_ = f32[2,32,12,32,128]{4,3,2,1,0:T(8,128)} custom-call(bf16[32,64,192]{2,1,0:T(8,128)(2,1)S(1)} %constant_dynamic-slice_fusion.2.middle_ref, f32[32,2,32,128]{3,2,1,0:T(8,128)S(1)} %constant_dynamic-slice_fusion.1.turn_ref, bf16[768,256]{1,0:T(8,128)(2,1)S(1)} %copy-done.2, ...), custom_call_target="tpu_custom_call", output_to_operand_aliasing={{}: (7, {})} | custom-call | flops 1 | bytes 1 | tf_op jit(solution)/shard_map/second_section/pallas_call | solution.py:252
  271.2 10.3 %collective-permute-done.14.refs_2_ = f32[1,2,4,64,128]{4,3,2,1,0:T(8,128)S(1)} collective-permute-done((f32[1,2,4,64,128]{4,3,2,1,0:T(8,128)S(1)}, f32[1,2,4,64,128]{4,3,2,1,0:T(8,128)S(1)}, u32[]{:S(2)}, u32[]{:S(2)}) %collective-permute-start.14) | collective-permute-done | bytes 262176 | tf_op jit(solution)/shard_map/ppermute | solution.py:405
  281.5 1.8 collective-permute-done.16.refs_3_
  283.2 2.9 %second_section.7 = f32[2,32,12,32,128]{4,3,2,1,0:T(8,128)} custom-call(bf16[32,64,192]{2,1,0:T(8,128)(2,1)S(1)} %constant_dynamic-slice_fusion.2.middle_ref, f32[32,2,32,128]{3,2,1,0:T(8,128)S(1)} %constant_dynamic-slice_fusion.1.turn_ref, bf16[768,256]{1,0:T(8,128)(2,1)S(1)} %copy-done.2, ...), custom_call_target="tpu_custom_call", output_to_operand_aliasing={{}: (7, {})} | custom-call | flops 1 | bytes 1 | tf_op jit(solution)/shard_map/second_section/pallas_call | solution.py:252
  (140 shorter events, 15.2 us)
Async XLA Ops:
  1.6 10.2 %copy-start.27 = (f32[16,12]{1,0:T(8,128)S(1)}, f32[16,12]{1,0:T(8,128)}, u32[]{:S(2)}) copy-start(f32[16,12]{1,0:T(8,128)} %param.10) | copy-start | bytes 2308
  1.6 10.8 %copy-start.8 = (f32[512,128]{1,0:T(8,128)S(1)}, f32[512,128]{1,0:T(8,128)}, u32[]{:S(2)}) copy-start(f32[512,128]{1,0:T(8,128)} %constant.133.clone.table_ref) | copy-start | bytes 786436
  6.2 50.7 %collective-permute-start = (f32[4,2,4,64,128]{4,3,2,1,0:T(8,128)}, f32[4,2,4,64,128]{4,3,2,1,0:T(8,128)S(1)}, u32[]{:S(2)}, u32[]{:S(2)}) collective-permute-start(f32[4,2,4,64,128]{4,3,2,1,0:T(8,128)} %get-tuple-element.52), channel_id=1, source_target_pairs={{0,8},{4,12},{8,0},{12,4},{1,9},{5,13},{9,1},{13,5},{2,10},{6,14},... | collective-permute-start | bytes 3145736 | tf_op jit(solution)/shard_map/ppermute | solution.py:405
  10.2 46.7 %collective-permute-start.1 = (f32[4,2,4,64,128]{4,3,2,1,0:T(8,128)S(1)}, f32[4,2,4,64,128]{4,3,2,1,0:T(8,128)}, u32[]{:S(2)}, u32[]{:S(2)}) collective-permute-start(f32[4,2,4,64,128]{4,3,2,1,0:T(8,128)S(1)} %get-tuple-element.53), channel_id=1, source_target_pairs={{0,12},{4,0},{8,4},{12,8},{1,13},{5,1},{9,5},{13,9},{2,14},{6,2},{... | collective-permute-start | bytes 3145736 | tf_op jit(solution)/shard_map/ppermute | solution.py:405
  12.4 44.7 %copy-start.31 = (f32[2,16,12]{1,0,2:T(2,128)S(1)}, f32[2,16,12]{1,0,2:T(2,128)}, u32[]{:S(2)}) copy-start(f32[2,16,12]{1,0,2:T(2,128)} %param.11) | copy-start | bytes 4612
  56.9 35.8 %copy-start.5 = (f32[4,2,4,64,128]{4,3,2,1,0:T(8,128)}, f32[4,2,4,64,128]{4,3,2,1,0:T(8,128)S(1)}, u32[]{:S(2)}) copy-start(f32[4,2,4,64,128]{4,3,2,1,0:T(8,128)S(1)} %collective-permute-done.refs_2_) | copy-start | bytes 3145732
  56.9 31.4 %collective-permute-start.2 = (f32[8,128,1024]{2,1,0:T(8,128)}, f32[8,128,1024]{2,1,0:T(8,128)}, u32[]{:S(2)}, u32[]{:S(2)}) collective-permute-start(f32[8,128,1024]{2,1,0:T(8,128)} %get-tuple-element.55), channel_id=1, source_target_pairs={{0,1},{1,0},{2,3},{3,2},{4,5},{5,4},{6,7},{7,6},{8,9},{9,8},{10,11... | collective-permute-start | bytes 12582920 | tf_op jit(solution)/shard_map/ppermute | solution.py:477
  57.7 44.5 %collective-permute-start.8 = (f32[2,16]{1,0:T(2,128)}, f32[2,16]{1,0:T(2,128)}, u32[]{:S(2)}, u32[]{:S(2)}) collective-permute-start(f32[2,16]{1,0:T(2,128)} %multiply_reduce_fusion.4), channel_id=1, source_target_pairs={{0,1},{1,0},{2,3},{3,2},{4,5},{5,4},{6,7},{7,6},{8,9},{9,8},{10,11... | collective-permute-start | bytes 392 | tf_op jit(solution)/shard_map/ppermute | solution.py:419
  58.1 93.1 %collective-permute-start.4 = (f32[4,2,4,64,128]{4,3,2,1,0:T(8,128)}, f32[4,2,4,64,128]{4,3,2,1,0:T(8,128)}, u32[]{:S(2)}, u32[]{:S(2)}) collective-permute-start(f32[4,2,4,64,128]{4,3,2,1,0:T(8,128)} %get-tuple-element.62), channel_id=1, source_target_pairs={{0,4},{4,8},{8,12},{12,0},{1,5},{5,9},{9,13},{13,1},{2,6},{6,10},{... | collective-permute-start | bytes 3145736 | tf_op jit(solution)/shard_map/ppermute | solution.py:405
  80.5 90.3 %collective-permute-start.10 = (f32[5,2,4,64,128]{4,3,2,1,0:T(8,128)}, f32[5,2,4,64,128]{4,3,2,1,0:T(8,128)}, u32[]{:S(2)}, u32[]{:S(2)}) collective-permute-start(f32[5,2,4,64,128]{4,3,2,1,0:T(8,128)} %copy-done.13), channel_id=1, source_target_pairs={{0,4},{4,8},{8,12},{12,0},{1,5},{5,9},{9,13},{13,1},{2,6},{6,10},{... | collective-permute-start | bytes 3932168 | tf_op jit(solution)/shard_map/ppermute | solution.py:405
  80.5 148.3 %collective-permute-start.11 = (f32[5,2,4,64,128]{4,3,2,1,0:T(8,128)}, f32[5,2,4,64,128]{4,3,2,1,0:T(8,128)}, u32[]{:S(2)}, u32[]{:S(2)}) collective-permute-start(f32[5,2,4,64,128]{4,3,2,1,0:T(8,128)} %get-tuple-element.71), channel_id=1, source_target_pairs={{0,8},{4,12},{8,0},{12,4},{1,9},{5,13},{9,1},{13,5},{2,10},{6,14},... | collective-permute-start | bytes 3932168 | tf_op jit(solution)/shard_map/ppermute | solution.py:405
  95.4 65.4 %collective-permute-start.3 = (f32[4,128,1024]{2,1,0:T(8,128)}, f32[4,128,1024]{2,1,0:T(8,128)}, u32[]{:S(2)}, u32[]{:S(2)}) collective-permute-start(f32[4,128,1024]{2,1,0:T(8,128)} %slice.35), channel_id=1, source_target_pairs={{0,2},{2,0},{1,3},{3,1},{4,6},{6,4},{5,7},{7,5},{8,10},{10,8},{9,1... | collective-permute-start | bytes 6291464 | tf_op jit(solution)/shard_map/ppermute | solution.py:419
  98.1 53.1 %copy-start.2 = (bf16[768,256]{1,0:T(8,128)(2,1)S(1)}, bf16[768,256]{1,0:T(8,128)(2,1)}, u32[]{:S(2)}) copy-start(bf16[768,256]{1,0:T(8,128)(2,1)} %constant.136.clone.last_ref) | copy-start | bytes 1179652
  103.4 39.5 %collective-permute-start.9 = (f32[2,16]{1,0:T(2,128)}, f32[2,16]{1,0:T(2,128)}, u32[]{:S(2)}, u32[]{:S(2)}) collective-permute-start(f32[2,16]{1,0:T(2,128)} %add.286), channel_id=1, source_target_pairs={{0,2},{2,0},{1,3},{3,1},{4,6},{6,4},{5,7},{7,5},{8,10},{10,8},{9,1... | collective-permute-start | bytes 392 | tf_op jit(solution)/shard_map/ppermute | solution.py:419
  152.4 8.3 %copy-start.21 = (f32[8,128,1024]{2,1,0:T(8,128)S(1)}, f32[8,128,1024]{2,1,0:T(8,128)}, u32[]{:S(2)}) copy-start(f32[8,128,1024]{2,1,0:T(8,128)} %copy-done.20) | copy-start | bytes 12582916
  162.9 59.2 %copy-start.34 = (f32[4,4]{0,1:T(4,128)S(1)}, f32[4,4]{0,1:T(4,128)}, u32[]{:S(2)}) copy-start(f32[4,4]{0,1:T(4,128)} %get-tuple-element.120) | copy-start | bytes 196
  163.0 59.2 %copy-start.35 = (f32[4,4]{0,1:T(4,128)S(1)}, f32[4,4]{0,1:T(4,128)}, u32[]{:S(2)}) copy-start(f32[4,4]{0,1:T(4,128)} %get-tuple-element.121) | copy-start | bytes 196
  163.0 59.2 %copy-start.36 = (f32[4,4]{0,1:T(4,128)S(1)}, f32[4,4]{0,1:T(4,128)}, u32[]{:S(2)}) copy-start(f32[4,4]{0,1:T(4,128)} %get-tuple-element.126) | copy-start | bytes 196
  163.0 59.2 %copy-start.37 = (f32[4,4]{0,1:T(4,128)S(1)}, f32[4,4]{0,1:T(4,128)}, u32[]{:S(2)}) copy-start(f32[4,4]{0,1:T(4,128)} %get-tuple-element.127) | copy-start | bytes 196
  163.0 59.3 %copy-start.43 = (f32[4]{0:T(128)S(1)}, f32[4]{0:T(128)}, u32[]{:S(2)}) copy-start(f32[4]{0:T(128)} %get-tuple-element.118) | copy-start | bytes 52
  163.0 59.3 %copy-start.44 = (f32[4]{0:T(128)S(1)}, f32[4]{0:T(128)}, u32[]{:S(2)}) copy-start(f32[4]{0:T(128)} %get-tuple-element.119) | copy-start | bytes 52
  163.0 59.3 %copy-start.46 = (pred[128]{0:T(512)(128)(4,1)S(1)}, pred[128]{0:T(512)(128)(4,1)}, u32[]{:S(2)}) copy-start(pred[128]{0:T(512)(128)(4,1)} %iota_compare_fusion) | copy-start | bytes 388
  163.0 59.4 %copy-start.23 = (s32[128,128]{1,0:T(8,128)S(1)}, s32[128,128]{1,0:T(8,128)}, u32[]{:S(2)}) copy-start(s32[128,128]{1,0:T(8,128)} %get-tuple-element.138) | copy-start | bytes 196612
  163.0 59.4 %copy-start.24 = (s32[128,128]{1,0:T(8,128)S(1)}, s32[128,128]{1,0:T(8,128)}, u32[]{:S(2)}) copy-start(s32[128,128]{1,0:T(8,128)} %get-tuple-element.139) | copy-start | bytes 196612
  163.0 59.4 %copy-start.25 = (f32[128,128]{1,0:T(8,128)S(1)}, f32[128,128]{1,0:T(8,128)}, u32[]{:S(2)}) copy-start(f32[128,128]{1,0:T(8,128)} %get-tuple-element.140) | copy-start | bytes 196612
  163.0 59.4 %copy-start.26 = (f32[128,128]{1,0:T(8,128)S(1)}, f32[128,128]{1,0:T(8,128)}, u32[]{:S(2)}) copy-start(f32[128,128]{1,0:T(8,128)} %get-tuple-element.141) | copy-start | bytes 196612
  163.1 59.4 %copy-start.28 = (s32[4]{0:T(128)S(1)}, s32[4]{0:T(128)}, u32[]{:S(2)}) copy-start(s32[4]{0:T(128)} %param.12) | copy-start | bytes 52
  163.1 59.3 %copy-start.30 = (f32[4]{0:T(128)S(1)}, f32[4]{0:T(128)}, u32[]{:S(2)}) copy-start(f32[4]{0:T(128)} %copy-done.29) | copy-start | bytes 52
  163.1 59.3 %copy-start.45 = (f32[4]{0:T(128)S(1)}, f32[4]{0:T(128)}, u32[]{:S(2)}) copy-start(f32[4]{0:T(128)} %get-tuple-element.130) | copy-start | bytes 52
  163.1 61.7 %copy-start.41 = (f32[4]{0:T(128)S(1)}, f32[4]{0:T(128)}, u32[]{:S(2)}) copy-start(f32[4]{0:T(128)} %get-tuple-element.124) | copy-start | bytes 52
  163.1 61.7 %copy-start.42 = (f32[4]{0:T(128)S(1)}, f32[4]{0:T(128)}, u32[]{:S(2)}) copy-start(f32[4]{0:T(128)} %get-tuple-element.125) | copy-start | bytes 52
  163.1 61.7 %copy-start.32 = (f32[4,8]{1,0:T(4,128)S(1)}, f32[4,8]{1,0:T(4,128)}, u32[]{:S(2)}) copy-start(f32[4,8]{1,0:T(4,128)} %get-tuple-element.116) | copy-start | bytes 388
  163.1 61.7 %copy-start.33 = (f32[4,8]{1,0:T(4,128)S(1)}, f32[4,8]{1,0:T(4,128)}, u32[]{:S(2)}) copy-start(f32[4,8]{1,0:T(4,128)} %get-tuple-element.117) | copy-start | bytes 388
  166.9 5.7 %collective-permute-start.5 = (f32[2,4,128]{2,1,0:T(4,128)S(1)}, f32[2,4,128]{2,1,0:T(4,128)S(1)}, u32[]{:S(2)}, u32[]{:S(2)}) collective-permute-start(f32[2,4,128]{2,1,0:T(4,128)S(1)} %slice_reduce_fusion), channel_id=1, source_target_pairs={{0,4},{4,8},{8,12},{12,0},{1,5},{5,9},{9,13},{13,1},{2,6},{6,10},{... | collective-permute-start | bytes 12296 | tf_op jit(solution)/shard_map/ppermute | solution.py:337
  167.8 50.5 %collective-permute-start.6 = (f32[2,4,128]{2,1,0:T(4,128)S(1)}, f32[2,4,128]{2,1,0:T(4,128)S(1)}, u32[]{:S(2)}, u32[]{:S(2)}) collective-permute-start(f32[2,4,128]{2,1,0:T(4,128)S(1)} %slice_reduce_fusion), channel_id=1, source_target_pairs={{0,8},{4,12},{8,0},{12,4},{1,9},{5,13},{9,1},{13,5},{2,10},{6,14},... | collective-permute-start | bytes 12296 | tf_op jit(solution)/shard_map/ppermute | solution.py:337
  170.2 48.1 %collective-permute-start.7 = (f32[2,4,128]{2,1,0:T(4,128)S(1)}, f32[2,4,128]{2,1,0:T(4,128)S(1)}, u32[]{:S(2)}, u32[]{:S(2)}) collective-permute-start(f32[2,4,128]{2,1,0:T(4,128)S(1)} %slice_reduce_fusion), channel_id=1, source_target_pairs={{0,12},{4,0},{8,4},{12,8},{1,13},{5,1},{9,5},{13,9},{2,14},{6,2},{... | collective-permute-start | bytes 12296 | tf_op jit(solution)/shard_map/ppermute | solution.py:337
  170.8 58.0 %collective-permute-start.12 = (f32[5,2,4,64,128]{4,3,2,1,0:T(8,128)}, f32[5,2,4,64,128]{4,3,2,1,0:T(8,128)}, u32[]{:S(2)}, u32[]{:S(2)}) collective-permute-start(f32[5,2,4,64,128]{4,3,2,1,0:T(8,128)} %get-tuple-element.72), channel_id=1, source_target_pairs={{0,12},{4,0},{8,4},{12,8},{1,13},{5,1},{9,5},{13,9},{2,14},{6,2},{... | collective-permute-start | bytes 3932168 | tf_op jit(solution)/shard_map/ppermute | solution.py:405
  172.6 91.5 %collective-permute-start.17 = (f32[2,2,4,64,128]{4,3,2,1,0:T(8,128)}, f32[2,2,4,64,128]{4,3,2,1,0:T(8,128)S(1)}, u32[]{:S(2)}, u32[]{:S(2)}) collective-permute-start(f32[2,2,4,64,128]{4,3,2,1,0:T(8,128)} %get-tuple-element.86), channel_id=1, source_target_pairs={{0,8},{4,12},{8,0},{12,4},{1,9},{5,13},{9,1},{13,5},{2,10},{6,14},... | collective-permute-start | bytes 1572872 | tf_op jit(solution)/shard_map/ppermute | solution.py:405
  218.3 43.4 %collective-permute-start.15 = (f32[2,2,4,64,128]{4,3,2,1,0:T(8,128)}, f32[2,2,4,64,128]{4,3,2,1,0:T(8,128)}, u32[]{:S(2)}, u32[]{:S(2)}) collective-permute-start(f32[2,2,4,64,128]{4,3,2,1,0:T(8,128)} %get-tuple-element.81), channel_id=1, source_target_pairs={{0,4},{4,8},{8,12},{12,0},{1,5},{5,9},{9,13},{13,1},{2,6},{6,10},{... | collective-permute-start | bytes 1572872 | tf_op jit(solution)/shard_map/ppermute | solution.py:405
  218.3 45.8 %collective-permute-start.18 = (f32[2,2,4,64,128]{4,3,2,1,0:T(8,128)}, f32[2,2,4,64,128]{4,3,2,1,0:T(8,128)}, u32[]{:S(2)}, u32[]{:S(2)}) collective-permute-start(f32[2,2,4,64,128]{4,3,2,1,0:T(8,128)} %get-tuple-element.87), channel_id=1, source_target_pairs={{0,12},{4,0},{8,4},{12,8},{1,13},{5,1},{9,5},{13,9},{2,14},{6,2},{... | collective-permute-start | bytes 1572872 | tf_op jit(solution)/shard_map/ppermute | solution.py:405
  229.0 16.3 %copy-start.1 = (f32[4,128,1024]{2,1,0:T(8,128)S(1)}, f32[4,128,1024]{2,1,0:T(8,128)}, u32[]{:S(2)}) copy-start(f32[4,128,1024]{2,1,0:T(8,128)} %copy-done) | copy-start | bytes 6291460
  245.3 15.0 %copy-start.17 = (f32[1,2,4,64,128]{4,3,2,1,0:T(8,128)S(1)}, f32[1,2,4,64,128]{4,3,2,1,0:T(8,128)}, u32[]{:S(2)}) copy-start(f32[1,2,4,64,128]{4,3,2,1,0:T(8,128)} %copy-done.16) | copy-start | bytes 786436
  245.3 16.4 %copy-start.15 = (f32[1,2,4,64,128]{4,3,2,1,0:T(8,128)S(1)}, f32[1,2,4,64,128]{4,3,2,1,0:T(8,128)}, u32[]{:S(2)}) copy-start(f32[1,2,4,64,128]{4,3,2,1,0:T(8,128)} %copy-done.14) | copy-start | bytes 786436
  245.3 18.8 %copy-start.10 = (f32[2,2,4,64,128]{4,3,2,1,0:T(8,128)S(1)}, f32[2,2,4,64,128]{4,3,2,1,0:T(8,128)}, u32[]{:S(2)}) copy-start(f32[2,2,4,64,128]{4,3,2,1,0:T(8,128)} %copy-done.9) | copy-start | bytes 1572868
  248.7 34.5 %copy-start.12 = (f32[1,2,4,64,128]{4,3,2,1,0:T(8,128)S(1)}, f32[1,2,4,64,128]{4,3,2,1,0:T(8,128)}, u32[]{:S(2)}) copy-start(f32[1,2,4,64,128]{4,3,2,1,0:T(8,128)} %copy-done.11) | copy-start | bytes 786436
  248.8 32.7 %collective-permute-start.14 = (f32[1,2,4,64,128]{4,3,2,1,0:T(8,128)S(1)}, f32[1,2,4,64,128]{4,3,2,1,0:T(8,128)S(1)}, u32[]{:S(2)}, u32[]{:S(2)}) collective-permute-start(f32[1,2,4,64,128]{4,3,2,1,0:T(8,128)S(1)} %copy-done.19), channel_id=1, source_target_pairs={{0,8},{4,12},{8,0},{12,4},{1,9},{5,13},{9,1},{13,5},{2,10},{6,14},... | collective-permute-start | bytes 786440 | tf_op jit(solution)/shard_map/ppermute | solution.py:405
  260.3 21.2 %collective-permute-start.13 = (f32[1,2,4,64,128]{4,3,2,1,0:T(8,128)S(1)}, f32[1,2,4,64,128]{4,3,2,1,0:T(8,128)S(1)}, u32[]{:S(2)}, u32[]{:S(2)}) collective-permute-start(f32[1,2,4,64,128]{4,3,2,1,0:T(8,128)S(1)} %copy-done.17), channel_id=1, source_target_pairs={{0,4},{4,8},{8,12},{12,0},{1,5},{5,9},{9,13},{13,1},{2,6},{6,10},{... | collective-permute-start | bytes 786440 | tf_op jit(solution)/shard_map/ppermute | solution.py:405
  261.7 21.5 %collective-permute-start.16 = (f32[1,2,4,64,128]{4,3,2,1,0:T(8,128)S(1)}, f32[1,2,4,64,128]{4,3,2,1,0:T(8,128)S(1)}, u32[]{:S(2)}, u32[]{:S(2)}) collective-permute-start(f32[1,2,4,64,128]{4,3,2,1,0:T(8,128)S(1)} %copy-done.15), channel_id=1, source_target_pairs={{0,12},{4,0},{8,4},{12,8},{1,13},{5,1},{9,5},{13,9},{2,14},{6,2},{... | collective-permute-start | bytes 786440 | tf_op jit(solution)/shard_map/ppermute | solution.py:405
  (18 other events, 47.5 us)
